TPU v7x, 512 devices: a whole 4x8x8 slice. The times are simulated.
512 devices in a mesh: tile: 128 (over y, x, z_hi, core), sub: 4 (over z_lo).
Axes of the slice: x: 4, y: 8, z: 8 (z_hi: 2, z_lo: 4; z = z_hi * 4 + z_lo), core: 2. Of those that a mesh axis runs over, the one named last changes fastest.
Arguments:
- features: bfloat16 [128, 128, 4096], P('tile', None, 'sub')
- cotangent: bfloat16 [128, 128, 4096], P('tile', None, 'sub')
- conv_weight: bfloat16 [128, 9, 128], replicated, may hold values from -0.1875 to 0.1875
- norm_gain: float32 [128], replicated, may hold values from 0.1 to 1.9
- norm_shift: float32 [128], replicated, may hold values from -3 to 3
- seam_code: int32 [128, 4], P('tile'), may hold values from 0 to 7, as said below
- corner_map: int32 [128, 4], P('tile'), may hold values from 0 to 1, as said below
Outputs:
- grad_input: bfloat16 [128, 128, 4096], P('tile', None, 'sub')
- grad_weight: float32 [128, 9, 128], replicated
- grad_gain: float32 [128], replicated
- grad_shift: float32 [128], replicated
Inputs may be any that keep to these rules, and one draw needn't show every extreme that they name: seam_code[t, e] = D + 4 * f: side e faces grid direction D (0: tile t - 4, 1: tile t + 1, 2: tile t + 4, 3: tile t - 1, modulo 128); f = 1 marks a strip that runs reversed across the seam. The four sides of a tile face four different directions. `corner_map`: 0 fills a corner from the side along row 0 or row 65, 1 from the side along column 0 or column 65.
All inputs are finite; a program needn't handle non-finite values.
Results may differ from a plain program's by a relative error of at most 0.002.
The roundings to bfloat16 on the way count: a program that leaves them out, or rounds other values in their place, can miss the bound.
Values may be sent and summed in bfloat16 or wider, within the bound.
No kernel may reach another device: no remote copies, remote signals or barrier semaphores. Data moves between devices by JAX's collectives and lax.ppermute only.
A program may use at most 64 MiB of HBM per device.

v0:
```python
import math

import jax
import jax.numpy as jnp
from jax import lax
from jax.sharding import PartitionSpec as P

GROUPS = 16
GC = 4
S = 64


EPSILON = 1e-05


def shifted_2(x, axis, by):
    devices = lax.axis_size(axis)
    return lax.ppermute(x, axis, [(i, (i + by) % devices) for i in range(devices)])


def cycle_gather(row_parts, col_parts):
    return (
        lax.all_gather(row_parts, "sub", axis=1, tiled=True),
        lax.all_gather(col_parts, "sub", axis=2, tiled=True),
    )


def seam_move(edge_strip, offset):
    return shifted_2(edge_strip, "tile", offset)


def pick_facing(strips, facing, wanted):
    matched = facing == wanted
    return jnp.sum(jnp.where(matched[:, None, None], strips, jnp.zeros_like(strips)), axis=0)


def by_direction(arriving, facing, rotate):
    lookup = facing[:, None] == (jnp.arange(4, dtype=jnp.int32)[None, :] + rotate) % 4
    return jnp.sum(
        jnp.where(lookup[:, None, :, None], arriving[None], jnp.zeros_like(arriving)[None]), axis=2
    )


def body(features, cotangent, conv_weight, norm_gain, norm_shift, seam_code, corner_map):
    channels = features.shape[1]
    tile_side = S
    block_rows = features.shape[2] // tile_side
    per_group = channels // GROUPS
    position = lax.axis_index("sub")
    sub_count = lax.axis_size("sub")
    at_top = position == 0
    at_bottom = position == sub_count - 1
    cell_total = lax.axis_size("tile") * sub_count * block_rows * tile_side
    entries = per_group * cell_total
    grad_scale = 1.0 / math.sqrt(cell_total)
    own_block = features[0].reshape(channels, block_rows, tile_side)
    grad_out = cotangent[0].reshape(channels, block_rows, tile_side)
    facing = seam_code[0] % 4
    reversed_flag = seam_code[0] // 4
    corner_pick = corner_map[0]
    offsets = [-GC, 1, GC, -1]
    values = own_block.astype(jnp.float32)
    chan_view = (channels, 1, 1)

    def expand(vector):
        return jnp.repeat(vector, per_group)

    def exchange_edges(source):
        row_parts = jnp.stack(
            [source[:, 0], source[:, block_rows - 1], grad_out[:, 0], grad_out[:, block_rows - 1]],
            axis=1,
        )
        col_parts = jnp.stack([source[:, :, 0], source[:, :, tile_side - 1]], axis=1)
        row_all, col_all = cycle_gather(row_parts, col_parts)
        tile_edges = jnp.stack(
            [row_all[:, 0], col_all[:, 1], row_all[:, 4 * sub_count - 3], col_all[:, 0]], axis=0
        )
        arriving = jnp.stack(
            [
                seam_move(pick_facing(tile_edges, facing, (direction + 2) % 4), -offsets[direction])
                for direction in range(4)
            ],
            axis=1,
        )
        return (row_all, col_all, arriving)

    grouped = values.reshape(GROUPS, per_group * block_rows * tile_side)
    group_mean_values = lax.psum(jnp.sum(grouped, axis=1), ("tile", "sub")) / entries
    centred = grouped - group_mean_values[:, None]
    spread = lax.psum(jnp.sum(centred * centred, axis=1), ("tile", "sub")) / entries
    mean_c = expand(group_mean_values)
    rstd_c = expand(lax.rsqrt(spread + EPSILON))
    view_shape = (channels,) + (1,) * (own_block.ndim - 1)
    normed = (own_block.astype(jnp.float32) - mean_c.reshape(view_shape)) * rstd_c.reshape(
        view_shape
    )
    act_own = jax.nn.silu(
        normed * norm_gain.reshape(view_shape) + norm_shift.reshape(view_shape)
    ).astype(jnp.bfloat16)
    row_all, col_all, arriving = exchange_edges(act_own)
    first_rows = row_all[:, 0::4]
    last_rows = row_all[:, 1::4]
    grad_firsts = row_all[:, 2::4]
    grad_lasts = row_all[:, 3::4]
    above_index = jnp.maximum(position - 1, 0)
    below_index = jnp.minimum(position + 1, sub_count - 1)
    row_above = lax.dynamic_index_in_dim(last_rows, above_index, axis=1, keepdims=False)
    row_below = lax.dynamic_index_in_dim(first_rows, below_index, axis=1, keepdims=False)
    grad_above = lax.dynamic_index_in_dim(grad_lasts, above_index, axis=1, keepdims=False)
    grad_below = lax.dynamic_index_in_dim(grad_firsts, below_index, axis=1, keepdims=False)
    halo_in = by_direction(arriving, facing, 0)
    halo_in = jnp.where(reversed_flag[:, None, None] == 1, halo_in[:, :, ::-1], halo_in)
    corner_zero = jnp.where(corner_pick[0] == 0, halo_in[0][:, 0], halo_in[3][:, 0])
    corner_one = jnp.where(corner_pick[1] == 0, halo_in[0][:, tile_side - 1], halo_in[1][:, 0])
    corner_two = jnp.where(
        corner_pick[2] == 0, halo_in[2][:, tile_side - 1], halo_in[1][:, tile_side - 1]
    )
    corner_three = jnp.where(corner_pick[3] == 0, halo_in[2][:, 0], halo_in[3][:, tile_side - 1])
    left_line = jnp.concatenate([corner_zero[:, None], halo_in[3], corner_three[:, None]], axis=1)
    right_line = jnp.concatenate([corner_one[:, None], halo_in[1], corner_two[:, None]], axis=1)
    left_col = lax.dynamic_slice_in_dim(left_line, position * block_rows, block_rows + 2, axis=1)
    right_col = lax.dynamic_slice_in_dim(right_line, position * block_rows, block_rows + 2, axis=1)
    top_line = jnp.where(at_top, halo_in[0], row_above)
    bottom_line = jnp.where(at_bottom, halo_in[2], row_below)
    middle = jnp.concatenate([top_line[:, None], act_own, bottom_line[:, None]], axis=1)
    padded = jnp.concatenate([left_col[:, :, None], middle, right_col[:, :, None]], axis=2)
    windows = jnp.stack(
        [
            padded[
                :,
                tap_index // 3 : tap_index // 3 + block_rows,
                tap_index % 3 : tap_index % 3 + tile_side,
            ]
            for tap_index in range(9)
        ],
        axis=0,
    )
    windows = windows.reshape(9 * channels, block_rows * tile_side)
    weight_part = lax.dot_general(
        grad_out.reshape(channels, block_rows * tile_side),
        windows,
        (((1,), (1,)), ((), ())),
        preferred_element_type=jnp.float32,
    ).reshape(channels, 9, channels)
    zero_row = jnp.zeros_like(grad_out[:, 0])
    grad_padded = jnp.concatenate(
        [
            jnp.where(at_top, zero_row, grad_above)[:, None],
            grad_out,
            jnp.where(at_bottom, zero_row, grad_below)[:, None],
        ],
        axis=1,
    )
    wide_grad = jnp.pad(grad_padded, ((0, 0), (1, 1), (2, 2)))
    shifted = jnp.stack(
        [
            wide_grad[
                :,
                2 - tap_index // 3 : 2 - tap_index // 3 + block_rows + 2,
                2 - tap_index % 3 : 2 - tap_index % 3 + tile_side + 2,
            ]
            for tap_index in range(9)
        ],
        axis=0,
    )
    shifted = shifted.reshape(9 * channels, (block_rows + 2) * (tile_side + 2))
    flipped_weight = jnp.transpose(conv_weight, (2, 1, 0)).reshape(channels, 9 * channels)
    pad_grad = jnp.dot(flipped_weight, shifted, preferred_element_type=jnp.float32).reshape(
        channels, block_rows + 2, tile_side + 2
    )
    top_grad = pad_grad[:, 0, 1 : tile_side + 1]
    bottom_grad = pad_grad[:, block_rows + 1, 1 : tile_side + 1]
    left_grad = pad_grad[:, 1 : block_rows + 1, 0]
    right_grad = pad_grad[:, 1 : block_rows + 1, tile_side + 1]
    corner_grads = [
        pad_grad[:, 0, 0],
        pad_grad[:, 0, tile_side + 1],
        pad_grad[:, block_rows + 1, tile_side + 1],
        pad_grad[:, block_rows + 1, 0],
    ]
    nothing = jnp.zeros_like(corner_grads[0])

    def part_of(corner_index, wanted, holder):
        return jnp.where(
            holder & (corner_pick[corner_index] == wanted), corner_grads[corner_index], nothing
        )

    top_grad = (
        top_grad.at[:, 0].add(part_of(0, 0, at_top)).at[:, tile_side - 1].add(part_of(1, 0, at_top))
    )
    bottom_grad = (
        bottom_grad.at[:, tile_side - 1]
        .add(part_of(2, 0, at_bottom))
        .at[:, 0]
        .add(part_of(3, 0, at_bottom))
    )
    left_grad = (
        left_grad.at[:, 0]
        .add(part_of(0, 1, at_top))
        .at[:, block_rows - 1]
        .add(part_of(3, 1, at_bottom))
    )
    right_grad = (
        right_grad.at[:, 0]
        .add(part_of(1, 1, at_top))
        .at[:, block_rows - 1]
        .add(part_of(2, 1, at_bottom))
    )
    zero_line = jnp.zeros_like(top_grad)
    row_sends = jnp.stack(
        [jnp.where(at_top, top_grad, zero_line), jnp.where(at_bottom, bottom_grad, zero_line)],
        axis=1,
    ).astype(jnp.bfloat16)
    col_sends = jnp.stack([left_grad, right_grad], axis=1).astype(jnp.bfloat16)
    row_back, col_back = cycle_gather(row_sends, col_sends)
    halo_grad = jnp.stack(
        [row_back[:, 0], col_back[:, 1], row_back[:, 2 * sub_count - 1], col_back[:, 0]], axis=0
    )
    turned = jnp.where(reversed_flag[:, None, None] == 1, halo_grad[:, :, ::-1], halo_grad)
    coming = jnp.stack(
        [
            seam_move(pick_facing(turned, facing, direction), offsets[direction])
            for direction in range(4)
        ],
        axis=1,
    )
    returned = by_direction(coming, facing, 2).astype(jnp.float32)
    act_grad = pad_grad[:, 1 : block_rows + 1, 1 : tile_side + 1]
    act_grad = act_grad.at[:, :, 0].add(
        lax.dynamic_slice_in_dim(returned[3], position * block_rows, block_rows, axis=1)
    )
    act_grad = act_grad.at[:, :, tile_side - 1].add(
        lax.dynamic_slice_in_dim(returned[1], position * block_rows, block_rows, axis=1)
    )
    act_grad = act_grad.at[:, 0].add(jnp.where(at_top, returned[0], jnp.zeros_like(returned[0])))
    act_grad = act_grad.at[:, block_rows - 1].add(
        jnp.where(at_bottom, returned[2], jnp.zeros_like(returned[2]))
    )
    normed = (values - mean_c.reshape(chan_view)) * rstd_c.reshape(chan_view)
    pre_act = normed * norm_gain.reshape(chan_view) + norm_shift.reshape(chan_view)
    sigmoid_of = jax.nn.sigmoid(pre_act)
    pre_grad = act_grad * (sigmoid_of * (1.0 + pre_act * (1.0 - sigmoid_of)))
    gain_part = jnp.sum(pre_grad * normed, axis=(1, 2))
    shift_part = jnp.sum(pre_grad, axis=(1, 2))
    weight_total, gain_total, shift_total = lax.psum(
        (weight_part, gain_part, shift_part), ("tile", "sub")
    )
    first_mean = (
        expand(jnp.sum((norm_gain * shift_total).reshape(GROUPS, per_group), axis=1)) / entries
    )
    second_mean = (
        expand(jnp.sum((norm_gain * gain_total).reshape(GROUPS, per_group), axis=1)) / entries
    )
    grad_input = (
        rstd_c.reshape(chan_view)
        * (
            pre_grad * norm_gain.reshape(chan_view)
            - first_mean.reshape(chan_view)
            - normed * second_mean.reshape(chan_view)
        )
    ).astype(jnp.bfloat16)
    return (
        grad_input.reshape(1, channels, block_rows * tile_side),
        weight_total * grad_scale,
        gain_total * grad_scale,
        shift_total * grad_scale,
    )


def solution(mesh):
    return jax.shard_map(
        body,
        mesh=mesh,
        in_specs=(
            P("tile", None, "sub"),
            P("tile", None, "sub"),
            P(),
            P(),
            P(),
            P("tile", None),
            P("tile", None),
        ),
        out_specs=(P("tile", None, "sub"), P(), P(), P()),
        check_vma=False,
    )
```

profile of v0, /device:TPU:1, one launch (start us, length us, event | category | flops | bytes accessed | tf_op | source)
XLA Modules:
  0.0 697.0 jit_solution(18078299407966842882)
XLA Ops:
  8.0 1.4 fusion.67
  13.9 1.1 copy.102
  16.0 106.1 %psum.35 = f32[16]{0:T(128)S(1)} all-reduce(f32[16]{0:T(128)S(1)} %reduce_sum.190), channel_id=1, replica_groups=mesh['tile'=128,'sub'=4] {'tile','sub'}, use_global_device_ids=true, to_apply=%region_2.3 | all-reduce | flops 16 | bytes 128 | tf_op jit(solution)/shard_map/psum | solution.py:88
  122.8 93.6 %psum.36 = f32[16]{0:T(128)S(1)} all-reduce(f32[16]{0:T(128)S(1)} %reduce_sum.193), channel_id=1, replica_groups=mesh['tile'=128,'sub'=4] {'tile','sub'}, use_global_device_ids=true, to_apply=%region_5.6 | all-reduce | flops 16 | bytes 128 | tf_op jit(solution)/shard_map/psum | solution.py:90
  217.6 11.0 %all_gather.12 = bf16[128,16,64]{0,2,1:T(8,128)(2,1)S(1)} all-gather(bf16[128,4,64]{0,2,1:T(8,128)(2,1)S(1)} %pad_maximum_fusion.3), channel_id=1, replica_groups=mesh['tile'=128,'sub'=4] {'sub'}, dimensions={1}, use_global_device_ids=true | all-gather | bytes 327680 | tf_op jit(solution)/shard_map/all_gather | solution.py:23
  229.8 1.1 copy.104
  231.8 1.4 copy.114
  234.5 10.2 %all_gather.15 = bf16[128,2,64]{0,2,1:T(8,128)(2,1)S(1)} all-gather(bf16[128,2,16]{0,2,1:T(8,128)(2,1)S(1)} %pad_maximum_fusion.10), channel_id=1, replica_groups=mesh['tile'=128,'sub'=4] {'sub'}, dimensions={2}, use_global_device_ids=true | all-gather | bytes 40960 | tf_op jit(solution)/shard_map/all_gather | solution.py:24
  245.3 1.3 fusion.46
  246.9 10.2 %all_gather.14 = bf16[128,2,64]{0,2,1:T(8,128)(2,1)S(1)} all-gather(bf16[128,2,16]{0,2,1:T(8,128)(2,1)S(1)} %pad_maximum_fusion.9), channel_id=1, replica_groups=mesh['tile'=128,'sub'=4] {'sub'}, dimensions={2}, use_global_device_ids=true | all-gather | bytes 40960 | tf_op jit(solution)/shard_map/all_gather | solution.py:24
  257.1 10.5 %all_gather.13 = bf16[128,8,64]{0,2,1:T(8,128)(2,1)S(1)} all-gather(bf16[128,2,64]{0,2,1:T(8,128)(2,1)S(1)} %pad_maximum_fusion.8), channel_id=1, replica_groups=mesh['tile'=128,'sub'=4] {'sub'}, dimensions={1}, use_global_device_ids=true | all-gather | bytes 163840 | tf_op jit(solution)/shard_map/all_gather | solution.py:23
  267.9 5.6 collective-permute-start
  273.4 14.7 %collective-permute-start.3 = (bf16[128,64]{0,1:T(8,128)(2,1)S(1)}, bf16[128,64]{0,1:T(8,128)(2,1)S(1)}, u32[]{:S(2)}, u32[]{:S(2)}) collective-permute-start(bf16[128,64]{0,1:T(8,128)(2,1)S(1)} %get-tuple-element.178), channel_id=1, source_target_pairs={{0,508},{4,0},{8,4},{12,8},{16,12},{20,16},{24,20},{28,24},{32,28}... | collective-permute-start | bytes 49160 | tf_op jit(solution)/shard_map/ppermute | solution.py:18
  288.2 1.9 collective-permute-start.2
  290.1 3.2 collective-permute-start.1
  293.3 7.0 collective-permute-start.6
  300.4 1.9 collective-permute-start.5
  302.4 1.9 collective-permute-start.4
  304.3 7.5 %collective-permute-start.7 = (bf16[128,64]{0,1:T(8,128)(2,1)S(1)}, bf16[128,64]{0,1:T(8,128)(2,1)S(1)}, u32[]{:S(2)}, u32[]{:S(2)}) collective-permute-start(bf16[128,64]{0,1:T(8,128)(2,1)S(1)} %get-tuple-element.215), channel_id=1, source_target_pairs={{0,4},{4,8},{8,12},{12,16},{16,20},{20,24},{24,28},{28,32},{32,36}... | collective-permute-start | bytes 49160 | tf_op jit(solution)/shard_map/ppermute | solution.py:18
  313.7 103.0 %all-reduce.1 = (f32[128]{0:T(128)S(1)}, f32[128]{0:T(128)S(1)}) all-reduce(f32[128]{0:T(128)S(1)} %get-tuple-element.173, f32[128]{0:T(128)S(1)} %get-tuple-element.172), channel_id=1, replica_groups=mesh['tile'=128,'sub'=4] {'tile','sub'}, use_global_device_ids=true, to_apply=%region_17.18 | all-reduce | flops 256 | bytes 2048 | tf_op jit(solution)/shard_map/psum | solution.py:245
  418.6 2.3 copy.108
  421.9 1.1 copy.109
  424.3 263.9 %all-reduce.4.cloned.1.call-done = f32[128,9,128]{2,0,1:T(8,128)} async-done(((f32[128,9,128]{2,0,1:T(8,128)}), f32[128,9,128]{2,0,1:T(8,128)}) %all-reduce.4.cloned.1.call-update) | async-done | bytes 589840 | tf_op jit(solution)/shard_map/psum | solution.py:245
  688.2 1.9 broadcast_multiply_fusion
  (136 shorter events, 13.0 us)
Async XLA Ops:
  7.2 226.1 %copy-start = (bf16[128,9,128]{2,0,1:T(8,128)(2,1)S(1)}, bf16[128,9,128]{2,0,1:T(8,128)(2,1)}, u32[]{:S(2)}) copy-start(bf16[128,9,128]{2,0,1:T(8,128)(2,1)} %param.33) | copy-start | bytes 884740
  7.2 210.2 %copy-start.1 = (bf16[1,128,1024]{2,1,0:T(8,128)(2,1)S(1)}, bf16[1,128,1024]{2,1,0:T(8,128)(2,1)}, u32[]{:S(2)}) copy-start(bf16[1,128,1024]{2,1,0:T(8,128)(2,1)} %param.32) | copy-start | bytes 786436
  7.2 681.1 %all-reduce.4.cloned.1.call-start = ((), (), s32[]{:S(2)}) async-start(), calls=%async_computation | async-start | bytes 1179648 | tf_op jit(solution)/shard_map/psum | solution.py:245
  233.2 1.1 copy-start.4
  234.2 79.1 %copy-start.2 = (f32[128]{0:T(128)S(1)}, f32[128]{0:T(128)}, u32[]{:S(2)}) copy-start(f32[128]{0:T(128)} %param.34) | copy-start | bytes 1540
  234.2 79.1 %copy-start.3 = (f32[128]{0:T(128)S(1)}, f32[128]{0:T(128)}, u32[]{:S(2)}) copy-start(f32[128]{0:T(128)} %param.35) | copy-start | bytes 1540
  267.9 32.5 %collective-permute-start = (bf16[128,64]{0,1:T(8,128)(2,1)S(1)}, bf16[128,64]{0,1:T(8,128)(2,1)S(1)}, u32[]{:S(2)}, u32[]{:S(2)}) collective-permute-start(bf16[128,64]{0,1:T(8,128)(2,1)S(1)} %get-tuple-element.177), channel_id=1, source_target_pairs={{0,496},{4,500},{8,504},{12,508},{16,0},{20,4},{24,8},{28,12},{32,... | collective-permute-start | bytes 49160 | tf_op jit(solution)/shard_map/ppermute | solution.py:18
  273.4 28.9 %collective-permute-start.3 = (bf16[128,64]{0,1:T(8,128)(2,1)S(1)}, bf16[128,64]{0,1:T(8,128)(2,1)S(1)}, u32[]{:S(2)}, u32[]{:S(2)}) collective-permute-start(bf16[128,64]{0,1:T(8,128)(2,1)S(1)} %get-tuple-element.178), channel_id=1, source_target_pairs={{0,508},{4,0},{8,4},{12,8},{16,12},{20,16},{24,20},{28,24},{32,28}... | collective-permute-start | bytes 49160 | tf_op jit(solution)/shard_map/ppermute | solution.py:18
  288.2 16.1 %collective-permute-start.2 = (bf16[128,64]{0,1:T(8,128)(2,1)S(1)}, bf16[128,64]{0,1:T(8,128)(2,1)S(1)}, u32[]{:S(2)}, u32[]{:S(2)}) collective-permute-start(bf16[128,64]{0,1:T(8,128)(2,1)S(1)} %get-tuple-element.179), channel_id=1, source_target_pairs={{0,16},{4,20},{8,24},{12,28},{16,32},{20,36},{24,40},{28,44},{32,4... | collective-permute-start | bytes 49160 | tf_op jit(solution)/shard_map/ppermute | solution.py:18
  290.1 21.7 %collective-permute-start.1 = (bf16[128,64]{0,1:T(8,128)(2,1)S(1)}, bf16[128,64]{0,1:T(8,128)(2,1)S(1)}, u32[]{:S(2)}, u32[]{:S(2)}) collective-permute-start(bf16[128,64]{0,1:T(8,128)(2,1)S(1)} %get-tuple-element.180), channel_id=1, source_target_pairs={{0,4},{4,8},{8,12},{12,16},{16,20},{20,24},{24,28},{28,32},{32,36}... | collective-permute-start | bytes 49160 | tf_op jit(solution)/shard_map/ppermute | solution.py:18
  293.3 18.7 %collective-permute-start.6 = (bf16[128,64]{0,1:T(8,128)(2,1)S(1)}, bf16[128,64]{0,1:T(8,128)(2,1)S(1)}, u32[]{:S(2)}, u32[]{:S(2)}) collective-permute-start(bf16[128,64]{0,1:T(8,128)(2,1)S(1)} %get-tuple-element.181), channel_id=1, source_target_pairs={{0,496},{4,500},{8,504},{12,508},{16,0},{20,4},{24,8},{28,12},{32,... | collective-permute-start | bytes 49160 | tf_op jit(solution)/shard_map/ppermute | solution.py:18
  300.4 11.6 %collective-permute-start.5 = (bf16[128,64]{0,1:T(8,128)(2,1)S(1)}, bf16[128,64]{0,1:T(8,128)(2,1)S(1)}, u32[]{:S(2)}, u32[]{:S(2)}) collective-permute-start(bf16[128,64]{0,1:T(8,128)(2,1)S(1)} %get-tuple-element.182), channel_id=1, source_target_pairs={{0,508},{4,0},{8,4},{12,8},{16,12},{20,16},{24,20},{28,24},{32,28}... | collective-permute-start | bytes 49160 | tf_op jit(solution)/shard_map/ppermute | solution.py:18
  302.4 9.7 %collective-permute-start.4 = (bf16[128,64]{0,1:T(8,128)(2,1)S(1)}, bf16[128,64]{0,1:T(8,128)(2,1)S(1)}, u32[]{:S(2)}, u32[]{:S(2)}) collective-permute-start(bf16[128,64]{0,1:T(8,128)(2,1)S(1)} %get-tuple-element.183), channel_id=1, source_target_pairs={{0,16},{4,20},{8,24},{12,28},{16,32},{20,36},{24,40},{28,44},{32,4... | collective-permute-start | bytes 49160 | tf_op jit(solution)/shard_map/ppermute | solution.py:18
  304.3 8.4 %collective-permute-start.7 = (bf16[128,64]{0,1:T(8,128)(2,1)S(1)}, bf16[128,64]{0,1:T(8,128)(2,1)S(1)}, u32[]{:S(2)}, u32[]{:S(2)}) collective-permute-start(bf16[128,64]{0,1:T(8,128)(2,1)S(1)} %get-tuple-element.215), channel_id=1, source_target_pairs={{0,4},{4,8},{8,12},{12,16},{16,20},{20,24},{24,28},{28,32},{32,36}... | collective-permute-start | bytes 49160 | tf_op jit(solution)/shard_map/ppermute | solution.py:18
Sparse Core Ops, SparseCore 0:
  423.1 265.1 all-reduce.3
where the time goes:
time: 698 us; the launch traced here: 697 us
  blocking collectives  345 us (49%)
  waiting for transfers between devices  265 us (38%)
  starting transfers between devices  43.8 us (6%)
  between operations  20.1 us (3%)
  local copies, waits for them, and re-layouts  13.3 us (2%)
  other arithmetic  8.54 us (1%)
    psum x1, waiting for transfers between devices, body(): lax.psum((weight_part, gain_part, shift_part), ('tile', 'sub'))  264 us
    psum x1, blocking collectives, body(): lax.psum(jnp.sum(grouped, axis=1), ('tile', 'sub')) / entries  106 us
    psum x1, blocking collectives, body(): lax.psum((weight_part, gain_part, shift_part), ('tile', 'sub'))  103 us
    psum x1, blocking collectives, body(): lax.psum(jnp.sum(centred * centred, axis=1), ('tile', 'sub')) / entries  93.6 us
    ppermute x8, starting transfers between devices, shifted_2(): lax.ppermute(x, axis, [(i, (i + by) % devices) for i in range(devices)])  43.7 us
    all_gather x2, blocking collectives, cycle_gather(): lax.all_gather(row_parts, 'sub', axis=1, tiled=True)  21.5 us
    all_gather x2, blocking collectives, cycle_gather(): lax.all_gather(col_parts, 'sub', axis=2, tiled=True)  20.5 us
  transfers between devices with their start and end apart: 9, of which 2 were waited for; matrix products, arithmetic and copies ran while one was open for 0% of the time, Pallas kernels for 0%

commit v1 on v0

v1 whole, which is shorter than its diff:
```python
import math

import jax
import jax.numpy as jnp
from jax import lax
from jax.experimental import pallas as pl
from jax.experimental.pallas import tpu as pltpu
from jax.sharding import Mesh
from jax.sharding import PartitionSpec as P

GC = 4
S = 64
PER_GROUP = 8
EPSILON = 1e-05
STEPS = (-GC, 1, GC, -1)
ROWS = 16
CELLS = ROWS * S
C = 128
EDGE = 2 * S + 2 * ROWS
CHUNK = 24

TILE = ("y", "x", "zh", "co")
AXES = {"y": 8, "x": 4, "zh": 2, "co": 2, "zl": 4}
NEAR = ("zh", "co", "zl")
FAR = ("y", "x")
N_NEAR = 16
N_FAR = 32
DEVICES = 512
ENTRIES = DEVICES * CELLS * PER_GROUP
LOCAL = CELLS * PER_GROUP
SCALE = 1.0 / math.sqrt(DEVICES * CELLS)

F32 = jnp.float32
BF16 = jnp.bfloat16
VMEM = pl.BlockSpec(memory_space=pltpu.VMEM)
SMEM = pl.BlockSpec(memory_space=pltpu.SMEM)
PARAMS = pltpu.CompilerParams(vmem_limit_bytes=40 * 1024 * 1024)


def group_sum(row):
    total = jnp.broadcast_to(row, (8, C))
    lane = lax.broadcasted_iota(jnp.int32, (8, C), 1)
    for by in (1, 2, 4):
        other = jnp.where(
            (lane & by) != 0, pltpu.roll(total, by, 1), pltpu.roll(total, C - by, 1)
        )
        total = total + other
    return total[0:1]


def merge(rows, count):
    means, squares = rows[:, :C], rows[:, C:]
    mean = jnp.sum(means, axis=0, keepdims=True) * (1.0 / rows.shape[0])
    gap = means - mean
    spread = jnp.sum(squares, axis=0, keepdims=True) + float(count) * jnp.sum(
        gap * gap, axis=0, keepdims=True
    )
    return mean, spread


def start_kernel(x_ref, c_ref, xt_ref, ct_ref, edge_ref, stat_ref, x_scr, c_scr):
    x = x_ref[0].astype(F32).T
    x_scr[...] = x
    xt_ref[...] = x.astype(BF16)
    c = c_ref[0].astype(F32).T
    c_scr[...] = c
    ct_ref[...] = c.astype(BF16)
    for base, scr, flat in ((0, x_scr, xt_ref), (EDGE, c_scr, ct_ref)):
        edge_ref[base : base + S] = flat[0:S]
        edge_ref[base + S : base + 2 * S] = flat[CELLS - S : CELLS]
        edge_ref[base + 2 * S : base + 2 * S + ROWS] = scr[
            pl.ds(0, ROWS, stride=S), :
        ].astype(BF16)
        edge_ref[base + 2 * S + ROWS : base + EDGE] = scr[
            pl.ds(S - 1, ROWS, stride=S), :
        ].astype(BF16)
    mean = group_sum(jnp.sum(x, axis=0, keepdims=True)) * (1.0 / LOCAL)
    gap = x - mean
    spread = group_sum(jnp.sum(gap * gap, axis=0, keepdims=True))
    stat_ref[...] = jnp.broadcast_to(
        jnp.concatenate([mean, spread], axis=1), (N_NEAR, 2 * C)
    )


def flip_matrix():
    a = lax.broadcasted_iota(jnp.int32, (S, S), 0)
    b = lax.broadcasted_iota(jnp.int32, (S, S), 1)
    return jnp.where(a + b == S - 1, 1.0, 0.0).astype(BF16)


def turned(strip, flag):
    back = jnp.dot(flip_matrix(), strip, preferred_element_type=F32)
    return jnp.where(flag == 1, back, strip.astype(F32)).astype(BF16)


def seam_kernel(
    place_ref, seam_ref, corner_ref, e0_ref, e1_ref, e2_ref, e3_ref, stat_ref, w_ref,
    m0_ref, m1_ref, m2_ref, m3_ref, rows_ref, out_stat_ref, all_scr, side_scr, grad_scr,
):
    place = place_ref[0]
    for k, ref in enumerate((e0_ref, e1_ref, e2_ref, e3_ref)):
        all_scr[(place + 4 - k) % 4] = ref[...]
    for kind in range(2):
        base = kind * EDGE
        side_scr[kind, 0] = all_scr[0, base : base + S]
        side_scr[kind, 2] = all_scr[3, base + S : base + 2 * S]
        for p in range(4):
            at = slice(p * ROWS, (p + 1) * ROWS)
            side_scr[kind, 3, at] = all_scr[p, base + 2 * S : base + 2 * S + ROWS]
            side_scr[kind, 1, at] = all_scr[p, base + 2 * S + ROWS : base + EDGE]
    row = lax.broadcasted_iota(jnp.int32, (S, C), 0)
    first, last = row == 0, row == S - 1
    taps = ((0, 1, 2), (2, 5, 8), (6, 7, 8), (0, 3, 6))
    ends = (((0, 0), (1, 0)), ((1, 1), (2, 1)), ((3, 0), (2, 0)), ((0, 1), (3, 1)))
    for e in range(4):
        strip = side_scr[1, e]
        parts = [
            jnp.dot(strip, w_ref[:, t * C : (t + 1) * C], preferred_element_type=F32)
            for t in taps[e]
        ]
        (start_at, start_is), (end_at, end_is) = ends[e]
        grad = parts[1]
        grad = grad + jnp.where(last, 0.0, pltpu.roll(parts[0], S - 1, 0))
        grad = grad + jnp.where(first, 0.0, pltpu.roll(parts[2], 1, 0))
        grad = grad + jnp.where(first & (corner_ref[0, start_at] == start_is), parts[0], 0.0)
        grad = grad + jnp.where(last & (corner_ref[0, end_at] == end_is), parts[2], 0.0)
        grad_scr[e] = turned(grad.astype(BF16), seam_ref[0, e] // 4)
    for d, ref in enumerate((m0_ref, m1_ref, m2_ref, m3_ref)):
        side = jnp.int32(0)
        for e in range(1, 4):
            side = jnp.where(seam_ref[0, e] % 4 == d, e, side)
        ref[0:S] = side_scr[0, side]
        ref[S : 2 * S] = grad_scr[side]
    above, below = jnp.maximum(place - 1, 0), jnp.minimum(place + 1, 3)
    rows_ref[0:S] = all_scr[above, S : 2 * S]
    rows_ref[S : 2 * S] = all_scr[below, 0:S]
    zero = jnp.zeros((S, C), BF16)
    rows_ref[2 * S : 3 * S] = jnp.where(place == 0, zero, all_scr[above, EDGE + S : EDGE + 2 * S])
    rows_ref[3 * S : 4 * S] = jnp.where(place == 3, zero, all_scr[below, EDGE : EDGE + S])
    mean, spread = merge(stat_ref[...], LOCAL)
    out_stat_ref[...] = jnp.broadcast_to(
        jnp.concatenate([mean, spread], axis=1), (N_FAR, 2 * C)
    )


def main_kernel(
    place_ref, seam_ref, corner_ref, xt_ref, ct_ref, cot_ref, rows_ref, stat_ref, w_ref,
    gain_ref, shift_ref, a0_ref, a1_ref, a2_ref, a3_ref,
    part_ref, pre_ref, norm_ref, in_scr, line_scr, left_scr, right_scr, act_scr,
):
    place = place_ref[0]
    for d, ref in enumerate((a0_ref, a1_ref, a2_ref, a3_ref)):
        in_scr[(d + 2) % 4] = ref[...]
    mean, spread = merge(stat_ref[...], LOCAL * N_NEAR)
    rstd = lax.rsqrt(spread * (1.0 / ENTRIES) + EPSILON)
    gain, shift = gain_ref[...], shift_ref[...]
    norm_ref[...] = jnp.concatenate([mean, rstd], axis=0)

    def affine(raw):
        normed = (raw.astype(F32) - mean) * rstd
        pre = normed * gain + shift
        return normed, pre, 1.0 / (1.0 + jnp.exp(-pre))

    def activated(raw):
        _, pre, sig = affine(raw)
        return (pre * sig).astype(BF16).astype(F32)

    def strip(e):
        return turned(in_scr[seam_ref[0, e] % 4, 0:S], seam_ref[0, e] // 4)

    top = activated(jnp.where(place == 0, strip(0), rows_ref[0:S]))
    bottom = activated(jnp.where(place == 3, strip(2), rows_ref[S : 2 * S]))
    right, left = activated(strip(1)), activated(strip(3))
    normed, pre, sig = affine(xt_ref[...])
    own = (pre * sig).astype(BF16).astype(F32)
    for k, (line, near, far, a, b, at) in enumerate(
        ((left, 0, 3, 0, 0, 0), (right, 1, 2, S - 1, S - 1, 1))
    ):
        line_scr[k, 8 : 8 + S] = line
        line_scr[k, 7:8] = jnp.where(corner_ref[0, near] == 0, top[a : a + 1], line[0:1])
        line_scr[k, 8 + S : 9 + S] = jnp.where(
            corner_ref[0, far] == 0, bottom[b : b + 1], line[S - 1 : S]
        )
    window = pl.ds(pl.multiple_of(place * ROWS, 8), 32)
    left_part = line_scr[0, window, :][7 : 7 + ROWS + 2]
    right_part = line_scr[1, window, :][7 : 7 + ROWS + 2]
    middle = jnp.concatenate([top, own, bottom], axis=0)
    wide = CELLS + 2 * S
    left_scr[...] = pltpu.roll(middle, 1, 0)
    left_scr[pl.ds(0, ROWS + 2, stride=S), :] = left_part
    right_scr[...] = pltpu.roll(middle, wide - 1, 0)
    right_scr[pl.ds(S - 1, ROWS + 2, stride=S), :] = right_part
    windows = jnp.concatenate(
        [left_scr[...].astype(BF16), middle.astype(BF16), right_scr[...].astype(BF16)], axis=1
    )
    grad_out = cot_ref[0]
    for i in range(3):
        part = jnp.dot(grad_out, windows[i * S : i * S + CELLS], preferred_element_type=F32)
        for j in range(3):
            for h in range(2):
                part_ref[pl.ds(h * 9 + 3 * i + j, 64, stride=CHUNK), :] = part[
                    h * 64 : (h + 1) * 64, j * C : (j + 1) * C
                ]

    grads = jnp.concatenate(
        [rows_ref[2 * S : 3 * S], ct_ref[...], rows_ref[3 * S : 4 * S]], axis=0
    ).astype(F32)
    column = lax.broadcasted_iota(jnp.int32, (wide, C), 0) & (S - 1)
    later = jnp.where(column == S - 1, 0.0, pltpu.roll(grads, wide - 1, 0))
    earlier = jnp.where(column == 0, 0.0, pltpu.roll(grads, 1, 0))
    shifted = jnp.concatenate(
        [later.astype(BF16), grads.astype(BF16), earlier.astype(BF16)], axis=1
    )
    act_grad = None
    for i in range(3):
        weight = jnp.concatenate(
            [w_ref[:, (3 * i + j) * C : (3 * i + j + 1) * C] for j in range(3)], axis=0
        )
        term = jnp.dot(
            shifted[(2 - i) * S : (2 - i) * S + CELLS], weight, preferred_element_type=F32
        )
        act_grad = term if act_grad is None else act_grad + term
    act_scr[...] = act_grad

    def returned(e, start, size):
        at = pl.ds(pl.multiple_of(S + start, 16), size)
        return in_scr[seam_ref[0, e] % 4, at, :].astype(F32)

    own_rows = place * ROWS
    act_scr[pl.ds(0, ROWS, stride=S), :] += returned(3, own_rows, ROWS)
    act_scr[pl.ds(S - 1, ROWS, stride=S), :] += returned(1, own_rows, ROWS)
    act_scr[0:S] += jnp.where(place == 0, returned(0, 0, S), 0.0)
    act_scr[CELLS - S : CELLS] += jnp.where(place == 3, returned(2, 0, S), 0.0)
    pre_grad = act_scr[...] * (sig * (1.0 + pre * (1.0 - sig)))
    pre_ref[...] = pre_grad
    gain_row = jnp.sum(pre_grad * normed, axis=0, keepdims=True)
    shift_row = jnp.sum(pre_grad, axis=0, keepdims=True)
    part_ref[pl.ds(18, 64, stride=CHUNK), :] = jnp.broadcast_to(gain_row, (64, C))
    part_ref[pl.ds(19, 64, stride=CHUNK), :] = jnp.broadcast_to(shift_row, (64, C))
    for k in range(20, CHUNK):
        part_ref[pl.ds(k, 64, stride=CHUNK), :] = jnp.zeros((64, C), F32)


def end_kernel(pre_ref, xt_ref, norm_ref, gain_ref, total_ref, out_ref, sums_ref):
    mean, rstd = norm_ref[0:1], norm_ref[1:2]
    gain = gain_ref[...]
    gain_total, shift_total = total_ref[18:19], total_ref[19:20]
    first = group_sum(gain * shift_total) * (1.0 / ENTRIES)
    second = group_sum(gain * gain_total) * (1.0 / ENTRIES)
    normed = (xt_ref[...].astype(F32) - mean) * rstd
    out = rstd * (pre_ref[...] * gain - first - normed * second)
    out_ref[0] = out.T.astype(BF16)
    sums_ref[...] = jnp.concatenate([gain_total, shift_total], axis=0) * SCALE


def shape(dims, dtype):
    return jax.ShapeDtypeStruct(dims, dtype)


def body(features, cotangent, conv_weight, norm_gain, norm_shift, seam_code, corner_map):
    place = lax.axis_index("zl").astype(jnp.int32).reshape(1)
    weight = conv_weight.reshape(C, 9 * C)
    gain, shift = norm_gain.reshape(1, C), norm_shift.reshape(1, C)
    xt, ct, edges, stats = pl.pallas_call(
        start_kernel,
        out_shape=(
            shape((CELLS, C), BF16),
            shape((CELLS, C), BF16),
            shape((2 * EDGE, C), BF16),
            shape((N_NEAR, 2 * C), F32),
        ),
        in_specs=[VMEM] * 2,
        out_specs=(VMEM,) * 4,
        scratch_shapes=[pltpu.VMEM((CELLS, C), F32)] * 2,
        compiler_params=PARAMS,
    )(features, cotangent)
    others = [
        lax.ppermute(edges, "zl", [(i, (i + by) % 4) for i in range(4)]) for by in (1, 2, 3)
    ]
    stats = lax.all_to_all(stats, NEAR, 0, 0, tiled=True)
    message = shape((2 * S, C), BF16)
    *messages, rows, stats = pl.pallas_call(
        seam_kernel,
        out_shape=(message,) * 4 + (shape((4 * S, C), BF16), shape((N_FAR, 2 * C), F32)),
        in_specs=[SMEM] * 3 + [VMEM] * 6,
        out_specs=(VMEM,) * 6,
        scratch_shapes=[
            pltpu.VMEM((4, 2 * EDGE, C), BF16),
            pltpu.VMEM((2, 4, S, C), BF16),
            pltpu.VMEM((4, S, C), BF16),
        ],
        compiler_params=PARAMS,
    )(place, seam_code, corner_map, edges, *others, stats, weight)
    arrived = [
        lax.ppermute(m, TILE, [(i, (i + by) % 128) for i in range(128)])
        for m, by in zip(messages, STEPS)
    ]
    stats = lax.all_to_all(stats, FAR, 0, 0, tiled=True)
    wide = CELLS + 2 * S
    parts, pre_grad, norm = pl.pallas_call(
        main_kernel,
        out_shape=(shape((64 * CHUNK, C), F32), shape((CELLS, C), F32), shape((2, C), F32)),
        in_specs=[SMEM] * 3 + [VMEM] * 12,
        out_specs=(VMEM,) * 3,
        scratch_shapes=[
            pltpu.VMEM((4, 2 * S, C), BF16),
            pltpu.VMEM((2, 80, C), F32),
            pltpu.VMEM((wide, C), F32),
            pltpu.VMEM((wide, C), F32),
            pltpu.VMEM((CELLS, C), F32),
        ],
        compiler_params=PARAMS,
    )(place, seam_code, corner_map, xt, ct, cotangent, rows, stats, weight, gain, shift, *arrived)
    parts = lax.all_to_all(parts.reshape(2, N_FAR, CHUNK, C), "co", 0, 0, tiled=True)
    parts = lax.all_to_all(jnp.sum(parts, axis=0), FAR, 0, 0, tiled=True)
    part = jnp.sum(parts, axis=0)
    near = lax.all_to_all(
        jnp.broadcast_to(part[None], (8, CHUNK, C)), ("zh", "zl"), 0, 0, tiled=True
    )
    total = jnp.sum(near, axis=0)
    half = lax.all_to_all(
        jnp.broadcast_to(total[None], (N_FAR, CHUNK, C)), FAR, 0, 0, tiled=True
    )
    whole = lax.all_gather(half, "co", axis=0, tiled=True)
    grad_input, sums = pl.pallas_call(
        end_kernel,
        out_shape=(shape((1, C, CELLS), BF16), shape((2, C), F32)),
        in_specs=[VMEM] * 5,
        out_specs=(VMEM,) * 2,
        compiler_params=PARAMS,
    )(pre_grad, xt, norm, gain, total)
    grad_weight = jnp.concatenate([whole[:, 0:9], whole[:, 9:18]], axis=0) * SCALE
    return grad_input, grad_weight, sums[0], sums[1]


def solution(mesh):
    fine = Mesh(mesh.devices.reshape(tuple(AXES.values())), tuple(AXES))
    return jax.shard_map(
        body,
        mesh=fine,
        in_specs=(
            P(TILE, None, "zl"),
            P(TILE, None, "zl"),
            P(),
            P(),
            P(),
            P(TILE, None),
            P(TILE, None),
        ),
        out_specs=(P(TILE, None, "zl"), P(), P(), P()),
        check_vma=False,
    )
```

time: 698 us -> 139 us (0.20)
  blocking collectives: 345 us -> 49.4 us
  waiting for transfers between devices: 265 us -> 24 us
  between operations: 20.1 us -> 0.83 us
  other arithmetic: 8.54 us -> 0.21 us
  starting transfers between devices: 43.8 us -> 51.4 us
    psum x3 -> x0, blocking collectives: 303 us -> none  [the longest x1 106 us: body(): lax.psum(jnp.sum(grouped, axis=1), ('tile', 'sub')) / entries]
    psum x1 -> x0, waiting for transfers between devices: 264 us -> none  [body(): lax.psum((weight_part, gain_part, shift_part), ('tile', 'sub'))]
    all_to_all x0 -> x3, blocking collectives: none -> 42.1 us  [the longest x1 18.2 us: body(): parts = lax.all_to_all(jnp.sum(parts, axis=0), FAR, 0, 0, tiled=True)]
    all_gather x4 -> x1, blocking collectives: 42 us -> 7.28 us  [body(): whole = lax.all_gather(half, 'co', axis=0, tiled=True)]
    all_to_all x0 -> x3, starting transfers between devices: none -> 25 us  [the longest x1 10.3 us: body(): stats = lax.all_to_all(stats, NEAR, 0, 0, tiled=True)]
    ppermute x8 -> x7, starting transfers between devices: 43.7 us -> 26.4 us  [the longest x4 13.8 us: body(): lax.ppermute(m, TILE, [(i, (i + by) % 128) for i in range(128)])]
    all_to_all x0 -> x3, waiting for transfers between devices: none -> 16.7 us  [the longest x1 9.86 us: body(): lax.all_to_all(jnp.broadcast_to(total[None], (N_FAR, CHUNK, C)), FAR, 0,...]
  transfers between devices with their start and end apart: 9 -> 10, of which waited for: 2 -> 4; matrix products, arithmetic and copies ran while one was open for 0% -> 1% of each run, Pallas kernels for 0% -> 1%
where the time goes in v1:
time: 139 us
  starting transfers between devices  51.4 us (37%)
  blocking collectives  49.4 us (36%)
  waiting for transfers between devices  24 us (17%)
  local copies, waits for them, and re-layouts  7.3 us (5%)
  Pallas kernels  5.59 us (4%)
    all_to_all x1, blocking collectives, body(): parts = lax.all_to_all(jnp.sum(parts, axis=0), FAR, 0, 0, tiled=True)  18.2 us
    all_to_all x1, blocking collectives, body(): lax.all_to_all(jnp.broadcast_to(part[None], (8, CHUNK, C)), ('zh', 'zl'),...  16 us
    ppermute x4, starting transfers between devices, body(): lax.ppermute(m, TILE, [(i, (i + by) % 128) for i in range(128)])  13.8 us
    ppermute x3, starting transfers between devices, body(): lax.ppermute(edges, 'zl', [(i, (i + by) % 4) for i in range(4)])  12.6 us
    all_to_all x1, starting transfers between devices, body(): stats = lax.all_to_all(stats, NEAR, 0, 0, tiled=True)  10.3 us
    all_to_all x1, waiting for transfers between devices, body(): lax.all_to_all(jnp.broadcast_to(total[None], (N_FAR, CHUNK, C)), FAR, 0,...  9.86 us
    all_to_all x1, starting transfers between devices, body(): stats = lax.all_to_all(stats, FAR, 0, 0, tiled=True)  9.67 us
    all_to_all x1, blocking collectives, body(): lax.all_to_all(parts.reshape(2, N_FAR, CHUNK, C), 'co', 0, 0, tiled=True)  7.81 us
  transfers between devices with their start and end apart: 10, of which 4 were waited for; matrix products, arithmetic and copies ran while one was open for 1% of the time, Pallas kernels for 1%

profile of v1, /device:TPU:1, one launch (start us, length us, event | category | flops | bytes accessed | tf_op | source)
XLA Modules:
  0.0 138.7 jit_solution(3121927757079885790)
XLA Ops:
  0.6 0.9 copy-done
  1.6 0.9 copy-done.2
  3.4 8.4 %collective-permute-start.2 = (bf16[320,128]{1,0:T(8,128)(2,1)S(1)}, bf16[320,128]{1,0:T(8,128)(2,1)S(1)}, u32[]{:S(2)}, u32[]{:S(2)}) collective-permute-start(bf16[320,128]{1,0:T(8,128)(2,1)S(1)} %get-tuple-element.21.e0_ref), channel_id=1, source_target_pairs={{0,3},{1,0},{2,1},{3,2},{4,7},{5,4},{6,5},{7,6},{8,11},{9,8},{10,9... | collective-permute-start | bytes 245768 | tf_op jit(solution)/shard_map/ppermute | solution.py:278
  11.8 1.9 %collective-permute-start.1 = (bf16[320,128]{1,0:T(8,128)(2,1)S(1)}, bf16[320,128]{1,0:T(8,128)(2,1)S(1)}, u32[]{:S(2)}, u32[]{:S(2)}) collective-permute-start(bf16[320,128]{1,0:T(8,128)(2,1)S(1)} %get-tuple-element.21.e0_ref), channel_id=1, source_target_pairs={{0,2},{1,3},{2,0},{3,1},{4,6},{5,7},{6,4},{7,5},{8,10},{9,11},{10,... | collective-permute-start | bytes 245768 | tf_op jit(solution)/shard_map/ppermute | solution.py:278
  13.7 2.2 %collective-permute-start = (bf16[320,128]{1,0:T(8,128)(2,1)S(1)}, bf16[320,128]{1,0:T(8,128)(2,1)S(1)}, u32[]{:S(2)}, u32[]{:S(2)}) collective-permute-start(bf16[320,128]{1,0:T(8,128)(2,1)S(1)} %get-tuple-element.21.e0_ref), channel_id=1, source_target_pairs={{0,1},{1,2},{2,3},{3,0},{4,5},{5,6},{6,7},{7,4},{8,9},{9,10},{10,1... | collective-permute-start | bytes 245768 | tf_op jit(solution)/shard_map/ppermute | solution.py:278
  16.6 10.3 %all-to-all-start = ((f32[16,1,256]{2,1,0:T(1,128)}), f32[16,1,256]{2,1,0:T(1,128)S(1)}, u32[]{:S(2)}, u32[]{:S(2)}) async-start(f32[16,1,256]{2,1,0:T(1,128)} %copy.27), calls=%async_computation | async-start | bytes 32768 | tf_op jit(solution)/shard_map/all_to_all | solution.py:280
  27.3 6.9 %all-to-all-done = f32[16,1,256]{2,1,0:T(1,128)S(1)} async-done(((f32[16,1,256]{2,1,0:T(1,128)}), f32[16,1,256]{2,1,0:T(1,128)S(1)}, u32[]{:S(2)}, u32[]{:S(2)}) %all-to-all-start) | async-done | bytes 16416 | tf_op jit(solution)/shard_map/all_to_all | solution.py:280
  34.9 1.4 shard_map.103
  36.9 9.7 %all-to-all-start.1 = ((f32[32,1,256]{2,1,0:T(1,128)}), f32[32,1,256]{2,1,0:T(1,128)S(1)}, u32[]{:S(2)}, u32[]{:S(2)}) async-start(f32[32,1,256]{2,1,0:T(1,128)} %copy.30), calls=%async_computation.1 | async-start | bytes 65536 | tf_op jit(solution)/shard_map/all_to_all | solution.py:298
  46.5 6.6 %collective-permute-start.3 = (bf16[128,128]{1,0:T(8,128)(2,1)S(1)}, bf16[128,128]{1,0:T(8,128)(2,1)S(1)}, u32[]{:S(2)}, u32[]{:S(2)}) collective-permute-start(bf16[128,128]{1,0:T(8,128)(2,1)S(1)} %get-tuple-element.25), channel_id=1, source_target_pairs={{0,496},{4,500},{8,504},{12,508},{16,0},{20,4},{24,8},{28,12},{32,... | collective-permute-start | bytes 98312 | tf_op jit(solution)/shard_map/ppermute | solution.py:295
  53.1 3.4 %collective-permute-start.4 = (bf16[128,128]{1,0:T(8,128)(2,1)S(1)}, bf16[128,128]{1,0:T(8,128)(2,1)S(1)}, u32[]{:S(2)}, u32[]{:S(2)}) collective-permute-start(bf16[128,128]{1,0:T(8,128)(2,1)S(1)} %get-tuple-element.26), channel_id=1, source_target_pairs={{0,4},{4,8},{8,12},{12,16},{16,20},{20,24},{24,28},{28,32},{32,36}... | collective-permute-start | bytes 98312 | tf_op jit(solution)/shard_map/ppermute | solution.py:295
  56.6 1.9 %collective-permute-start.5 = (bf16[128,128]{1,0:T(8,128)(2,1)S(1)}, bf16[128,128]{1,0:T(8,128)(2,1)S(1)}, u32[]{:S(2)}, u32[]{:S(2)}) collective-permute-start(bf16[128,128]{1,0:T(8,128)(2,1)S(1)} %get-tuple-element.27), channel_id=1, source_target_pairs={{0,16},{4,20},{8,24},{12,28},{16,32},{20,36},{24,40},{28,44},{32,4... | collective-permute-start | bytes 98312 | tf_op jit(solution)/shard_map/ppermute | solution.py:295
  58.5 1.9 %collective-permute-start.6 = (bf16[128,128]{1,0:T(8,128)(2,1)S(1)}, bf16[128,128]{1,0:T(8,128)(2,1)S(1)}, u32[]{:S(2)}, u32[]{:S(2)}) collective-permute-start(bf16[128,128]{1,0:T(8,128)(2,1)S(1)} %get-tuple-element.28), channel_id=1, source_target_pairs={{0,508},{4,0},{8,4},{12,8},{16,12},{20,16},{24,20},{28,24},{32,28}... | collective-permute-start | bytes 98312 | tf_op jit(solution)/shard_map/ppermute | solution.py:295
  60.5 4.6 %collective-permute-done.5.a2_ref = bf16[128,128]{1,0:T(8,128)(2,1)S(1)} collective-permute-done((bf16[128,128]{1,0:T(8,128)(2,1)S(1)}, bf16[128,128]{1,0:T(8,128)(2,1)S(1)}, u32[]{:S(2)}, u32[]{:S(2)}) %collective-permute-start.5) | collective-permute-done | bytes 32800 | tf_op jit(solution)/shard_map/ppermute | solution.py:295
  65.0 2.7 %collective-permute-done.6.a3_ref = bf16[128,128]{1,0:T(8,128)(2,1)S(1)} collective-permute-done((bf16[128,128]{1,0:T(8,128)(2,1)S(1)}, bf16[128,128]{1,0:T(8,128)(2,1)S(1)}, u32[]{:S(2)}, u32[]{:S(2)}) %collective-permute-start.6) | collective-permute-done | bytes 32800 | tf_op jit(solution)/shard_map/ppermute | solution.py:295
  68.4 2.4 %shard_map.104 = (f32[1536,128]{1,0:T(8,128)S(1)}, f32[1024,128]{1,0:T(8,128)S(1)}, f32[2,128]{1,0:T(2,128)S(1)}) custom-call(s32[1]{0:T(128)} %bitcast.place_ref, s32[1,4]{1,0:T(1,128)S(1)} %copy-done.3, s32[1,4]{1,0:T(1,128)S(1)} %copy-done.4, bf16[1024,128]{1,0:T(8,128)(2,1)S(1)} %get-tuple-element.19.xt_ref, ...), custom_call_target="tpu_custom_call" | custom-call | tf_op jit(solution)/shard_map/pallas_call | solution.py:300
  70.8 7.8 %all_to_all.42 = f32[2,32,24,128]{3,2,1,0:T(8,128)S(1)} all-to-all(f32[2,32,24,128]{3,2,1,0:T(8,128)S(1)} %bitcast.17), channel_id=1, replica_groups=mesh['y'=8,'x'=4,'zh'=2,'co'=2,'zl'=4] {'co'}, dimensions={0} | all-to-all | bytes 1572864 | tf_op jit(solution)/shard_map/all_to_all | solution.py:314
  78.6 18.2 %all_to_all.43 = f32[32,24,128]{2,1,0:T(8,128)S(1)} all-to-all(f32[32,24,128]{2,1,0:T(8,128)S(1)} %reduce_sum.27), channel_id=1, replica_groups=mesh['y'=8,'x'=4,'zh'=2,'co'=2,'zl'=4] {'y','x'}, dimensions={0} | all-to-all | bytes 786432 | tf_op jit(solution)/shard_map/all_to_all | solution.py:315
  96.9 16.0 %all_to_all.44 = f32[8,24,128]{2,1,0:T(8,128)S(1)} all-to-all(f32[8,24,128]{2,1,0:T(8,128)S(1)} %broadcast_in_dim.4), channel_id=1, replica_groups=mesh['y'=8,'x'=4,'zh'=2,'co'=2,'zl'=4] {'zh','zl'}, dimensions={0} | all-to-all | bytes 196608 | tf_op jit(solution)/shard_map/all_to_all | solution.py:317
  113.7 5.1 %all-to-all-start.5 = ((f32[32,24,128]{2,1,0:T(8,128)}), f32[32,24,128]{2,1,0:T(8,128)S(1)}, u32[]{:S(2)}, u32[]{:S(2)}) async-start(f32[32,24,128]{2,1,0:T(8,128)} %broadcast_in_dim.5), calls=%async_computation.5 | async-start | bytes 786432 | tf_op jit(solution)/shard_map/all_to_all | solution.py:321
  118.8 1.1 shard_map.105
  120.4 9.9 %all-to-all-done.5 = f32[32,24,128]{2,1,0:T(8,128)S(1)} async-done(((f32[32,24,128]{2,1,0:T(8,128)}), f32[32,24,128]{2,1,0:T(8,128)S(1)}, u32[]{:S(2)}, u32[]{:S(2)}) %all-to-all-start.5) | async-done | bytes 393248 | tf_op jit(solution)/shard_map/all_to_all | solution.py:321
  130.3 7.3 %all_gather.3 = f32[64,24,128]{2,1,0:T(8,128)S(1)} all-gather(f32[32,24,128]{2,1,0:T(8,128)S(1)} %all-to-all-done.5), channel_id=1, replica_groups=mesh['y'=8,'x'=4,'zh'=2,'co'=2,'zl'=4] {'co'}, dimensions={0}, use_global_device_ids=true | all-gather | bytes 1179648 | tf_op jit(solution)/shard_map/all_gather | solution.py:324
  137.7 1.0 copy.32
  (35 shorter events, 5.5 us)
Async XLA Ops:
  0.6 1.0 copy-start
  1.6 0.9 copy-start.2
  2.5 24.3 %copy-start.7 = (bf16[128,9,128]{2,0,1:T(8,128)(2,1)S(1)}, bf16[128,9,128]{2,0,1:T(8,128)(2,1)}, u32[]{:S(2)}) copy-start(bf16[128,9,128]{2,0,1:T(8,128)(2,1)} %param.9) | copy-start | bytes 884740
  3.4 30.8 %collective-permute-start.2 = (bf16[320,128]{1,0:T(8,128)(2,1)S(1)}, bf16[320,128]{1,0:T(8,128)(2,1)S(1)}, u32[]{:S(2)}, u32[]{:S(2)}) collective-permute-start(bf16[320,128]{1,0:T(8,128)(2,1)S(1)} %get-tuple-element.21.e0_ref), channel_id=1, source_target_pairs={{0,3},{1,0},{2,1},{3,2},{4,7},{5,4},{6,5},{7,6},{8,11},{9,8},{10,9... | collective-permute-start | bytes 245768 | tf_op jit(solution)/shard_map/ppermute | solution.py:278
  11.8 22.4 %collective-permute-start.1 = (bf16[320,128]{1,0:T(8,128)(2,1)S(1)}, bf16[320,128]{1,0:T(8,128)(2,1)S(1)}, u32[]{:S(2)}, u32[]{:S(2)}) collective-permute-start(bf16[320,128]{1,0:T(8,128)(2,1)S(1)} %get-tuple-element.21.e0_ref), channel_id=1, source_target_pairs={{0,2},{1,3},{2,0},{3,1},{4,6},{5,7},{6,4},{7,5},{8,10},{9,11},{10,... | collective-permute-start | bytes 245768 | tf_op jit(solution)/shard_map/ppermute | solution.py:278
  13.7 20.4 %collective-permute-start = (bf16[320,128]{1,0:T(8,128)(2,1)S(1)}, bf16[320,128]{1,0:T(8,128)(2,1)S(1)}, u32[]{:S(2)}, u32[]{:S(2)}) collective-permute-start(bf16[320,128]{1,0:T(8,128)(2,1)S(1)} %get-tuple-element.21.e0_ref), channel_id=1, source_target_pairs={{0,1},{1,2},{2,3},{3,0},{4,5},{5,6},{6,7},{7,4},{8,9},{9,10},{10,1... | collective-permute-start | bytes 245768 | tf_op jit(solution)/shard_map/ppermute | solution.py:278
  16.6 17.6 %all-to-all-start = ((f32[16,1,256]{2,1,0:T(1,128)}), f32[16,1,256]{2,1,0:T(1,128)S(1)}, u32[]{:S(2)}, u32[]{:S(2)}) async-start(f32[16,1,256]{2,1,0:T(1,128)} %copy.27), calls=%async_computation | async-start | bytes 32768 | tf_op jit(solution)/shard_map/all_to_all | solution.py:280
  34.2 0.7 copy-start.3
  34.2 0.7 copy-start.4
  34.9 32.9 %copy-start.1 = (bf16[1,128,1024]{2,1,0:T(8,128)(2,1)S(1)}, bf16[1,128,1024]{2,1,0:T(8,128)(2,1)}, u32[]{:S(2)}) copy-start(bf16[1,128,1024]{2,1,0:T(8,128)(2,1)} %cot_ref.1) | copy-start | bytes 786436
  36.9 23.6 %all-to-all-start.1 = ((f32[32,1,256]{2,1,0:T(1,128)}), f32[32,1,256]{2,1,0:T(1,128)S(1)}, u32[]{:S(2)}, u32[]{:S(2)}) async-start(f32[32,1,256]{2,1,0:T(1,128)} %copy.30), calls=%async_computation.1 | async-start | bytes 65536 | tf_op jit(solution)/shard_map/all_to_all | solution.py:298
  46.5 13.9 %collective-permute-start.3 = (bf16[128,128]{1,0:T(8,128)(2,1)S(1)}, bf16[128,128]{1,0:T(8,128)(2,1)S(1)}, u32[]{:S(2)}, u32[]{:S(2)}) collective-permute-start(bf16[128,128]{1,0:T(8,128)(2,1)S(1)} %get-tuple-element.25), channel_id=1, source_target_pairs={{0,496},{4,500},{8,504},{12,508},{16,0},{20,4},{24,8},{28,12},{32,... | collective-permute-start | bytes 98312 | tf_op jit(solution)/shard_map/ppermute | solution.py:295
  53.1 7.3 %collective-permute-start.4 = (bf16[128,128]{1,0:T(8,128)(2,1)S(1)}, bf16[128,128]{1,0:T(8,128)(2,1)S(1)}, u32[]{:S(2)}, u32[]{:S(2)}) collective-permute-start(bf16[128,128]{1,0:T(8,128)(2,1)S(1)} %get-tuple-element.26), channel_id=1, source_target_pairs={{0,4},{4,8},{8,12},{12,16},{16,20},{20,24},{24,28},{28,32},{32,36}... | collective-permute-start | bytes 98312 | tf_op jit(solution)/shard_map/ppermute | solution.py:295
  56.6 8.5 %collective-permute-start.5 = (bf16[128,128]{1,0:T(8,128)(2,1)S(1)}, bf16[128,128]{1,0:T(8,128)(2,1)S(1)}, u32[]{:S(2)}, u32[]{:S(2)}) collective-permute-start(bf16[128,128]{1,0:T(8,128)(2,1)S(1)} %get-tuple-element.27), channel_id=1, source_target_pairs={{0,16},{4,20},{8,24},{12,28},{16,32},{20,36},{24,40},{28,44},{32,4... | collective-permute-start | bytes 98312 | tf_op jit(solution)/shard_map/ppermute | solution.py:295
  58.5 9.2 %collective-permute-start.6 = (bf16[128,128]{1,0:T(8,128)(2,1)S(1)}, bf16[128,128]{1,0:T(8,128)(2,1)S(1)}, u32[]{:S(2)}, u32[]{:S(2)}) collective-permute-start(bf16[128,128]{1,0:T(8,128)(2,1)S(1)} %get-tuple-element.28), channel_id=1, source_target_pairs={{0,508},{4,0},{8,4},{12,8},{16,12},{20,16},{24,20},{28,24},{32,28}... | collective-permute-start | bytes 98312 | tf_op jit(solution)/shard_map/ppermute | solution.py:295
  67.7 0.7 copy-start.5
  67.7 0.7 copy-start.6
  113.7 16.5 %all-to-all-start.5 = ((f32[32,24,128]{2,1,0:T(8,128)}), f32[32,24,128]{2,1,0:T(8,128)S(1)}, u32[]{:S(2)}, u32[]{:S(2)}) async-start(f32[32,24,128]{2,1,0:T(8,128)} %broadcast_in_dim.5), calls=%async_computation.5 | async-start | bytes 786432 | tf_op jit(solution)/shard_map/all_to_all | solution.py:321

commit v2 on v1

v2 whole, which is shorter than its diff:
```python
import functools
import math

import jax
import jax.numpy as jnp
from jax import lax
from jax.experimental import pallas as pl
from jax.experimental.pallas import tpu as pltpu
from jax.sharding import Mesh
from jax.sharding import PartitionSpec as P

GC = 4
S = 64
PER_GROUP = 8
EPSILON = 1e-05
STEPS = (-GC, 1, GC, -1)
ROWS = 16
CELLS = ROWS * S
C = 128
LINE = 2 * S
CHUNK = 20

TILE = ("y", "x", "zh", "co")
AXES = {"y": 8, "x": 4, "zh": 2, "co": 2, "zl": 4}
NEAR = ("zh", "co", "zl")
FAR = ("y", "x")
N_NEAR = 16
N_FAR = 32
DEVICES = 512
ENTRIES = DEVICES * CELLS * PER_GROUP
LOCAL = CELLS * PER_GROUP
SCALE = 1.0 / math.sqrt(DEVICES * CELLS)

F32 = jnp.float32
BF16 = jnp.bfloat16
VMEM = pl.BlockSpec(memory_space=pltpu.VMEM)
SMEM = pl.BlockSpec(memory_space=pltpu.SMEM)
PARAMS = pltpu.CompilerParams(vmem_limit_bytes=40 * 1024 * 1024)


def group_sum(row):
    total = jnp.broadcast_to(row, (8, C))
    lane = lax.broadcasted_iota(jnp.int32, (8, C), 1)
    for by in (1, 2, 4):
        other = jnp.where(
            (lane & by) != 0, pltpu.roll(total, by, 1), pltpu.roll(total, C - by, 1)
        )
        total = total + other
    return total[0:1]


def packed(mean, spread):
    lane = lax.broadcasted_iota(jnp.int32, (1, C), 1)
    return jnp.where(lane % 2 == 0, mean, spread)


def unpacked(row):
    row = jnp.broadcast_to(row, (8, C))
    even = lax.broadcasted_iota(jnp.int32, (8, C), 1) % 2 == 0
    mean = jnp.where(even, row, pltpu.roll(row, 1, 1))
    spread = jnp.where(even, pltpu.roll(row, C - 1, 1), row)
    return mean[0:1], spread[0:1]


def merge(rows, count):
    means, squares = zip(*[unpacked(row) for row in rows])
    mean = sum(means) * (1.0 / len(means))
    spread = sum(squares) + float(count) * sum((m - mean) * (m - mean) for m in means)
    return mean, spread


def start_kernel(
    info_ref, gain_ref, shift_ref, x_ref, c_ref,
    xt_ref, ct_ref, send_ref, keep_ref, stat_ref, x_scr, c_scr, side_scr,
):
    place = info_ref[0]
    half = place // 2
    x = x_ref[0].astype(F32).T
    x_scr[...] = x
    xt_ref[...] = x.astype(BF16)
    mean = group_sum(jnp.sum(x, axis=0, keepdims=True)) * (1.0 / LOCAL)
    gap = x - mean
    spread = group_sum(jnp.sum(gap * gap, axis=0, keepdims=True))
    stat_ref[...] = jnp.broadcast_to(packed(mean, spread)[None], (N_FAR, 1, C))
    c = c_ref[0].astype(F32).T
    c_scr[...] = c
    ct_ref[...] = c.astype(BF16)
    zero = jnp.zeros((S, C), BF16)
    own = pl.ds(pl.multiple_of(place * ROWS, ROWS), ROWS)
    for kind, (scr, flat) in enumerate(((x_scr, xt_ref), (c_scr, ct_ref))):
        first, last = flat[0:S], flat[CELLS - S : CELLS]
        side_scr[kind, 0] = jnp.where(place == 0, first, zero)
        side_scr[kind, 2] = jnp.where(place == 3, last, zero)
        for side, column in ((1, S - 1), (3, 0)):
            side_scr[kind, side] = zero
            side_scr[kind, side, own, :] = scr[pl.ds(column, ROWS, stride=S), :].astype(BF16)
        send_ref[2, kind * S : (kind + 1) * S] = jnp.where(place == 1, last, first)
        for k in range(2):
            at = slice(kind * S, (kind + 1) * S)
            send_ref[k, at] = side_scr[kind, side_facing(info_ref, 2 - 2 * half + k)]
            keep_ref[k, at] = side_scr[kind, side_facing(info_ref, 2 * half + k)]


def middle_kernel(
    info_ref, keep_ref, in_ref, xt_ref, ct_ref, in_stat_ref, send_ref, left_ref, stat_ref
):
    odd = info_ref[0] % 2
    send_ref[0] = keep_ref[1 - odd] + in_ref[1 - odd]
    left_ref[...] = keep_ref[odd] + in_ref[odd]
    send_ref[2] = in_ref[2]
    stat_ref[...] = packed(*merge([in_stat_ref[k] for k in range(N_FAR)], LOCAL))[None]
    for kind, flat in enumerate((xt_ref, ct_ref)):
        send_ref[1, kind * S : (kind + 1) * S] = jnp.where(
            odd == 1, flat[0:S], flat[CELLS - S : CELLS]
        )


def side_facing(info_ref, direction):
    side = jnp.int32(0)
    for e in range(1, 4):
        side = jnp.where(info_ref[1 + e] % 4 == direction, e, side)
    return side


def side_parts(info_ref, side):
    first = jnp.where(side == 1, 2, jnp.where(side == 2, 6, 0))
    step = jnp.where(side % 2 == 1, 3, 1)
    start = jnp.where(side == 1, 1, jnp.where(side == 2, 3, 0))
    end = jnp.where(side == 0, 1, jnp.where(side == 3, 3, 2))
    mine = side % 2
    taps = [first, first + step, first + 2 * step]
    return taps, info_ref[5 + start] == mine, info_ref[5 + end] == mine


def flip_matrix():
    a = lax.broadcasted_iota(jnp.int32, (S, S), 0)
    b = lax.broadcasted_iota(jnp.int32, (S, S), 1)
    return jnp.where(a + b == S - 1, 1.0, 0.0).astype(BF16)


def turned(strip, flag):
    back = jnp.dot(flip_matrix(), strip, preferred_element_type=F32)
    return jnp.where(flag == 1, back, strip.astype(F32)).astype(BF16)


def seam_kernel(
    info_ref, keep_ref, in_ref, in_stat_ref, w_ref, message_ref, strips_ref, rows_ref, stat_ref,
):
    place = info_ref[0]
    odd = place % 2 == 1
    side = side_facing(info_ref, place)
    strips = keep_ref[...] + in_ref[0]
    strips_ref[...] = strips
    grads = strips[S : 2 * S]
    taps, at_start, at_end = side_parts(info_ref, side)
    parts = [jnp.dot(grads, w_ref[tap], preferred_element_type=F32) for tap in taps]
    row = lax.broadcasted_iota(jnp.int32, (S, C), 0)
    first, last = row == 0, row == S - 1
    grad = parts[1]
    grad = grad + jnp.where(last, 0.0, pltpu.roll(parts[0], S - 1, 0))
    grad = grad + jnp.where(first, 0.0, pltpu.roll(parts[2], 1, 0))
    grad = grad + jnp.where(first & at_start, parts[0], 0.0)
    grad = grad + jnp.where(last & at_end, parts[2], 0.0)
    message_ref[0:S] = strips[0:S]
    message_ref[S : 2 * S] = turned(grad.astype(BF16), info_ref[1 + side] // 4)
    direct, passed = in_ref[1], in_ref[2]
    above, below = jnp.where(odd, direct, passed), jnp.where(odd, passed, direct)
    zero = jnp.zeros((S, C), BF16)
    rows_ref[0:S] = above[0:S]
    rows_ref[S : 2 * S] = below[0:S]
    rows_ref[2 * S : 3 * S] = jnp.where(place == 0, zero, above[S : 2 * S])
    rows_ref[3 * S : 4 * S] = jnp.where(place == 3, zero, below[S : 2 * S])
    stat_ref[...] = jnp.broadcast_to(in_stat_ref[...], (N_NEAR, 1, C))


def main_kernel(
    info_ref, xt_ref, ct_ref, cot_ref, rows_ref, in_stat_ref, w_ref, gain_ref, shift_ref,
    strips_ref, in_ref, part_ref, pre_ref, norm_ref, weight_scr,
):
    place = info_ref[0]
    mean, spread = merge([in_stat_ref[k] for k in range(N_NEAR)], LOCAL * N_FAR)
    rstd = lax.rsqrt(spread * (1.0 / ENTRIES) + EPSILON)
    gain, shift = gain_ref[...], shift_ref[...]
    norm_ref[...] = jnp.concatenate([mean, rstd], axis=0)

    def affine(raw):
        normed = (raw.astype(F32) - mean) * rstd
        pre = normed * gain + shift
        return normed, pre, 1.0 / (1.0 + jnp.exp(-pre))

    def activated(raw):
        _, pre, sig = affine(raw)
        return (pre * sig).astype(BF16).astype(F32)

    wide = CELLS + 2 * S
    column = lax.broadcasted_iota(jnp.int32, (wide, C), 0) & (S - 1)
    starts, ends = column == 0, column == S - 1

    def beside(middle):
        before = jnp.where(starts, 0.0, pltpu.roll(middle, 1, 0))
        after = jnp.where(ends, 0.0, pltpu.roll(middle, wide - 1, 0))
        return before.astype(BF16), middle.astype(BF16), after.astype(BF16)

    top = jnp.where(place == 0, 0.0, activated(rows_ref[0:S]))
    bottom = jnp.where(place == 3, 0.0, activated(rows_ref[S : 2 * S]))
    normed, pre, sig = affine(xt_ref[...])
    own = (pre * sig).astype(BF16).astype(F32)
    windows = jnp.concatenate(beside(jnp.concatenate([top, own, bottom], axis=0)), axis=1)
    grad_out = cot_ref[0]
    for i in range(3):
        part = jnp.dot(grad_out, windows[i * S : i * S + CELLS], preferred_element_type=F32)
        for j in range(3):
            weight_scr[3 * i + j] = part[:, j * C : (j + 1) * C]

    side = side_facing(info_ref, place)
    taps, at_start, at_end = side_parts(info_ref, side)
    halo = activated(turned(in_ref[0:S], info_ref[1 + side] // 4)).astype(BF16)
    halo = jnp.concatenate([halo, halo], axis=0)
    strip = strips_ref[S : 2 * S].astype(F32)
    row = lax.broadcasted_iota(jnp.int32, (S, C), 0)
    first, last = row == 0, row == S - 1
    lines = (
        (jnp.where(last, 0.0, pltpu.roll(strip, S - 1, 0)), jnp.where(first & at_start, strip, 0.0)),
        (strip, jnp.zeros((S, C), F32)),
        (jnp.where(first, 0.0, pltpu.roll(strip, 1, 0)), jnp.where(last & at_end, strip, 0.0)),
    )
    for tap, pair in zip(taps, lines):
        weight_scr[tap] += lax.dot_general(
            jnp.concatenate(pair, axis=0).astype(BF16),
            halo,
            (((0,), (0,)), ((), ())),
            preferred_element_type=F32,
        )
    for tap in range(9):
        for h in range(2):
            part_ref[pl.ds(h * 9 + tap, 64, stride=CHUNK), :] = weight_scr[
                tap, h * 64 : (h + 1) * 64
            ]

    grads = jnp.concatenate(
        [rows_ref[2 * S : 3 * S], ct_ref[...], rows_ref[3 * S : 4 * S]], axis=0
    ).astype(F32)
    shifted = jnp.concatenate(beside(grads)[::-1], axis=1)
    act_grad = None
    for i in range(3):
        weight = jnp.concatenate([w_ref[3 * i + j] for j in range(3)], axis=0)
        term = jnp.dot(
            shifted[(2 - i) * S : (2 - i) * S + CELLS], weight, preferred_element_type=F32
        )
        act_grad = term if act_grad is None else act_grad + term
    pre_grad = act_grad * (sig * (1.0 + pre * (1.0 - sig)))
    pre_ref[...] = pre_grad
    gain_row = jnp.sum(pre_grad * normed, axis=0, keepdims=True)
    shift_row = jnp.sum(pre_grad, axis=0, keepdims=True)
    normed, pre, sig = affine(strips_ref[0:S])
    more = in_ref[S : 2 * S].astype(F32) * (sig * (1.0 + pre * (1.0 - sig)))
    gain_row = gain_row + jnp.sum(more * normed, axis=0, keepdims=True)
    shift_row = shift_row + jnp.sum(more, axis=0, keepdims=True)
    part_ref[pl.ds(18, 64, stride=CHUNK), :] = jnp.broadcast_to(gain_row, (64, C))
    part_ref[pl.ds(19, 64, stride=CHUNK), :] = jnp.broadcast_to(shift_row, (64, C))


def end_kernel(
    info_ref, pre_ref, xt_ref, norm_ref, gain_ref, shift_ref, total_ref, pair_ref, others_ref,
    out_ref, sums_ref, side_scr, more_scr,
):
    place = info_ref[0]
    base, odd = place // 2 * 2, place % 2
    for k in range(2):
        at = (odd + k) % 2
        side_scr[base + at] = pair_ref[k]
        side_scr[(base + 2) % 4 + at] = others_ref[k]
    own = pl.ds(pl.multiple_of(place * ROWS, ROWS), ROWS)
    more_scr[...] = jnp.zeros((CELLS, C), F32)
    more_scr[0:S] = jnp.where(place == 0, side_scr[info_ref[1] % 4].astype(F32), 0.0)
    more_scr[CELLS - S : CELLS] = jnp.where(place == 3, side_scr[info_ref[3] % 4].astype(F32), 0.0)
    for e, at in ((4, 0), (2, S - 1)):
        more_scr[pl.ds(at, ROWS, stride=S), :] += side_scr[info_ref[e] % 4, own, :].astype(F32)
    mean, rstd = norm_ref[0:1], norm_ref[1:2]
    gain = gain_ref[...]
    gain_total, shift_total = total_ref[18:19], total_ref[19:20]
    first = group_sum(gain * shift_total) * (1.0 / ENTRIES)
    second = group_sum(gain * gain_total) * (1.0 / ENTRIES)
    normed = (xt_ref[...].astype(F32) - mean) * rstd
    pre = normed * gain + shift_ref[...]
    sig = 1.0 / (1.0 + jnp.exp(-pre))
    pre_grad = pre_ref[...] + more_scr[...] * (sig * (1.0 + pre * (1.0 - sig)))
    out = rstd * (pre_grad * gain - first - normed * second)
    out_ref[0] = out.T.astype(BF16)
    sums_ref[...] = jnp.concatenate([gain_total, shift_total], axis=0) * SCALE


def weight_kernel(whole_ref, out_ref):
    for tap in range(9):
        for h in range(2):
            out_ref[tap, h * 64 : (h + 1) * 64] = (
                whole_ref[pl.ds(h * 9 + tap, 64, stride=CHUNK), :] * SCALE
            )


def sum_kernel(parts, copies, in_ref, out_ref):
    rows = in_ref.shape[0] // parts
    total = in_ref[0:rows]
    for k in range(1, parts):
        total = total + in_ref[k * rows : (k + 1) * rows]
    for k in range(copies):
        out_ref[k * rows : (k + 1) * rows] = total


def summed(x, parts, copies):
    rows = x.size // C
    return pl.pallas_call(
        functools.partial(sum_kernel, parts, copies),
        out_shape=shape((rows // parts * copies, C), F32),
        in_specs=[VMEM],
        out_specs=VMEM,
        compiler_params=PARAMS,
    )(x.reshape(rows, C))


def sum_and_pair_kernel(parts, copies, in_ref, own_ref, other_ref, out_ref, pair_ref):
    pair_ref[0] = own_ref[S : 2 * S]
    pair_ref[1] = other_ref[S : 2 * S]
    sum_kernel(parts, copies, in_ref, out_ref)


def exchanged(x, axes, parts):
    x = x.reshape(parts, x.shape[0] // parts // 4, 4, C)
    return lax.all_to_all(x, axes, 0, 0, tiled=True)


def shape(dims, dtype):
    return jax.ShapeDtypeStruct(dims, dtype)


def body(features, cotangent, conv_weight, norm_gain, norm_shift, seam_code, corner_map):
    place = lax.axis_index("zl").astype(jnp.int32).reshape(1)
    info = jnp.concatenate([place, seam_code[0], corner_map[0]])
    weight = conv_weight.transpose(1, 0, 2)
    gain, shift = norm_gain.reshape(1, C), norm_shift.reshape(1, C)
    xt, ct, send, keep, stats = pl.pallas_call(
        start_kernel,
        out_shape=(
            shape((CELLS, C), BF16),
            shape((CELLS, C), BF16),
            shape((3, LINE, C), BF16),
            shape((2, LINE, C), BF16),
            shape((N_FAR, 1, C), F32),
        ),
        in_specs=[SMEM] + [VMEM] * 4,
        out_specs=(VMEM,) * 5,
        scratch_shapes=[pltpu.VMEM((CELLS, C), F32)] * 2 + [pltpu.VMEM((2, 4, S, C), BF16)],
        compiler_params=PARAMS,
    )(info, gain, shift, features, cotangent)
    came = lax.ppermute(send, "zl", [(i, i ^ 2) for i in range(4)])
    stats = lax.all_to_all(stats, FAR, 0, 0, tiled=True)
    send, keep, stats = pl.pallas_call(
        middle_kernel,
        out_shape=(shape((3, LINE, C), BF16), shape((LINE, C), BF16), shape((1, 1, C), F32)),
        in_specs=[SMEM] + [VMEM] * 5,
        out_specs=(VMEM,) * 3,
        compiler_params=PARAMS,
    )(info, keep, came, xt, ct, stats)
    came = lax.ppermute(send, "zl", [(i, i ^ 1) for i in range(4)])
    message, strips, rows, stats = pl.pallas_call(
        seam_kernel,
        out_shape=(
            shape((LINE, C), BF16),
            shape((LINE, C), BF16),
            shape((2 * LINE, C), BF16),
            shape((N_NEAR, 1, C), F32),
        ),
        in_specs=[SMEM] + [VMEM] * 4,
        out_specs=(VMEM,) * 4,
        compiler_params=PARAMS,
    )(info, keep, came, stats, weight)
    message = lax.ppermute(
        message,
        tuple(AXES),
        [(4 * t + s, 4 * ((t + STEPS[s]) % 128) + (s + 2) % 4) for t in range(128) for s in range(4)],
    )
    stats = lax.all_to_all(stats, NEAR, 0, 0, tiled=True)
    parts, pre_grad, norm = pl.pallas_call(
        main_kernel,
        out_shape=(
            shape((64 * CHUNK, C), F32),
            shape((CELLS, C), F32),
            shape((2, C), F32),
        ),
        in_specs=[SMEM] + [VMEM] * 10,
        out_specs=(VMEM,) * 3,
        scratch_shapes=[pltpu.VMEM((9, C, C), F32)],
        compiler_params=PARAMS,
    )(info, xt, ct, cotangent, rows, stats, weight, gain, shift, strips, message)
    other = lax.ppermute(message, "zl", [(i, i ^ 1) for i in range(4)])
    parts = summed(exchanged(parts, "co", 2), 2, 1)
    parts, pair = pl.pallas_call(
        functools.partial(sum_and_pair_kernel, N_FAR, 8),
        out_shape=(shape((8 * CHUNK, C), F32), shape((2, S, C), BF16)),
        in_specs=[VMEM] * 3,
        out_specs=(VMEM,) * 2,
        compiler_params=PARAMS,
    )(exchanged(parts, FAR, N_FAR).reshape(N_FAR * CHUNK, C), message, other)
    others = lax.ppermute(pair, "zl", [(i, i ^ 2) for i in range(4)])
    parts = summed(exchanged(parts, ("zh", "zl"), 8), 8, N_FAR)
    half = exchanged(parts, FAR, N_FAR)
    whole = lax.all_gather(half, "co", axis=0, tiled=True)
    grad_input, sums = pl.pallas_call(
        end_kernel,
        out_shape=(shape((1, C, CELLS), BF16), shape((2, C), F32)),
        in_specs=[SMEM] + [VMEM] * 8,
        out_specs=(VMEM,) * 2,
        scratch_shapes=[pltpu.VMEM((4, S, C), BF16), pltpu.VMEM((CELLS, C), F32)],
        compiler_params=PARAMS,
    )(info, pre_grad, xt, norm, gain, shift, parts, pair, others)
    grad_weight = pl.pallas_call(
        weight_kernel,
        out_shape=shape((9, C, C), F32),
        in_specs=[VMEM],
        out_specs=VMEM,
        compiler_params=PARAMS,
    )(whole.reshape(64 * CHUNK, C)).transpose(1, 0, 2)
    return grad_input, grad_weight, sums[0], sums[1]


def solution(mesh):
    fine = Mesh(mesh.devices.reshape(tuple(AXES.values())), tuple(AXES))
    return jax.shard_map(
        body,
        mesh=fine,
        in_specs=(
            P(TILE, None, "zl"),
            P(TILE, None, "zl"),
            P(),
            P(),
            P(),
            P(TILE, None),
            P(TILE, None),
        ),
        out_specs=(P(TILE, None, "zl"), P(), P(), P()),
        check_vma=False,
    )
```

time: 139 us -> 119 us (0.86)
  starting transfers between devices: 51.4 us -> 27.9 us
  blocking collectives: 49.4 us -> 57.6 us
  waiting for transfers between devices: 24 us -> 18.5 us
  Pallas kernels: 5.59 us -> 10 us
  local copies, waits for them, and re-layouts: 7.3 us -> 3.75 us
    all_to_all x3 -> x2, starting transfers between devices: 25 us -> 10.3 us  [exchanged(): return lax.all_to_all(x, axes, 0, 0, tiled=True)]
    all_to_all x3 -> x4, blocking collectives: 42.1 us -> 51.1 us  [the longest x1 18.7 us: body(): stats = lax.all_to_all(stats, NEAR, 0, 0, tiled=True)]
    ppermute x7 -> x5, starting transfers between devices: 26.4 us -> 17.6 us  [the longest x1 6.64 us: body(): came = lax.ppermute(send, 'zl', [(i, i ^ 2) for i in range(4)])]
    all_to_all x3 -> x2, waiting for transfers between devices: 16.7 us -> 9.94 us  [exchanged(): return lax.all_to_all(x, axes, 0, 0, tiled=True)]
    pallas_call x1 -> x6, Pallas kernels: 1.35 us -> 3.97 us  [the longest x2 1.51 us: summed(): pl.pallas_call(functools.partial(sum_kernel, parts, copies), out_shape=sh...]
    ppermute x7 -> x5, waiting for transfers between devices: 7.28 us -> 8.59 us  [the longest x1 3.87 us: body(): others = lax.ppermute(pair, 'zl', [(i, i ^ 2) for i in range(4)])]
    unnamed x20 -> x16, local copies, waits for them, and re-layouts: 4.45 us -> 3.24 us
  transfers between devices with their start and end apart: 10 -> 7, of which waited for: 4 -> 5; matrix products, arithmetic and copies ran while one was open for 1% -> 0% of each run, Pallas kernels for 1% -> 2%
where the time goes in v2:
time: 119 us
  blocking collectives  57.6 us (48%)
  starting transfers between devices  27.9 us (23%)
  waiting for transfers between devices  18.5 us (16%)
  Pallas kernels  10 us (8%)
  local copies, waits for them, and re-layouts  3.75 us (3%)
    all_to_all x1, blocking collectives, body(): stats = lax.all_to_all(stats, NEAR, 0, 0, tiled=True)  18.7 us
    all_to_all x1, blocking collectives, body(): stats = lax.all_to_all(stats, FAR, 0, 0, tiled=True)  18.1 us
    all_to_all x2, blocking collectives, exchanged(): return lax.all_to_all(x, axes, 0, 0, tiled=True)  14.3 us
    all_to_all x2, starting transfers between devices, exchanged(): return lax.all_to_all(x, axes, 0, 0, tiled=True)  10.3 us
    all_to_all x2, waiting for transfers between devices, exchanged(): return lax.all_to_all(x, axes, 0, 0, tiled=True)  9.94 us
    ppermute x1, starting transfers between devices, body(): came = lax.ppermute(send, 'zl', [(i, i ^ 2) for i in range(4)])  6.64 us
    all_gather x1, blocking collectives, body(): whole = lax.all_gather(half, 'co', axis=0, tiled=True)  6.52 us
    ppermute x1, starting transfers between devices, body(): came = lax.ppermute(send, 'zl', [(i, i ^ 1) for i in range(4)])  4.13 us
  transfers between devices with their start and end apart: 7, of which 5 were waited for; matrix products, arithmetic and copies ran while one was open for 0% of the time, Pallas kernels for 2%

profile of v2, /device:TPU:1, one launch (start us, length us, event | category | flops | bytes accessed | tf_op | source)
XLA Modules:
  0.0 118.7 jit_solution(6833830407698219462)
XLA Ops:
  2.1 0.9 copy-done.1
  3.0 0.9 copy-done.3
  4.0 1.4 %shard_map.102 = (bf16[1024,128]{1,0:T(8,128)(2,1)S(1)}, bf16[1024,128]{1,0:T(8,128)(2,1)S(1)}, bf16[3,128,128]{2,1,0:T(8,128)(2,1)S(1)}, bf16[2,128,128]{2,1,0:T(8,128)(2,1)S(1)}, f32[32,1,128]{2,1,0:T(1,128)S(1)}) custom-call(s32[9]{0:T(128)S(1)} %pad_add_fusion.info_ref, f32[1,128]{1,0:T(1,128)S(1)} %bitcast.27, f32[1,128]{1,0:T(1,128)S(1)} %bitcast.30, ...), custom_call_target="tpu_custom_call" | custom-call | tf_op jit(solution)/shard_map/pallas_call | solution.py:341
  5.4 6.6 %collective-permute-start = (bf16[3,128,128]{2,1,0:T(8,128)(2,1)S(1)}, bf16[3,128,128]{2,1,0:T(8,128)(2,1)S(1)}, u32[]{:S(2)}, u32[]{:S(2)}) collective-permute-start(bf16[3,128,128]{2,1,0:T(8,128)(2,1)S(1)} %get-tuple-element.26), channel_id=1, source_target_pairs={{0,2},{1,3},{2,0},{3,1},{4,6},{5,7},{6,4},{7,5},{8,10},{9,11},{10,... | collective-permute-start | bytes 294920 | tf_op jit(solution)/shard_map/ppermute | solution.py:355
  12.0 18.1 %all_to_all.30.in_stat_ref = f32[32,1,128]{2,1,0:T(1,128)S(1)} all-to-all(f32[32,1,128]{2,1,0:T(1,128)S(1)} %get-tuple-element.27), channel_id=1, replica_groups=mesh['y'=8,'x'=4,'zh'=2,'co'=2,'zl'=4] {'y','x'}, dimensions={0} | all-to-all | bytes 32768 | tf_op jit(solution)/shard_map/all_to_all | solution.py:356
  30.8 4.1 %collective-permute-start.1 = (bf16[3,128,128]{2,1,0:T(8,128)(2,1)S(1)}, bf16[3,128,128]{2,1,0:T(8,128)(2,1)S(1)}, u32[]{:S(2)}, u32[]{:S(2)}) collective-permute-start(bf16[3,128,128]{2,1,0:T(8,128)(2,1)S(1)} %get-tuple-element.29), channel_id=1, source_target_pairs={{0,1},{1,0},{2,3},{3,2},{4,5},{5,4},{6,7},{7,6},{8,9},{9,8},{10,11... | collective-permute-start | bytes 294920 | tf_op jit(solution)/shard_map/ppermute | solution.py:364
  34.9 2.0 %collective-permute-done.1.in_ref = bf16[3,128,128]{2,1,0:T(8,128)(2,1)S(1)} collective-permute-done((bf16[3,128,128]{2,1,0:T(8,128)(2,1)S(1)}, bf16[3,128,128]{2,1,0:T(8,128)(2,1)S(1)}, u32[]{:S(2)}, u32[]{:S(2)}) %collective-permute-start.1) | collective-permute-done | bytes 98336 | tf_op jit(solution)/shard_map/ppermute | solution.py:364
  36.9 0.8 shard_map.104
  37.8 2.6 %collective-permute-start.2 = (bf16[128,128]{1,0:T(8,128)(2,1)S(1)}, bf16[128,128]{1,0:T(8,128)(2,1)S(1)}, u32[]{:S(2)}, u32[]{:S(2)}) collective-permute-start(bf16[128,128]{1,0:T(8,128)(2,1)S(1)} %get-tuple-element.34), channel_id=1, source_target_pairs={{0,498},{1,7},{2,16},{3,509},{4,502},{5,11},{6,20},{7,1},{8,506},{... | collective-permute-start | bytes 98312 | tf_op jit(solution)/shard_map/ppermute | solution.py:377
  40.3 18.7 %all_to_all.31.in_stat_ref = f32[16,1,128]{2,1,0:T(1,128)S(1)} all-to-all(f32[16,1,128]{2,1,0:T(1,128)S(1)} %get-tuple-element.32), channel_id=1, replica_groups=mesh['y'=8,'x'=4,'zh'=2,'co'=2,'zl'=4] {'zh','co','zl'}, dimensions={0} | all-to-all | bytes 16384 | tf_op jit(solution)/shard_map/all_to_all | solution.py:382
  59.0 2.4 %shard_map.105 = (f32[1280,128]{1,0:T(8,128)S(1)}, f32[1024,128]{1,0:T(8,128)S(1)}, f32[2,128]{1,0:T(2,128)S(1)}) custom-call(s32[9]{0:T(128)S(1)} %pad_add_fusion.info_ref, bf16[1024,128]{1,0:T(8,128)(2,1)S(1)} %get-tuple-element.23.xt_ref, bf16[1024,128]{1,0:T(8,128)(2,1)S(1)} %get-tuple-element.24.ct_ref, bf16[1,128,1024]{2,1,0:T(8,128)(2,1)S(1)} %copy-done.2, ...), custom_call_target="tpu_custom_call" | custom-call | tf_op jit(solution)/shard_map/pallas_call | solution.py:383
  61.4 4.6 %all_to_all.32 = f32[2,160,4,128]{3,2,1,0:T(4,128)S(1)} all-to-all(f32[2,160,4,128]{3,2,1,0:T(4,128)S(1)} %bitcast.24), channel_id=1, replica_groups=mesh['y'=8,'x'=4,'zh'=2,'co'=2,'zl'=4] {'co'}, dimensions={0} | all-to-all | bytes 1310720 | tf_op jit(solution)/shard_map/all_to_all | solution.py:329
  66.7 5.6 %all-to-all-start.3 = ((f32[32,5,4,128]{3,2,1,0:T(4,128)}), f32[32,5,4,128]{3,2,1,0:T(4,128)S(1)}, u32[]{:S(2)}, u32[]{:S(2)}) async-start(f32[32,5,4,128]{3,2,1,0:T(4,128)} %bitcast.8), calls=%async_computation.3 | async-start | bytes 655360 | tf_op jit(solution)/shard_map/all_to_all | solution.py:329
  72.3 2.2 %collective-permute-start.3 = (bf16[128,128]{1,0:T(8,128)(2,1)S(1)}, bf16[128,128]{1,0:T(8,128)(2,1)S(1)}, u32[]{:S(2)}, u32[]{:S(2)}) collective-permute-start(bf16[128,128]{1,0:T(8,128)(2,1)S(1)} %collective-permute-done.2.in_ref.own_ref), channel_id=1, source_target_pairs={{0,1},{1,0},{2,3},{3,2},{4,5},{5,4},{6,7},{7,6},{8,9},{9,8},{10,11... | collective-permute-start | bytes 98312 | tf_op jit(solution)/shard_map/ppermute | solution.py:395
  74.5 2.7 %collective-permute-done.3.other_ref = bf16[128,128]{1,0:T(8,128)(2,1)S(1)} collective-permute-done((bf16[128,128]{1,0:T(8,128)(2,1)S(1)}, bf16[128,128]{1,0:T(8,128)(2,1)S(1)}, u32[]{:S(2)}, u32[]{:S(2)}) %collective-permute-start.3) | collective-permute-done | bytes 32800 | tf_op jit(solution)/shard_map/ppermute | solution.py:395
  77.3 7.8 %all-to-all-done.3 = f32[32,5,4,128]{3,2,1,0:T(4,128)S(1)} async-done(((f32[32,5,4,128]{3,2,1,0:T(4,128)}), f32[32,5,4,128]{3,2,1,0:T(4,128)S(1)}, u32[]{:S(2)}, u32[]{:S(2)}) %all-to-all-start.3) | async-done | bytes 327712 | tf_op jit(solution)/shard_map/all_to_all | solution.py:329
  85.1 9.8 %all_to_all.33 = f32[8,5,4,128]{3,2,1,0:T(4,128)S(1)} all-to-all(f32[8,5,4,128]{3,2,1,0:T(4,128)S(1)} %bitcast.26), channel_id=1, replica_groups=mesh['y'=8,'x'=4,'zh'=2,'co'=2,'zl'=4] {'zh','zl'}, dimensions={0} | all-to-all | bytes 163840 | tf_op jit(solution)/shard_map/all_to_all | solution.py:329
  95.6 4.8 %all-to-all-start.5 = ((f32[32,5,4,128]{3,2,1,0:T(4,128)}), f32[32,5,4,128]{3,2,1,0:T(4,128)S(1)}, u32[]{:S(2)}, u32[]{:S(2)}) async-start(f32[32,5,4,128]{3,2,1,0:T(4,128)} %bitcast.12), calls=%async_computation.5 | async-start | bytes 655360 | tf_op jit(solution)/shard_map/all_to_all | solution.py:329
  100.4 2.0 %collective-permute-start.4 = (bf16[2,64,128]{2,1,0:T(8,128)(2,1)S(1)}, bf16[2,64,128]{2,1,0:T(8,128)(2,1)S(1)}, u32[]{:S(2)}, u32[]{:S(2)}) collective-permute-start(bf16[2,64,128]{2,1,0:T(8,128)(2,1)S(1)} %get-tuple-element.39.pair_ref), channel_id=1, source_target_pairs={{0,2},{1,3},{2,0},{3,1},{4,6},{5,7},{6,4},{7,5},{8,10},{9,11},{10,... | collective-permute-start | bytes 98312 | tf_op jit(solution)/shard_map/ppermute | solution.py:404
  102.4 3.9 %collective-permute-done.4.others_ref = bf16[2,64,128]{2,1,0:T(8,128)(2,1)S(1)} collective-permute-done((bf16[2,64,128]{2,1,0:T(8,128)(2,1)S(1)}, bf16[2,64,128]{2,1,0:T(8,128)(2,1)S(1)}, u32[]{:S(2)}, u32[]{:S(2)}) %collective-permute-start.4) | collective-permute-done | bytes 32800 | tf_op jit(solution)/shard_map/ppermute | solution.py:404
  106.3 2.3 %shard_map.109 = (bf16[1,128,1024]{2,1,0:T(8,128)(2,1)}, f32[2,128]{1,0:T(2,128)S(1)}) custom-call(s32[9]{0:T(128)S(1)} %pad_add_fusion.info_ref, f32[1024,128]{1,0:T(8,128)S(1)} %get-tuple-element.35.pre_ref, bf16[1024,128]{1,0:T(8,128)(2,1)S(1)} %get-tuple-element.23.xt_ref, f32[2,128]{1,0:T(2,128)S(1)} %get-tuple-element.36.norm_ref, ...), custom_call_target="tpu_custom_call" | custom-call | tf_op jit(solution)/shard_map/pallas_call | solution.py:408
  109.1 2.1 %all-to-all-done.5 = f32[32,5,4,128]{3,2,1,0:T(4,128)S(1)} async-done(((f32[32,5,4,128]{3,2,1,0:T(4,128)}), f32[32,5,4,128]{3,2,1,0:T(4,128)S(1)}, u32[]{:S(2)}, u32[]{:S(2)}) %all-to-all-start.5) | async-done | bytes 327712 | tf_op jit(solution)/shard_map/all_to_all | solution.py:329
  111.3 6.5 %all_gather.3 = f32[64,5,4,128]{3,2,1,0:T(4,128)S(1)} all-gather(f32[32,5,4,128]{3,2,1,0:T(4,128)S(1)} %all-to-all-done.5), channel_id=1, replica_groups=mesh['y'=8,'x'=4,'zh'=2,'co'=2,'zl'=4] {'co'}, dimensions={0}, use_global_device_ids=true | all-gather | bytes 983040 | tf_op jit(solution)/shard_map/all_gather | solution.py:407
  117.8 0.9 shard_map.110
  (22 shorter events, 4.2 us)
Async XLA Ops:
  0.6 0.7 copy-start.6
  0.6 0.7 copy-start.7
  1.4 0.7 copy-start.4
  1.4 0.7 copy-start.5
  2.1 0.9 copy-start.1
  3.0 0.9 copy-start.3
  5.4 24.7 %collective-permute-start = (bf16[3,128,128]{2,1,0:T(8,128)(2,1)S(1)}, bf16[3,128,128]{2,1,0:T(8,128)(2,1)S(1)}, u32[]{:S(2)}, u32[]{:S(2)}) collective-permute-start(bf16[3,128,128]{2,1,0:T(8,128)(2,1)S(1)} %get-tuple-element.26), channel_id=1, source_target_pairs={{0,2},{1,3},{2,0},{3,1},{4,6},{5,7},{6,4},{7,5},{8,10},{9,11},{10,... | collective-permute-start | bytes 294920 | tf_op jit(solution)/shard_map/ppermute | solution.py:355
  30.1 6.8 %copy-start = (bf16[128,9,128]{2,0,1:T(8,128)(2,1)S(1)}, bf16[128,9,128]{2,0,1:T(8,128)(2,1)}, u32[]{:S(2)}) copy-start(bf16[128,9,128]{2,0,1:T(8,128)(2,1)} %param.9) | copy-start | bytes 884740
  30.8 28.3 %copy-start.2 = (bf16[1,128,1024]{2,1,0:T(8,128)(2,1)S(1)}, bf16[1,128,1024]{2,1,0:T(8,128)(2,1)}, u32[]{:S(2)}) copy-start(bf16[1,128,1024]{2,1,0:T(8,128)(2,1)} %cot_ref.1) | copy-start | bytes 786436
  30.8 6.1 %collective-permute-start.1 = (bf16[3,128,128]{2,1,0:T(8,128)(2,1)S(1)}, bf16[3,128,128]{2,1,0:T(8,128)(2,1)S(1)}, u32[]{:S(2)}, u32[]{:S(2)}) collective-permute-start(bf16[3,128,128]{2,1,0:T(8,128)(2,1)S(1)} %get-tuple-element.29), channel_id=1, source_target_pairs={{0,1},{1,0},{2,3},{3,2},{4,5},{5,4},{6,7},{7,6},{8,9},{9,8},{10,11... | collective-permute-start | bytes 294920 | tf_op jit(solution)/shard_map/ppermute | solution.py:364
  37.8 21.3 %collective-permute-start.2 = (bf16[128,128]{1,0:T(8,128)(2,1)S(1)}, bf16[128,128]{1,0:T(8,128)(2,1)S(1)}, u32[]{:S(2)}, u32[]{:S(2)}) collective-permute-start(bf16[128,128]{1,0:T(8,128)(2,1)S(1)} %get-tuple-element.34), channel_id=1, source_target_pairs={{0,498},{1,7},{2,16},{3,509},{4,502},{5,11},{6,20},{7,1},{8,506},{... | collective-permute-start | bytes 98312 | tf_op jit(solution)/shard_map/ppermute | solution.py:377
  66.7 18.3 %all-to-all-start.3 = ((f32[32,5,4,128]{3,2,1,0:T(4,128)}), f32[32,5,4,128]{3,2,1,0:T(4,128)S(1)}, u32[]{:S(2)}, u32[]{:S(2)}) async-start(f32[32,5,4,128]{3,2,1,0:T(4,128)} %bitcast.8), calls=%async_computation.3 | async-start | bytes 655360 | tf_op jit(solution)/shard_map/all_to_all | solution.py:329
  72.3 5.0 %collective-permute-start.3 = (bf16[128,128]{1,0:T(8,128)(2,1)S(1)}, bf16[128,128]{1,0:T(8,128)(2,1)S(1)}, u32[]{:S(2)}, u32[]{:S(2)}) collective-permute-start(bf16[128,128]{1,0:T(8,128)(2,1)S(1)} %collective-permute-done.2.in_ref.own_ref), channel_id=1, source_target_pairs={{0,1},{1,0},{2,3},{3,2},{4,5},{5,4},{6,7},{7,6},{8,9},{9,8},{10,11... | collective-permute-start | bytes 98312 | tf_op jit(solution)/shard_map/ppermute | solution.py:395
  95.6 15.6 %all-to-all-start.5 = ((f32[32,5,4,128]{3,2,1,0:T(4,128)}), f32[32,5,4,128]{3,2,1,0:T(4,128)S(1)}, u32[]{:S(2)}, u32[]{:S(2)}) async-start(f32[32,5,4,128]{3,2,1,0:T(4,128)} %bitcast.12), calls=%async_computation.5 | async-start | bytes 655360 | tf_op jit(solution)/shard_map/all_to_all | solution.py:329
  100.4 5.9 %collective-permute-start.4 = (bf16[2,64,128]{2,1,0:T(8,128)(2,1)S(1)}, bf16[2,64,128]{2,1,0:T(8,128)(2,1)S(1)}, u32[]{:S(2)}, u32[]{:S(2)}) collective-permute-start(bf16[2,64,128]{2,1,0:T(8,128)(2,1)S(1)} %get-tuple-element.39.pair_ref), channel_id=1, source_target_pairs={{0,2},{1,3},{2,0},{3,1},{4,6},{5,7},{6,4},{7,5},{8,10},{9,11},{10,... | collective-permute-start | bytes 98312 | tf_op jit(solution)/shard_map/ppermute | solution.py:404

commit v3 on v2

--- a/solution.py
+++ b/solution.py
@@ -18,11 +18,13 @@
 CELLS = ROWS * S
 C = 128
 LINE = 2 * S
+EDGE = 2 * S + 2 * ROWS
 CHUNK = 20
 
 TILE = ("y", "x", "zh", "co")
-AXES = {"y": 8, "x": 4, "zh": 2, "co": 2, "zl": 4}
-NEAR = ("zh", "co", "zl")
+AXES = {"y": 8, "x": 4, "zh": 2, "co": 2, "z2": 2, "z1": 2}
+SUB = ("z2", "z1")
+NEAR = ("zh", "co", "z2", "z1")
 FAR = ("y", "x")
 N_NEAR = 16
 N_FAR = 32
@@ -69,50 +71,54 @@
     return mean, spread
 
 
-def start_kernel(
-    info_ref, gain_ref, shift_ref, x_ref, c_ref,
-    xt_ref, ct_ref, send_ref, keep_ref, stat_ref, x_scr, c_scr, side_scr,
-):
-    place = info_ref[0]
-    half = place // 2
+def start_kernel(x_ref, c_ref, xt_ref, ct_ref, edge_ref, stat_ref, x_scr, c_scr):
     x = x_ref[0].astype(F32).T
     x_scr[...] = x
     xt_ref[...] = x.astype(BF16)
+    c = c_ref[0].astype(F32).T
+    c_scr[...] = c
+    ct_ref[...] = c.astype(BF16)
+    for kind, (scr, flat) in enumerate(((x_scr, xt_ref), (c_scr, ct_ref))):
+        edge_ref[kind, 0:S] = flat[0:S]
+        edge_ref[kind, S : 2 * S] = flat[CELLS - S : CELLS]
+        for k, column in enumerate((S - 1, 0)):
+            edge_ref[kind, 2 * S + k * ROWS : 2 * S + (k + 1) * ROWS] = scr[
+                pl.ds(column, ROWS, stride=S), :
+            ].astype(BF16)
     mean = group_sum(jnp.sum(x, axis=0, keepdims=True)) * (1.0 / LOCAL)
     gap = x - mean
     spread = group_sum(jnp.sum(gap * gap, axis=0, keepdims=True))
     stat_ref[...] = jnp.broadcast_to(packed(mean, spread)[None], (N_FAR, 1, C))
-    c = c_ref[0].astype(F32).T
-    c_scr[...] = c
-    ct_ref[...] = c.astype(BF16)
+
+
+def middle_kernel(
+    info_ref, own_ref, other_ref, gain_ref, shift_ref,
+    send_ref, left_ref, affine_ref, side_scr,
+):
+    place = info_ref[0]
+    odd = place % 2
+    pair = (place + 2) % 4
+    affine_ref[0:1], affine_ref[1:2] = gain_ref[...], shift_ref[...]
     zero = jnp.zeros((S, C), BF16)
-    own = pl.ds(pl.multiple_of(place * ROWS, ROWS), ROWS)
-    for kind, (scr, flat) in enumerate(((x_scr, xt_ref), (c_scr, ct_ref))):
-        first, last = flat[0:S], flat[CELLS - S : CELLS]
-        side_scr[kind, 0] = jnp.where(place == 0, first, zero)
-        side_scr[kind, 2] = jnp.where(place == 3, last, zero)
-        for side, column in ((1, S - 1), (3, 0)):
+    first, last = slice(0, S), slice(S, 2 * S)
+    for kind in range(2):
+        side_scr[kind, 0] = jnp.where(
+            place == 0, own_ref[kind, first], jnp.where(pair == 0, other_ref[kind, first], zero)
+        )
+        side_scr[kind, 2] = jnp.where(
+            place == 3, own_ref[kind, last], jnp.where(pair == 3, other_ref[kind, last], zero)
+        )
+        for k, side in enumerate((1, 3)):
+            at = slice(2 * S + k * ROWS, 2 * S + (k + 1) * ROWS)
             side_scr[kind, side] = zero
-            side_scr[kind, side, own, :] = scr[pl.ds(column, ROWS, stride=S), :].astype(BF16)
-        send_ref[2, kind * S : (kind + 1) * S] = jnp.where(place == 1, last, first)
-        for k in range(2):
-            at = slice(kind * S, (kind + 1) * S)
-            send_ref[k, at] = side_scr[kind, side_facing(info_ref, 2 - 2 * half + k)]
-            keep_ref[k, at] = side_scr[kind, side_facing(info_ref, 2 * half + k)]
-
-
-def middle_kernel(
-    info_ref, keep_ref, in_ref, xt_ref, ct_ref, in_stat_ref, send_ref, left_ref, stat_ref
-):
-    odd = info_ref[0] % 2
-    send_ref[0] = keep_ref[1 - odd] + in_ref[1 - odd]
-    left_ref[...] = keep_ref[odd] + in_ref[odd]
-    send_ref[2] = in_ref[2]
-    stat_ref[...] = packed(*merge([in_stat_ref[k] for k in range(N_FAR)], LOCAL))[None]
-    for kind, flat in enumerate((xt_ref, ct_ref)):
-        send_ref[1, kind * S : (kind + 1) * S] = jnp.where(
-            odd == 1, flat[0:S], flat[CELLS - S : CELLS]
-        )
+            for who, ref in ((place, own_ref), (pair, other_ref)):
+                rows = pl.ds(pl.multiple_of(who * ROWS, ROWS), ROWS)
+                side_scr[kind, side, rows, :] = ref[kind, at]
+        here = slice(kind * S, (kind + 1) * S)
+        send_ref[0, here] = side_scr[kind, side_facing(info_ref, place + 1 - 2 * odd)]
+        left_ref[here] = side_scr[kind, side_facing(info_ref, place)]
+        send_ref[1, here] = jnp.where(odd == 1, own_ref[kind, first], own_ref[kind, last])
+        send_ref[2, here] = jnp.where(place == 0, other_ref[kind, first], other_ref[kind, last])
 
 
 def side_facing(info_ref, direction):
@@ -149,7 +155,8 @@
     place = info_ref[0]
     odd = place % 2 == 1
     side = side_facing(info_ref, place)
-    strips = keep_ref[...] + in_ref[0]
+    other = 1 - place % 2
+    strips = keep_ref[...] + in_ref[other, 0]
     strips_ref[...] = strips
     grads = strips[S : 2 * S]
     taps, at_start, at_end = side_parts(info_ref, side)
@@ -163,24 +170,25 @@
     grad = grad + jnp.where(last & at_end, parts[2], 0.0)
     message_ref[0:S] = strips[0:S]
     message_ref[S : 2 * S] = turned(grad.astype(BF16), info_ref[1 + side] // 4)
-    direct, passed = in_ref[1], in_ref[2]
+    direct, passed = in_ref[other, 1], in_ref[other, 2]
     above, below = jnp.where(odd, direct, passed), jnp.where(odd, passed, direct)
     zero = jnp.zeros((S, C), BF16)
     rows_ref[0:S] = above[0:S]
     rows_ref[S : 2 * S] = below[0:S]
     rows_ref[2 * S : 3 * S] = jnp.where(place == 0, zero, above[S : 2 * S])
     rows_ref[3 * S : 4 * S] = jnp.where(place == 3, zero, below[S : 2 * S])
-    stat_ref[...] = jnp.broadcast_to(in_stat_ref[...], (N_NEAR, 1, C))
+    stats = packed(*merge([in_stat_ref[k] for k in range(N_FAR)], LOCAL))
+    stat_ref[...] = jnp.broadcast_to(stats[None], (N_NEAR, 1, C))
 
 
 def main_kernel(
-    info_ref, xt_ref, ct_ref, cot_ref, rows_ref, in_stat_ref, w_ref, gain_ref, shift_ref,
-    strips_ref, in_ref, part_ref, pre_ref, norm_ref, weight_scr,
+    info_ref, xt_ref, ct_ref, cot_ref, rows_ref, in_stat_ref, w_ref, affine_ref,
+    strips_ref, in_ref, keep_ref, send_ref, pre_ref, norm_ref, weight_scr,
 ):
     place = info_ref[0]
     mean, spread = merge([in_stat_ref[k] for k in range(N_NEAR)], LOCAL * N_FAR)
     rstd = lax.rsqrt(spread * (1.0 / ENTRIES) + EPSILON)
-    gain, shift = gain_ref[...], shift_ref[...]
+    gain, shift = affine_ref[0:1], affine_ref[1:2]
     norm_ref[...] = jnp.concatenate([mean, rstd], axis=0)
 
     def affine(raw):
@@ -231,11 +239,20 @@
             (((0,), (0,)), ((), ())),
             preferred_element_type=F32,
         )
+    core = info_ref[9]
+
+    def put(row, low, high):
+        at = pl.ds(row, N_FAR, stride=CHUNK)
+        keep_ref[at, :] = jnp.where(core == 0, low, high)
+        send_ref[at, :] = jnp.where(core == 0, high, low)
+
     for tap in range(9):
         for h in range(2):
-            part_ref[pl.ds(h * 9 + tap, 64, stride=CHUNK), :] = weight_scr[
-                tap, h * 64 : (h + 1) * 64
-            ]
+            put(
+                h * 9 + tap,
+                weight_scr[tap, h * 64 : h * 64 + 32],
+                weight_scr[tap, h * 64 + 32 : (h + 1) * 64],
+            )
 
     grads = jnp.concatenate(
         [rows_ref[2 * S : 3 * S], ct_ref[...], rows_ref[3 * S : 4 * S]], axis=0
@@ -256,13 +273,14 @@
     more = in_ref[S : 2 * S].astype(F32) * (sig * (1.0 + pre * (1.0 - sig)))
     gain_row = gain_row + jnp.sum(more * normed, axis=0, keepdims=True)
     shift_row = shift_row + jnp.sum(more, axis=0, keepdims=True)
-    part_ref[pl.ds(18, 64, stride=CHUNK), :] = jnp.broadcast_to(gain_row, (64, C))
-    part_ref[pl.ds(19, 64, stride=CHUNK), :] = jnp.broadcast_to(shift_row, (64, C))
+    for k, row in ((18, gain_row), (19, shift_row)):
+        row = jnp.broadcast_to(row, (N_FAR, C))
+        put(k, row, row)
 
 
 def end_kernel(
-    info_ref, pre_ref, xt_ref, norm_ref, gain_ref, shift_ref, total_ref, pair_ref, others_ref,
-    out_ref, sums_ref, side_scr, more_scr,
+    info_ref, pre_ref, xt_ref, norm_ref, affine_ref, total_ref, pair_ref, others_ref,
+    out_ref, gain_sum_ref, shift_sum_ref, side_scr, more_scr,
 ):
     place = info_ref[0]
     base, odd = place // 2 * 2, place % 2
@@ -277,17 +295,18 @@
     for e, at in ((4, 0), (2, S - 1)):
         more_scr[pl.ds(at, ROWS, stride=S), :] += side_scr[info_ref[e] % 4, own, :].astype(F32)
     mean, rstd = norm_ref[0:1], norm_ref[1:2]
-    gain = gain_ref[...]
+    gain, shift = affine_ref[0:1], affine_ref[1:2]
     gain_total, shift_total = total_ref[18:19], total_ref[19:20]
     first = group_sum(gain * shift_total) * (1.0 / ENTRIES)
     second = group_sum(gain * gain_total) * (1.0 / ENTRIES)
     normed = (xt_ref[...].astype(F32) - mean) * rstd
-    pre = normed * gain + shift_ref[...]
+    pre = normed * gain + shift
     sig = 1.0 / (1.0 + jnp.exp(-pre))
     pre_grad = pre_ref[...] + more_scr[...] * (sig * (1.0 + pre * (1.0 - sig)))
     out = rstd * (pre_grad * gain - first - normed * second)
     out_ref[0] = out.T.astype(BF16)
-    sums_ref[...] = jnp.concatenate([gain_total, shift_total], axis=0) * SCALE
+    gain_sum_ref[...] = gain_total * SCALE
+    shift_sum_ref[...] = shift_total * SCALE
 
 
 def weight_kernel(whole_ref, out_ref):
@@ -307,6 +326,10 @@
         out_ref[k * rows : (k + 1) * rows] = total
 
 
+def add_kernel(a_ref, b_ref, out_ref):
+    out_ref[...] = a_ref[...] + b_ref[...]
+
+
 def summed(x, parts, copies):
     rows = x.size // C
     return pl.pallas_call(
@@ -334,34 +357,39 @@
 
 
 def body(features, cotangent, conv_weight, norm_gain, norm_shift, seam_code, corner_map):
-    place = lax.axis_index("zl").astype(jnp.int32).reshape(1)
-    info = jnp.concatenate([place, seam_code[0], corner_map[0]])
+    place = lax.axis_index(SUB).astype(jnp.int32).reshape(1)
+    core = lax.axis_index("co").astype(jnp.int32).reshape(1)
+    info = jnp.concatenate([place, seam_code[0], corner_map[0], core])
     weight = conv_weight.transpose(1, 0, 2)
     gain, shift = norm_gain.reshape(1, C), norm_shift.reshape(1, C)
-    xt, ct, send, keep, stats = pl.pallas_call(
+    xt, ct, edges, stats = pl.pallas_call(
         start_kernel,
         out_shape=(
             shape((CELLS, C), BF16),
             shape((CELLS, C), BF16),
-            shape((3, LINE, C), BF16),
-            shape((2, LINE, C), BF16),
+            shape((2, EDGE, C), BF16),
             shape((N_FAR, 1, C), F32),
         ),
+        in_specs=[VMEM] * 2,
+        out_specs=(VMEM,) * 4,
+        scratch_shapes=[pltpu.VMEM((CELLS, C), F32)] * 2,
+        compiler_params=PARAMS,
+    )(features, cotangent)
+    came = lax.ppermute(edges, "z2", [(0, 1), (1, 0)])
+    stats = lax.all_to_all(stats, FAR, 0, 0, tiled=True)
+    send, keep, affine = pl.pallas_call(
+        middle_kernel,
+        out_shape=(
+            shape((3, LINE, C), BF16),
+            shape((LINE, C), BF16),
+            shape((2, C), F32),
+        ),
         in_specs=[SMEM] + [VMEM] * 4,
-        out_specs=(VMEM,) * 5,
-        scratch_shapes=[pltpu.VMEM((CELLS, C), F32)] * 2 + [pltpu.VMEM((2, 4, S, C), BF16)],
-        compiler_params=PARAMS,
-    )(info, gain, shift, features, cotangent)
-    came = lax.ppermute(send, "zl", [(i, i ^ 2) for i in range(4)])
-    stats = lax.all_to_all(stats, FAR, 0, 0, tiled=True)
-    send, keep, stats = pl.pallas_call(
-        middle_kernel,
-        out_shape=(shape((3, LINE, C), BF16), shape((LINE, C), BF16), shape((1, 1, C), F32)),
-        in_specs=[SMEM] + [VMEM] * 5,
         out_specs=(VMEM,) * 3,
-        compiler_params=PARAMS,
-    )(info, keep, came, xt, ct, stats)
-    came = lax.ppermute(send, "zl", [(i, i ^ 1) for i in range(4)])
+        scratch_shapes=[pltpu.VMEM((2, 4, S, C), BF16)],
+        compiler_params=PARAMS,
+    )(info, edges, came, gain, shift)
+    came = lax.all_gather(send, "z1", axis=0, tiled=False)
     message, strips, rows, stats = pl.pallas_call(
         seam_kernel,
         out_shape=(
@@ -380,20 +408,28 @@
         [(4 * t + s, 4 * ((t + STEPS[s]) % 128) + (s + 2) % 4) for t in range(128) for s in range(4)],
     )
     stats = lax.all_to_all(stats, NEAR, 0, 0, tiled=True)
-    parts, pre_grad, norm = pl.pallas_call(
+    parts, send, pre_grad, norm = pl.pallas_call(
         main_kernel,
         out_shape=(
-            shape((64 * CHUNK, C), F32),
+            shape((N_FAR * CHUNK, C), F32),
+            shape((N_FAR * CHUNK, C), F32),
             shape((CELLS, C), F32),
             shape((2, C), F32),
         ),
-        in_specs=[SMEM] + [VMEM] * 10,
-        out_specs=(VMEM,) * 3,
+        in_specs=[SMEM] + [VMEM] * 9,
+        out_specs=(VMEM,) * 4,
         scratch_shapes=[pltpu.VMEM((9, C, C), F32)],
         compiler_params=PARAMS,
-    )(info, xt, ct, cotangent, rows, stats, weight, gain, shift, strips, message)
-    other = lax.ppermute(message, "zl", [(i, i ^ 1) for i in range(4)])
-    parts = summed(exchanged(parts, "co", 2), 2, 1)
+    )(info, xt, ct, cotangent, rows, stats, weight, affine, strips, message)
+    other = lax.ppermute(message, "z1", [(0, 1), (1, 0)])
+    send = lax.ppermute(send, "co", [(0, 1), (1, 0)])
+    parts = pl.pallas_call(
+        add_kernel,
+        out_shape=shape((N_FAR * CHUNK, C), F32),
+        in_specs=[VMEM] * 2,
+        out_specs=VMEM,
+        compiler_params=PARAMS,
+    )(parts, send)
     parts, pair = pl.pallas_call(
         functools.partial(sum_and_pair_kernel, N_FAR, 8),
         out_shape=(shape((8 * CHUNK, C), F32), shape((2, S, C), BF16)),
@@ -401,18 +437,18 @@
         out_specs=(VMEM,) * 2,
         compiler_params=PARAMS,
     )(exchanged(parts, FAR, N_FAR).reshape(N_FAR * CHUNK, C), message, other)
-    others = lax.ppermute(pair, "zl", [(i, i ^ 2) for i in range(4)])
-    parts = summed(exchanged(parts, ("zh", "zl"), 8), 8, N_FAR)
+    others = lax.ppermute(pair, "z2", [(0, 1), (1, 0)])
+    parts = summed(exchanged(parts, ("zh", "z2", "z1"), 8), 8, N_FAR)
     half = exchanged(parts, FAR, N_FAR)
     whole = lax.all_gather(half, "co", axis=0, tiled=True)
-    grad_input, sums = pl.pallas_call(
+    grad_input, grad_gain, grad_shift = pl.pallas_call(
         end_kernel,
-        out_shape=(shape((1, C, CELLS), BF16), shape((2, C), F32)),
-        in_specs=[SMEM] + [VMEM] * 8,
-        out_specs=(VMEM,) * 2,
+        out_shape=(shape((1, C, CELLS), BF16), shape((1, C), F32), shape((1, C), F32)),
+        in_specs=[SMEM] + [VMEM] * 7,
+        out_specs=(VMEM,) * 3,
         scratch_shapes=[pltpu.VMEM((4, S, C), BF16), pltpu.VMEM((CELLS, C), F32)],
         compiler_params=PARAMS,
-    )(info, pre_grad, xt, norm, gain, shift, parts, pair, others)
+    )(info, pre_grad, xt, norm, affine, parts, pair, others)
     grad_weight = pl.pallas_call(
         weight_kernel,
         out_shape=shape((9, C, C), F32),
@@ -420,7 +456,7 @@
         out_specs=VMEM,
         compiler_params=PARAMS,
     )(whole.reshape(64 * CHUNK, C)).transpose(1, 0, 2)
-    return grad_input, grad_weight, sums[0], sums[1]
+    return grad_input, grad_weight, grad_gain.reshape(C), grad_shift.reshape(C)
 
 
 def solution(mesh):
@@ -429,14 +465,14 @@
         body,
         mesh=fine,
         in_specs=(
-            P(TILE, None, "zl"),
-            P(TILE, None, "zl"),
+            P(TILE, None, SUB),
+            P(TILE, None, SUB),
             P(),
             P(),
             P(),
             P(TILE, None),
             P(TILE, None),
         ),
-        out_specs=(P(TILE, None, "zl"), P(), P(), P()),
+        out_specs=(P(TILE, None, SUB), P(), P(), P()),
         check_vma=False,
     )

time: 119 us -> 110 us (0.924)
  blocking collectives: 57.6 us -> 38.9 us
  starting transfers between devices: 27.9 us -> 37.1 us
  waiting for transfers between devices: 18.5 us -> 21 us
  local copies, waits for them, and re-layouts: 3.75 us -> 1.92 us
    all_to_all x1 -> x0, blocking collectives: 18.1 us -> none  [body(): stats = lax.all_to_all(stats, FAR, 0, 0, tiled=True)]
    all_to_all x0 -> x1, starting transfers between devices: none -> 9.68 us  [body(): stats = lax.all_to_all(stats, FAR, 0, 0, tiled=True)]
    all_gather x0 -> x1, blocking collectives: none -> 5.05 us  [body(): came = lax.all_gather(send, 'z1', axis=0, tiled=False)]
    all_to_all x2 -> x1, blocking collectives: 14.3 us -> 9.78 us  [exchanged(): return lax.all_to_all(x, axes, 0, 0, tiled=True)]
    all_to_all x0 -> x1, waiting for transfers between devices: none -> 2.74 us  [body(): stats = lax.all_to_all(stats, FAR, 0, 0, tiled=True)]
    ppermute x4, starting transfers between devices: 15 us -> 13.6 us  [the longest x1 6.76 us: body(): came = lax.ppermute(edges, 'z2', [(0, 1), (1, 0)])]
    unnamed x16, local copies, waits for them, and re-layouts: 3.24 us -> 1.92 us
    pallas_call x1 -> x2, Pallas kernels: 2.37 us -> 3.1 us  [the longest x1 2.34 us: body(): pl.pallas_call(main_kernel, out_shape=(shape((N_FAR * CHUNK, C), F32), sh...]
  transfers between devices with their start and end apart: 7 -> 8, of which waited for: 5 -> 6; matrix products, arithmetic and copies ran while one was open for 0% -> 0% of each run, Pallas kernels for 2% -> 3%
where the time goes in v3:
time: 110 us
  blocking collectives  38.9 us (35%)
  starting transfers between devices  37.1 us (34%)
  waiting for transfers between devices  21 us (19%)
  Pallas kernels  9.94 us (9%)
  local copies, waits for them, and re-layouts  1.92 us (2%)
    all_to_all x1, blocking collectives, body(): stats = lax.all_to_all(stats, NEAR, 0, 0, tiled=True)  17.6 us
    all_to_all x2, waiting for transfers between devices, exchanged(): return lax.all_to_all(x, axes, 0, 0, tiled=True)  10.5 us
    all_to_all x2, starting transfers between devices, exchanged(): return lax.all_to_all(x, axes, 0, 0, tiled=True)  10.3 us
    all_to_all x1, blocking collectives, exchanged(): return lax.all_to_all(x, axes, 0, 0, tiled=True)  9.78 us
    all_to_all x1, starting transfers between devices, body(): stats = lax.all_to_all(stats, FAR, 0, 0, tiled=True)  9.68 us
    ppermute x1, starting transfers between devices, body(): came = lax.ppermute(edges, 'z2', [(0, 1), (1, 0)])  6.76 us
    all_gather x1, blocking collectives, body(): whole = lax.all_gather(half, 'co', axis=0, tiled=True)  6.52 us
    all_gather x1, blocking collectives, body(): came = lax.all_gather(send, 'z1', axis=0, tiled=False)  5.05 us
  transfers between devices with their start and end apart: 8, of which 6 were waited for; matrix products, arithmetic and copies ran while one was open for 0% of the time, Pallas kernels for 3%

profile of v3, /device:TPU:1, one launch (start us, length us, event | category | flops | bytes accessed | tf_op | source)
XLA Modules:
  0.0 109.7 jit_solution(15405990673882165149)
XLA Ops:
  0.6 0.9 copy-done.1
  1.6 0.9 copy-done.3
  2.5 1.4 %shard_map.102 = (bf16[1024,128]{1,0:T(8,128)(2,1)S(1)}, bf16[1024,128]{1,0:T(8,128)(2,1)S(1)}, bf16[2,160,128]{2,1,0:T(8,128)(2,1)S(1)}, f32[32,1,128]{2,1,0:T(1,128)}) custom-call(bf16[1,128,1024]{2,1,0:T(8,128)(2,1)S(1)} %copy-done.3, bf16[1,128,1024]{2,1,0:T(8,128)(2,1)S(1)} %copy-done.1), custom_call_target="tpu_custom_call" | custom-call | tf_op jit(solution)/shard_map/pallas_call | solution.py:365
  4.0 6.8 %collective-permute-start = (bf16[2,160,128]{2,1,0:T(8,128)(2,1)S(1)}, bf16[2,160,128]{2,1,0:T(8,128)(2,1)S(1)}, u32[]{:S(2)}, u32[]{:S(2)}) collective-permute-start(bf16[2,160,128]{2,1,0:T(8,128)(2,1)S(1)} %get-tuple-element.26.own_ref), channel_id=1, source_target_pairs={{0,2},{2,0},{1,3},{3,1},{4,6},{6,4},{5,7},{7,5},{8,10},{10,8},{9,1... | collective-permute-start | bytes 245768 | tf_op jit(solution)/shard_map/ppermute | solution.py:378
  10.8 9.7 %all-to-all-start = ((f32[32,1,128]{2,1,0:T(1,128)}), f32[32,1,128]{2,1,0:T(1,128)S(1)}, u32[]{:S(2)}, u32[]{:S(2)}) async-start(f32[32,1,128]{2,1,0:T(1,128)} %get-tuple-element.29), calls=%async_computation | async-start | bytes 32768 | tf_op jit(solution)/shard_map/all_to_all | solution.py:379
  21.2 5.0 %all-gather = bf16[6,128,128]{2,1,0:T(8,128)(2,1)S(1)} all-gather(bf16[3,128,128]{2,1,0:T(8,128)(2,1)S(1)} %get-tuple-element.28), channel_id=2, replica_groups=mesh['y'=8,'x'=4,'zh'=2,'co'=2,'z2'=2,'z1'=2] {'z1'}, dimensions={0}, use_global_device_ids=true | all-gather | bytes 294912 | tf_op jit(solution)/shard_map/all_gather | solution.py:392
  26.2 2.7 %all-to-all-done.in_stat_ref = f32[32,1,128]{2,1,0:T(1,128)S(1)} async-done(((f32[32,1,128]{2,1,0:T(1,128)}), f32[32,1,128]{2,1,0:T(1,128)S(1)}, u32[]{:S(2)}, u32[]{:S(2)}) %all-to-all-start) | async-done | bytes 16416 | tf_op jit(solution)/shard_map/all_to_all | solution.py:379
  29.8 3.5 %collective-permute-start.1 = (bf16[128,128]{1,0:T(8,128)(2,1)S(1)}, bf16[128,128]{1,0:T(8,128)(2,1)S(1)}, u32[]{:S(2)}, u32[]{:S(2)}) collective-permute-start(bf16[128,128]{1,0:T(8,128)(2,1)S(1)} %get-tuple-element.34), channel_id=1, source_target_pairs={{0,498},{1,7},{2,16},{3,509},{4,502},{5,11},{6,20},{7,1},{8,506},{... | collective-permute-start | bytes 98312 | tf_op jit(solution)/shard_map/ppermute | solution.py:405
  33.3 17.6 %all_to_all.25.in_stat_ref = f32[16,1,128]{2,1,0:T(1,128)S(1)} all-to-all(f32[16,1,128]{2,1,0:T(1,128)S(1)} %get-tuple-element.31), channel_id=1, replica_groups=mesh['y'=8,'x'=4,'zh'=2,'co'=2,'z2'=2,'z1'=2] {'zh','co','z2','z1'}, dimensions={0} | all-to-all | bytes 16384 | tf_op jit(solution)/shard_map/all_to_all | solution.py:410
  50.9 2.3 %shard_map.105 = (f32[640,128]{1,0:T(8,128)S(1)}, f32[640,128]{1,0:T(8,128)S(1)}, f32[1024,128]{1,0:T(8,128)S(1)}, f32[2,128]{1,0:T(2,128)S(1)}) custom-call(s32[10]{0:T(128)S(1)} %pad_add_fusion.info_ref, bf16[1024,128]{1,0:T(8,128)(2,1)S(1)} %get-tuple-element.24.xt_ref, bf16[1024,128]{1,0:T(8,128)(2,1)S(1)} %get-tuple-element.25.ct_ref, ...), custom_call_target="tpu_custom_call" | custom-call | tf_op jit(solution)/shard_map/pallas_call | solution.py:411
  53.3 2.6 %collective-permute-start.2 = (f32[640,128]{1,0:T(8,128)S(1)}, f32[640,128]{1,0:T(8,128)S(1)}, u32[]{:S(2)}, u32[]{:S(2)}) collective-permute-start(f32[640,128]{1,0:T(8,128)S(1)} %get-tuple-element.38), channel_id=1, source_target_pairs={{0,4},{4,0},{1,5},{5,1},{2,6},{6,2},{3,7},{7,3},{8,12},{12,8},{9,1... | collective-permute-start | bytes 983048 | tf_op jit(solution)/shard_map/ppermute | solution.py:425
  55.9 1.2 %collective-permute-done.2.b_ref = f32[640,128]{1,0:T(8,128)S(1)} collective-permute-done((f32[640,128]{1,0:T(8,128)S(1)}, f32[640,128]{1,0:T(8,128)S(1)}, u32[]{:S(2)}, u32[]{:S(2)}) %collective-permute-start.2) | collective-permute-done | bytes 327712 | tf_op jit(solution)/shard_map/ppermute | solution.py:425
  57.9 5.5 %all-to-all-start.2 = ((f32[32,5,4,128]{3,2,1,0:T(4,128)}), f32[32,5,4,128]{3,2,1,0:T(4,128)S(1)}, u32[]{:S(2)}, u32[]{:S(2)}) async-start(f32[32,5,4,128]{3,2,1,0:T(4,128)} %bitcast.8), calls=%async_computation.2 | async-start | bytes 655360 | tf_op jit(solution)/shard_map/all_to_all | solution.py:352
  63.4 2.2 %collective-permute-start.3 = (bf16[128,128]{1,0:T(8,128)(2,1)S(1)}, bf16[128,128]{1,0:T(8,128)(2,1)S(1)}, u32[]{:S(2)}, u32[]{:S(2)}) collective-permute-start(bf16[128,128]{1,0:T(8,128)(2,1)S(1)} %collective-permute-done.1.in_ref.own_ref), channel_id=1, source_target_pairs={{0,1},{1,0},{2,3},{3,2},{4,5},{5,4},{6,7},{7,6},{8,9},{9,8},{10,11... | collective-permute-start | bytes 98312 | tf_op jit(solution)/shard_map/ppermute | solution.py:424
  65.6 2.7 %collective-permute-done.3.other_ref = bf16[128,128]{1,0:T(8,128)(2,1)S(1)} collective-permute-done((bf16[128,128]{1,0:T(8,128)(2,1)S(1)}, bf16[128,128]{1,0:T(8,128)(2,1)S(1)}, u32[]{:S(2)}, u32[]{:S(2)}) %collective-permute-start.3) | collective-permute-done | bytes 32800 | tf_op jit(solution)/shard_map/ppermute | solution.py:424
  68.3 7.8 %all-to-all-done.2 = f32[32,5,4,128]{3,2,1,0:T(4,128)S(1)} async-done(((f32[32,5,4,128]{3,2,1,0:T(4,128)}), f32[32,5,4,128]{3,2,1,0:T(4,128)S(1)}, u32[]{:S(2)}, u32[]{:S(2)}) %all-to-all-start.2) | async-done | bytes 327712 | tf_op jit(solution)/shard_map/all_to_all | solution.py:352
  76.2 9.8 %all_to_all.26 = f32[8,5,4,128]{3,2,1,0:T(4,128)S(1)} all-to-all(f32[8,5,4,128]{3,2,1,0:T(4,128)S(1)} %bitcast.23), channel_id=1, replica_groups=mesh['y'=8,'x'=4,'zh'=2,'co'=2,'z2'=2,'z1'=2] {'zh','z2','z1'}, dimensions={0} | all-to-all | bytes 163840 | tf_op jit(solution)/shard_map/all_to_all | solution.py:352
  86.7 4.8 %all-to-all-start.4 = ((f32[32,5,4,128]{3,2,1,0:T(4,128)}), f32[32,5,4,128]{3,2,1,0:T(4,128)S(1)}, u32[]{:S(2)}, u32[]{:S(2)}) async-start(f32[32,5,4,128]{3,2,1,0:T(4,128)} %bitcast.12), calls=%async_computation.4 | async-start | bytes 655360 | tf_op jit(solution)/shard_map/all_to_all | solution.py:352
  91.5 2.0 %collective-permute-start.4 = (bf16[2,64,128]{2,1,0:T(8,128)(2,1)S(1)}, bf16[2,64,128]{2,1,0:T(8,128)(2,1)S(1)}, u32[]{:S(2)}, u32[]{:S(2)}) collective-permute-start(bf16[2,64,128]{2,1,0:T(8,128)(2,1)S(1)} %get-tuple-element.40.pair_ref), channel_id=1, source_target_pairs={{0,2},{2,0},{1,3},{3,1},{4,6},{6,4},{5,7},{7,5},{8,10},{10,8},{9,1... | collective-permute-start | bytes 98312 | tf_op jit(solution)/shard_map/ppermute | solution.py:440
  93.5 3.9 %collective-permute-done.4.others_ref = bf16[2,64,128]{2,1,0:T(8,128)(2,1)S(1)} collective-permute-done((bf16[2,64,128]{2,1,0:T(8,128)(2,1)S(1)}, bf16[2,64,128]{2,1,0:T(8,128)(2,1)S(1)}, u32[]{:S(2)}, u32[]{:S(2)}) %collective-permute-start.4) | collective-permute-done | bytes 32800 | tf_op jit(solution)/shard_map/ppermute | solution.py:440
  97.4 2.3 %shard_map.109 = (bf16[1,128,1024]{2,1,0:T(8,128)(2,1)}, f32[1,128]{1,0:T(1,128)}, f32[1,128]{1,0:T(1,128)}) custom-call(s32[10]{0:T(128)S(1)} %pad_add_fusion.info_ref, f32[1024,128]{1,0:T(8,128)S(1)} %get-tuple-element.35.pre_ref, bf16[1024,128]{1,0:T(8,128)(2,1)S(1)} %get-tuple-element.24.xt_ref, f32[2,128]{1,0:T(2,128)S(1)} %get-tuple-element.36.norm_ref, ...), custom_call_target="tpu_custom_call" | custom-call | tf_op jit(solution)/shard_map/pallas_call | solution.py:444
  99.7 2.7 %all-to-all-done.4 = f32[32,5,4,128]{3,2,1,0:T(4,128)S(1)} async-done(((f32[32,5,4,128]{3,2,1,0:T(4,128)}), f32[32,5,4,128]{3,2,1,0:T(4,128)S(1)}, u32[]{:S(2)}, u32[]{:S(2)}) %all-to-all-start.4) | async-done | bytes 327712 | tf_op jit(solution)/shard_map/all_to_all | solution.py:352
  102.3 6.5 %all_gather.11 = f32[64,5,4,128]{3,2,1,0:T(4,128)S(1)} all-gather(f32[32,5,4,128]{3,2,1,0:T(4,128)S(1)} %all-to-all-done.4), channel_id=1, replica_groups=mesh['y'=8,'x'=4,'zh'=2,'co'=2,'z2'=2,'z1'=2] {'co'}, dimensions={0}, use_global_device_ids=true | all-gather | bytes 983040 | tf_op jit(solution)/shard_map/all_gather | solution.py:443
  108.8 0.9 shard_map.110
  (22 shorter events, 3.1 us)
Async XLA Ops:
  0.6 1.0 copy-start.1
  1.6 0.9 copy-start.3
  2.5 17.9 %copy-start.6 = (s32[1,4]{1,0:T(1,128)S(1)}, s32[1,4]{1,0:T(1,128)}, u32[]{:S(2)}) copy-start(s32[1,4]{1,0:T(1,128)} %param.13) | copy-start | bytes 52
  2.5 17.9 %copy-start.7 = (s32[1,4]{1,0:T(1,128)S(1)}, s32[1,4]{1,0:T(1,128)}, u32[]{:S(2)}) copy-start(s32[1,4]{1,0:T(1,128)} %param.12) | copy-start | bytes 52
  2.5 18.0 %copy-start.4 = (f32[128]{0:T(128)S(1)}, f32[128]{0:T(128)}, u32[]{:S(2)}) copy-start(f32[128]{0:T(128)} %param.10) | copy-start | bytes 1540
  2.5 18.0 %copy-start.5 = (f32[128]{0:T(128)S(1)}, f32[128]{0:T(128)}, u32[]{:S(2)}) copy-start(f32[128]{0:T(128)} %param.11) | copy-start | bytes 1540
  4.0 25.0 %copy-start = (bf16[128,9,128]{2,0,1:T(8,128)(2,1)S(1)}, bf16[128,9,128]{2,0,1:T(8,128)(2,1)}, u32[]{:S(2)}) copy-start(bf16[128,9,128]{2,0,1:T(8,128)(2,1)} %param.9) | copy-start | bytes 884740
  4.0 16.6 %collective-permute-start = (bf16[2,160,128]{2,1,0:T(8,128)(2,1)S(1)}, bf16[2,160,128]{2,1,0:T(8,128)(2,1)S(1)}, u32[]{:S(2)}, u32[]{:S(2)}) collective-permute-start(bf16[2,160,128]{2,1,0:T(8,128)(2,1)S(1)} %get-tuple-element.26.own_ref), channel_id=1, source_target_pairs={{0,2},{2,0},{1,3},{3,1},{4,6},{6,4},{5,7},{7,5},{8,10},{10,8},{9,1... | collective-permute-start | bytes 245768 | tf_op jit(solution)/shard_map/ppermute | solution.py:378
  10.8 18.2 %all-to-all-start = ((f32[32,1,128]{2,1,0:T(1,128)}), f32[32,1,128]{2,1,0:T(1,128)S(1)}, u32[]{:S(2)}, u32[]{:S(2)}) async-start(f32[32,1,128]{2,1,0:T(1,128)} %get-tuple-element.29), calls=%async_computation | async-start | bytes 32768 | tf_op jit(solution)/shard_map/all_to_all | solution.py:379
  29.0 22.0 %copy-start.2 = (bf16[1,128,1024]{2,1,0:T(8,128)(2,1)S(1)}, bf16[1,128,1024]{2,1,0:T(8,128)(2,1)}, u32[]{:S(2)}) copy-start(bf16[1,128,1024]{2,1,0:T(8,128)(2,1)} %cot_ref.1) | copy-start | bytes 786436
  29.8 21.1 %collective-permute-start.1 = (bf16[128,128]{1,0:T(8,128)(2,1)S(1)}, bf16[128,128]{1,0:T(8,128)(2,1)S(1)}, u32[]{:S(2)}, u32[]{:S(2)}) collective-permute-start(bf16[128,128]{1,0:T(8,128)(2,1)S(1)} %get-tuple-element.34), channel_id=1, source_target_pairs={{0,498},{1,7},{2,16},{3,509},{4,502},{5,11},{6,20},{7,1},{8,506},{... | collective-permute-start | bytes 98312 | tf_op jit(solution)/shard_map/ppermute | solution.py:405
  53.3 3.8 %collective-permute-start.2 = (f32[640,128]{1,0:T(8,128)S(1)}, f32[640,128]{1,0:T(8,128)S(1)}, u32[]{:S(2)}, u32[]{:S(2)}) collective-permute-start(f32[640,128]{1,0:T(8,128)S(1)} %get-tuple-element.38), channel_id=1, source_target_pairs={{0,4},{4,0},{1,5},{5,1},{2,6},{6,2},{3,7},{7,3},{8,12},{12,8},{9,1... | collective-permute-start | bytes 983048 | tf_op jit(solution)/shard_map/ppermute | solution.py:425
  57.9 18.2 %all-to-all-start.2 = ((f32[32,5,4,128]{3,2,1,0:T(4,128)}), f32[32,5,4,128]{3,2,1,0:T(4,128)S(1)}, u32[]{:S(2)}, u32[]{:S(2)}) async-start(f32[32,5,4,128]{3,2,1,0:T(4,128)} %bitcast.8), calls=%async_computation.2 | async-start | bytes 655360 | tf_op jit(solution)/shard_map/all_to_all | solution.py:352
  63.4 5.0 %collective-permute-start.3 = (bf16[128,128]{1,0:T(8,128)(2,1)S(1)}, bf16[128,128]{1,0:T(8,128)(2,1)S(1)}, u32[]{:S(2)}, u32[]{:S(2)}) collective-permute-start(bf16[128,128]{1,0:T(8,128)(2,1)S(1)} %collective-permute-done.1.in_ref.own_ref), channel_id=1, source_target_pairs={{0,1},{1,0},{2,3},{3,2},{4,5},{5,4},{6,7},{7,6},{8,9},{9,8},{10,11... | collective-permute-start | bytes 98312 | tf_op jit(solution)/shard_map/ppermute | solution.py:424
  86.7 15.6 %all-to-all-start.4 = ((f32[32,5,4,128]{3,2,1,0:T(4,128)}), f32[32,5,4,128]{3,2,1,0:T(4,128)S(1)}, u32[]{:S(2)}, u32[]{:S(2)}) async-start(f32[32,5,4,128]{3,2,1,0:T(4,128)} %bitcast.12), calls=%async_computation.4 | async-start | bytes 655360 | tf_op jit(solution)/shard_map/all_to_all | solution.py:352
  91.5 5.9 %collective-permute-start.4 = (bf16[2,64,128]{2,1,0:T(8,128)(2,1)S(1)}, bf16[2,64,128]{2,1,0:T(8,128)(2,1)S(1)}, u32[]{:S(2)}, u32[]{:S(2)}) collective-permute-start(bf16[2,64,128]{2,1,0:T(8,128)(2,1)S(1)} %get-tuple-element.40.pair_ref), channel_id=1, source_target_pairs={{0,2},{2,0},{1,3},{3,1},{4,6},{6,4},{5,7},{7,5},{8,10},{10,8},{9,1... | collective-permute-start | bytes 98312 | tf_op jit(solution)/shard_map/ppermute | solution.py:440

commit v4 on v3

--- a/solution.py
+++ b/solution.py
@@ -37,6 +37,7 @@
 BF16 = jnp.bfloat16
 VMEM = pl.BlockSpec(memory_space=pltpu.VMEM)
 SMEM = pl.BlockSpec(memory_space=pltpu.SMEM)
+START_VMEM = 56098816
 PARAMS = pltpu.CompilerParams(vmem_limit_bytes=40 * 1024 * 1024)
 
 
@@ -71,11 +72,23 @@
     return mean, spread
 
 
-def start_kernel(x_ref, c_ref, xt_ref, ct_ref, edge_ref, stat_ref, x_scr, c_scr):
-    x = x_ref[0].astype(F32).T
+def start_kernel(
+    x_hbm, c_hbm, xt_ref, ct_ref, edge_ref, stat_ref, x_in, c_in, x_scr, c_scr, sems
+):
+    copies = []
+    for kind, (far, near) in enumerate(((x_hbm, x_in), (c_hbm, c_in))):
+        for k in range(4):
+            at = pl.ds(k * 32, 32)
+            copies.append(pltpu.make_async_copy(far.at[0, at], near.at[at], sems.at[kind, k]))
+            copies[-1].start()
+    for copy in copies[:4]:
+        copy.wait()
+    x = x_in[...].astype(F32).T
     x_scr[...] = x
     xt_ref[...] = x.astype(BF16)
-    c = c_ref[0].astype(F32).T
+    for copy in copies[4:]:
+        copy.wait()
+    c = c_in[...].astype(F32).T
     c_scr[...] = c
     ct_ref[...] = c.astype(BF16)
     for kind, (scr, flat) in enumerate(((x_scr, xt_ref), (c_scr, ct_ref))):
@@ -91,14 +104,33 @@
     stat_ref[...] = jnp.broadcast_to(packed(mean, spread)[None], (N_FAR, 1, C))
 
 
+def corners_of(info_ref, side):
+    start = jnp.where(side == 1, 1, jnp.where(side == 2, 3, 0))
+    end = jnp.where(side == 0, 1, jnp.where(side == 3, 3, 2))
+    return info_ref[5 + start] == side % 2, info_ref[5 + end] == side % 2
+
+
+TAPS = ((0, 1, 2), (2, 5, 8), (6, 7, 8), (0, 3, 6))
+FIRST, LAST, CORE, SIDE, AT_START, AT_END, BACK, ODD = 0, 1, 2, 3, 7, 8, 9, 10
+
+
 def middle_kernel(
     info_ref, own_ref, other_ref, gain_ref, shift_ref,
-    send_ref, left_ref, affine_ref, side_scr,
+    send_ref, left_ref, affine_ref, mark_ref, side_scr,
 ):
     place = info_ref[0]
     odd = place % 2
     pair = (place + 2) % 4
     affine_ref[0:1], affine_ref[1:2] = gain_ref[...], shift_ref[...]
+    mine = side_facing(info_ref, place)
+    at_start, at_end = corners_of(info_ref, mine)
+    marks = (
+        [place == 0, place == 3, info_ref[9] == 1]
+        + [mine == e for e in range(4)]
+        + [at_start, at_end, info_ref[1 + mine] // 4 == 1, odd == 1]
+    )
+    for k, mark in enumerate(marks):
+        mark_ref[k : k + 1] = jnp.full((1, C), jnp.where(mark, 1.0, 0.0), F32)
     zero = jnp.zeros((S, C), BF16)
     first, last = slice(0, S), slice(S, 2 * S)
     for kind in range(2):
@@ -128,16 +160,6 @@
     return side
 
 
-def side_parts(info_ref, side):
-    first = jnp.where(side == 1, 2, jnp.where(side == 2, 6, 0))
-    step = jnp.where(side % 2 == 1, 3, 1)
-    start = jnp.where(side == 1, 1, jnp.where(side == 2, 3, 0))
-    end = jnp.where(side == 0, 1, jnp.where(side == 3, 3, 2))
-    mine = side % 2
-    taps = [first, first + step, first + 2 * step]
-    return taps, info_ref[5 + start] == mine, info_ref[5 + end] == mine
-
-
 def flip_matrix():
     a = lax.broadcasted_iota(jnp.int32, (S, S), 0)
     b = lax.broadcasted_iota(jnp.int32, (S, S), 1)
@@ -146,114 +168,56 @@
 
 def turned(strip, flag):
     back = jnp.dot(flip_matrix(), strip, preferred_element_type=F32)
-    return jnp.where(flag == 1, back, strip.astype(F32)).astype(BF16)
+    return jnp.where(flag, back, strip.astype(F32)).astype(BF16)
 
 
 def seam_kernel(
-    info_ref, keep_ref, in_ref, in_stat_ref, w_ref, message_ref, strips_ref, rows_ref, stat_ref,
+    mark_ref, keep_ref, in_ref, in_stat_ref, w_ref, message_ref, strips_ref, rows_ref, stat_ref,
 ):
-    place = info_ref[0]
-    odd = place % 2 == 1
-    side = side_facing(info_ref, place)
-    other = 1 - place % 2
-    strips = keep_ref[...] + in_ref[other, 0]
+    def mark(k):
+        return mark_ref[k : k + 1] > 0.5
+
+    def other(k):
+        return jnp.where(mark(ODD), in_ref[0, k].astype(F32), in_ref[1, k].astype(F32))
+
+    strips = (keep_ref[...].astype(F32) + other(0)).astype(BF16)
     strips_ref[...] = strips
     grads = strips[S : 2 * S]
-    taps, at_start, at_end = side_parts(info_ref, side)
-    parts = [jnp.dot(grads, w_ref[tap], preferred_element_type=F32) for tap in taps]
+    parts = []
+    for k in range(3):
+        weight = w_ref[TAPS[0][k]].astype(F32)
+        for e in range(1, 4):
+            weight = jnp.where(mark(SIDE + e), w_ref[TAPS[e][k]].astype(F32), weight)
+        parts.append(jnp.dot(grads, weight.astype(BF16), preferred_element_type=F32))
     row = lax.broadcasted_iota(jnp.int32, (S, C), 0)
     first, last = row == 0, row == S - 1
     grad = parts[1]
     grad = grad + jnp.where(last, 0.0, pltpu.roll(parts[0], S - 1, 0))
     grad = grad + jnp.where(first, 0.0, pltpu.roll(parts[2], 1, 0))
-    grad = grad + jnp.where(first & at_start, parts[0], 0.0)
-    grad = grad + jnp.where(last & at_end, parts[2], 0.0)
+    grad = grad + jnp.where(first & mark(AT_START), parts[0], 0.0)
+    grad = grad + jnp.where(last & mark(AT_END), parts[2], 0.0)
     message_ref[0:S] = strips[0:S]
-    message_ref[S : 2 * S] = turned(grad.astype(BF16), info_ref[1 + side] // 4)
-    direct, passed = in_ref[other, 1], in_ref[other, 2]
-    above, below = jnp.where(odd, direct, passed), jnp.where(odd, passed, direct)
-    zero = jnp.zeros((S, C), BF16)
-    rows_ref[0:S] = above[0:S]
-    rows_ref[S : 2 * S] = below[0:S]
-    rows_ref[2 * S : 3 * S] = jnp.where(place == 0, zero, above[S : 2 * S])
-    rows_ref[3 * S : 4 * S] = jnp.where(place == 3, zero, below[S : 2 * S])
+    message_ref[S : 2 * S] = turned(grad.astype(BF16), mark(BACK))
+    direct, passed = other(1), other(2)
+    above = jnp.where(mark(ODD), direct, passed)
+    below = jnp.where(mark(ODD), passed, direct)
+    rows_ref[0:S] = above[0:S].astype(BF16)
+    rows_ref[S : 2 * S] = below[0:S].astype(BF16)
+    rows_ref[2 * S : 3 * S] = jnp.where(mark(FIRST), 0.0, above[S : 2 * S]).astype(BF16)
+    rows_ref[3 * S : 4 * S] = jnp.where(mark(LAST), 0.0, below[S : 2 * S]).astype(BF16)
     stats = packed(*merge([in_stat_ref[k] for k in range(N_FAR)], LOCAL))
     stat_ref[...] = jnp.broadcast_to(stats[None], (N_NEAR, 1, C))
 
 
-def main_kernel(
-    info_ref, xt_ref, ct_ref, cot_ref, rows_ref, in_stat_ref, w_ref, affine_ref,
-    strips_ref, in_ref, keep_ref, send_ref, pre_ref, norm_ref, weight_scr,
-):
-    place = info_ref[0]
-    mean, spread = merge([in_stat_ref[k] for k in range(N_NEAR)], LOCAL * N_FAR)
-    rstd = lax.rsqrt(spread * (1.0 / ENTRIES) + EPSILON)
-    gain, shift = affine_ref[0:1], affine_ref[1:2]
-    norm_ref[...] = jnp.concatenate([mean, rstd], axis=0)
-
-    def affine(raw):
-        normed = (raw.astype(F32) - mean) * rstd
-        pre = normed * gain + shift
-        return normed, pre, 1.0 / (1.0 + jnp.exp(-pre))
-
-    def activated(raw):
-        _, pre, sig = affine(raw)
-        return (pre * sig).astype(BF16).astype(F32)
-
-    wide = CELLS + 2 * S
-    column = lax.broadcasted_iota(jnp.int32, (wide, C), 0) & (S - 1)
-    starts, ends = column == 0, column == S - 1
-
-    def beside(middle):
-        before = jnp.where(starts, 0.0, pltpu.roll(middle, 1, 0))
-        after = jnp.where(ends, 0.0, pltpu.roll(middle, wide - 1, 0))
-        return before.astype(BF16), middle.astype(BF16), after.astype(BF16)
-
-    top = jnp.where(place == 0, 0.0, activated(rows_ref[0:S]))
-    bottom = jnp.where(place == 3, 0.0, activated(rows_ref[S : 2 * S]))
-    normed, pre, sig = affine(xt_ref[...])
-    own = (pre * sig).astype(BF16).astype(F32)
-    windows = jnp.concatenate(beside(jnp.concatenate([top, own, bottom], axis=0)), axis=1)
-    grad_out = cot_ref[0]
-    for i in range(3):
-        part = jnp.dot(grad_out, windows[i * S : i * S + CELLS], preferred_element_type=F32)
-        for j in range(3):
-            weight_scr[3 * i + j] = part[:, j * C : (j + 1) * C]
-
-    side = side_facing(info_ref, place)
-    taps, at_start, at_end = side_parts(info_ref, side)
-    halo = activated(turned(in_ref[0:S], info_ref[1 + side] // 4)).astype(BF16)
-    halo = jnp.concatenate([halo, halo], axis=0)
-    strip = strips_ref[S : 2 * S].astype(F32)
-    row = lax.broadcasted_iota(jnp.int32, (S, C), 0)
-    first, last = row == 0, row == S - 1
-    lines = (
-        (jnp.where(last, 0.0, pltpu.roll(strip, S - 1, 0)), jnp.where(first & at_start, strip, 0.0)),
-        (strip, jnp.zeros((S, C), F32)),
-        (jnp.where(first, 0.0, pltpu.roll(strip, 1, 0)), jnp.where(last & at_end, strip, 0.0)),
-    )
-    for tap, pair in zip(taps, lines):
-        weight_scr[tap] += lax.dot_general(
-            jnp.concatenate(pair, axis=0).astype(BF16),
-            halo,
-            (((0,), (0,)), ((), ())),
-            preferred_element_type=F32,
-        )
-    core = info_ref[9]
-
-    def put(row, low, high):
-        at = pl.ds(row, N_FAR, stride=CHUNK)
-        keep_ref[at, :] = jnp.where(core == 0, low, high)
-        send_ref[at, :] = jnp.where(core == 0, high, low)
-
-    for tap in range(9):
-        for h in range(2):
-            put(
-                h * 9 + tap,
-                weight_scr[tap, h * 64 : h * 64 + 32],
-                weight_scr[tap, h * 64 + 32 : (h + 1) * 64],
-            )
-
+def beside(middle):
+    wide = middle.shape[0]
+    column = lax.broadcasted_iota(jnp.int32, middle.shape, 0) & (S - 1)
+    before = jnp.where(column == 0, 0.0, pltpu.roll(middle, 1, 0))
+    after = jnp.where(column == S - 1, 0.0, pltpu.roll(middle, wide - 1, 0))
+    return before.astype(BF16), middle.astype(BF16), after.astype(BF16)
+
+
+def grad_kernel(ct_ref, rows_ref, w_ref, out_ref):
     grads = jnp.concatenate(
         [rows_ref[2 * S : 3 * S], ct_ref[...], rows_ref[3 * S : 4 * S]], axis=0
     ).astype(F32)
@@ -265,7 +229,79 @@
             shifted[(2 - i) * S : (2 - i) * S + CELLS], weight, preferred_element_type=F32
         )
         act_grad = term if act_grad is None else act_grad + term
-    pre_grad = act_grad * (sig * (1.0 + pre * (1.0 - sig)))
+    out_ref[...] = act_grad
+
+
+def main_kernel(
+    mark_ref, xt_ref, cot_ref, rows_ref, in_stat_ref, affine_ref, act_grad_ref,
+    strips_ref, in_ref, keep_ref, send_ref, pre_ref, norm_ref, weight_scr,
+):
+    def mark(k):
+        return mark_ref[k : k + 1] > 0.5
+
+    mean, spread = merge([in_stat_ref[k] for k in range(N_NEAR)], LOCAL * N_FAR)
+    rstd = lax.rsqrt(spread * (1.0 / ENTRIES) + EPSILON)
+    gain, shift = affine_ref[0:1], affine_ref[1:2]
+    norm_ref[...] = jnp.concatenate([mean, rstd], axis=0)
+
+    def affine(raw):
+        normed = (raw.astype(F32) - mean) * rstd
+        pre = normed * gain + shift
+        return normed, pre, 1.0 / (1.0 + jnp.exp(-pre))
+
+    def activated(raw):
+        _, pre, sig = affine(raw)
+        return (pre * sig).astype(BF16).astype(F32)
+
+    top = jnp.where(mark(FIRST), 0.0, activated(rows_ref[0:S]))
+    bottom = jnp.where(mark(LAST), 0.0, activated(rows_ref[S : 2 * S]))
+    normed, pre, sig = affine(xt_ref[...])
+    own = (pre * sig).astype(BF16).astype(F32)
+    windows = jnp.concatenate(beside(jnp.concatenate([top, own, bottom], axis=0)), axis=1)
+    grad_out = cot_ref[0]
+    for i in range(3):
+        part = jnp.dot(grad_out, windows[i * S : i * S + CELLS], preferred_element_type=F32)
+        for j in range(3):
+            weight_scr[3 * i + j] = part[:, j * C : (j + 1) * C]
+
+    halo = activated(turned(in_ref[0:S], mark(BACK))).astype(BF16)
+    halo = jnp.concatenate([halo, halo], axis=0)
+    strip = strips_ref[S : 2 * S].astype(F32)
+    row = lax.broadcasted_iota(jnp.int32, (S, C), 0)
+    first, last = row == 0, row == S - 1
+    lines = (
+        (jnp.where(last, 0.0, pltpu.roll(strip, S - 1, 0)), jnp.where(first & mark(AT_START), strip, 0.0)),
+        (strip, jnp.zeros((S, C), F32)),
+        (jnp.where(first, 0.0, pltpu.roll(strip, 1, 0)), jnp.where(last & mark(AT_END), strip, 0.0)),
+    )
+    terms = [
+        lax.dot_general(
+            jnp.concatenate(pair, axis=0).astype(BF16),
+            halo,
+            (((0,), (0,)), ((), ())),
+            preferred_element_type=F32,
+        )
+        for pair in lines
+    ]
+    for e, taps in enumerate(TAPS):
+        for tap, term in zip(taps, terms):
+            weight_scr[tap] += jnp.where(mark(SIDE + e), term, 0.0)
+    second = mark(CORE)
+
+    def put(row, low, high):
+        at = pl.ds(row, N_FAR, stride=CHUNK)
+        keep_ref[at, :] = jnp.where(second, high, low)
+        send_ref[at, :] = jnp.where(second, low, high)
+
+    for tap in range(9):
+        for h in range(2):
+            put(
+                h * 9 + tap,
+                weight_scr[tap, h * 64 : h * 64 + 32],
+                weight_scr[tap, h * 64 + 32 : (h + 1) * 64],
+            )
+
+    pre_grad = act_grad_ref[...] * (sig * (1.0 + pre * (1.0 - sig)))
     pre_ref[...] = pre_grad
     gain_row = jnp.sum(pre_grad * normed, axis=0, keepdims=True)
     shift_row = jnp.sum(pre_grad, axis=0, keepdims=True)
@@ -288,12 +324,16 @@
         at = (odd + k) % 2
         side_scr[base + at] = pair_ref[k]
         side_scr[(base + 2) % 4 + at] = others_ref[k]
-    own = pl.ds(pl.multiple_of(place * ROWS, ROWS), ROWS)
+
+    def returned(e, start, size):
+        at = pl.ds(pl.multiple_of(start, ROWS), size)
+        return side_scr[info_ref[1 + e] % 4, at, :].astype(F32)
+
     more_scr[...] = jnp.zeros((CELLS, C), F32)
-    more_scr[0:S] = jnp.where(place == 0, side_scr[info_ref[1] % 4].astype(F32), 0.0)
-    more_scr[CELLS - S : CELLS] = jnp.where(place == 3, side_scr[info_ref[3] % 4].astype(F32), 0.0)
-    for e, at in ((4, 0), (2, S - 1)):
-        more_scr[pl.ds(at, ROWS, stride=S), :] += side_scr[info_ref[e] % 4, own, :].astype(F32)
+    more_scr[0:S] = jnp.where(place == 0, returned(0, 0, S), 0.0)
+    more_scr[CELLS - S : CELLS] = jnp.where(place == 3, returned(2, 0, S), 0.0)
+    for e, column in ((3, 0), (1, S - 1)):
+        more_scr[pl.ds(column, ROWS, stride=S), :] += returned(e, place * ROWS, ROWS)
     mean, rstd = norm_ref[0:1], norm_ref[1:2]
     gain, shift = affine_ref[0:1], affine_ref[1:2]
     gain_total, shift_total = total_ref[18:19], total_ref[19:20]
@@ -326,8 +366,9 @@
         out_ref[k * rows : (k + 1) * rows] = total
 
 
-def add_kernel(a_ref, b_ref, out_ref):
-    out_ref[...] = a_ref[...] + b_ref[...]
+def add_kernel(mark_ref, own_ref, both_ref, out_ref):
+    second = mark_ref[CORE : CORE + 1] > 0.5
+    out_ref[...] = own_ref[...] + jnp.where(second, both_ref[0], both_ref[1])
 
 
 def summed(x, parts, copies):
@@ -370,22 +411,25 @@
             shape((2, EDGE, C), BF16),
             shape((N_FAR, 1, C), F32),
         ),
-        in_specs=[VMEM] * 2,
+        in_specs=[pl.BlockSpec(memory_space=pltpu.HBM)] * 2,
         out_specs=(VMEM,) * 4,
-        scratch_shapes=[pltpu.VMEM((CELLS, C), F32)] * 2,
-        compiler_params=PARAMS,
+        scratch_shapes=[pltpu.VMEM((C, CELLS), BF16)] * 2
+        + [pltpu.VMEM((CELLS, C), F32)] * 2
+        + [pltpu.SemaphoreType.DMA((2, 4))],
+        compiler_params=pltpu.CompilerParams(vmem_limit_bytes=START_VMEM),
     )(features, cotangent)
     came = lax.ppermute(edges, "z2", [(0, 1), (1, 0)])
     stats = lax.all_to_all(stats, FAR, 0, 0, tiled=True)
-    send, keep, affine = pl.pallas_call(
+    send, keep, affine, marks = pl.pallas_call(
         middle_kernel,
         out_shape=(
             shape((3, LINE, C), BF16),
             shape((LINE, C), BF16),
             shape((2, C), F32),
+            shape((16, C), F32),
         ),
         in_specs=[SMEM] + [VMEM] * 4,
-        out_specs=(VMEM,) * 3,
+        out_specs=(VMEM,) * 4,
         scratch_shapes=[pltpu.VMEM((2, 4, S, C), BF16)],
         compiler_params=PARAMS,
     )(info, edges, came, gain, shift)
@@ -398,16 +442,26 @@
             shape((2 * LINE, C), BF16),
             shape((N_NEAR, 1, C), F32),
         ),
-        in_specs=[SMEM] + [VMEM] * 4,
+        in_specs=[VMEM] * 5,
         out_specs=(VMEM,) * 4,
         compiler_params=PARAMS,
-    )(info, keep, came, stats, weight)
+    )(marks, keep, came, stats, weight)
     message = lax.ppermute(
         message,
         tuple(AXES),
         [(4 * t + s, 4 * ((t + STEPS[s]) % 128) + (s + 2) % 4) for t in range(128) for s in range(4)],
     )
     stats = lax.all_to_all(stats, NEAR, 0, 0, tiled=True)
+    act_grad = pl.pallas_call(
+        grad_kernel,
+        out_shape=shape((CELLS, C), F32),
+        in_specs=[VMEM] * 3,
+        out_specs=VMEM,
+        compiler_params=PARAMS,
+        cost_estimate=pl.CostEstimate(
+            flops=18 * CELLS * C * C, bytes_accessed=10 * CELLS * C, transcendentals=0
+        ),
+    )(ct, rows, weight)
     parts, send, pre_grad, norm = pl.pallas_call(
         main_kernel,
         out_shape=(
@@ -416,20 +470,20 @@
             shape((CELLS, C), F32),
             shape((2, C), F32),
         ),
-        in_specs=[SMEM] + [VMEM] * 9,
+        in_specs=[VMEM] * 9,
         out_specs=(VMEM,) * 4,
         scratch_shapes=[pltpu.VMEM((9, C, C), F32)],
         compiler_params=PARAMS,
-    )(info, xt, ct, cotangent, rows, stats, weight, affine, strips, message)
+    )(marks, xt, cotangent, rows, stats, affine, act_grad, strips, message)
     other = lax.ppermute(message, "z1", [(0, 1), (1, 0)])
-    send = lax.ppermute(send, "co", [(0, 1), (1, 0)])
+    both = lax.all_gather(send, "co", axis=0, tiled=False)
     parts = pl.pallas_call(
         add_kernel,
         out_shape=shape((N_FAR * CHUNK, C), F32),
-        in_specs=[VMEM] * 2,
+        in_specs=[VMEM] * 3,
         out_specs=VMEM,
         compiler_params=PARAMS,
-    )(parts, send)
+    )(marks, parts, both)
     parts, pair = pl.pallas_call(
         functools.partial(sum_and_pair_kernel, N_FAR, 8),
         out_shape=(shape((8 * CHUNK, C), F32), shape((2, S, C), BF16)),

time: 110 us -> 107 us (0.973)
  blocking collectives: 38.9 us -> 23.9 us
  starting transfers between devices: 37.1 us -> 45.3 us
  waiting for transfers between devices: 21 us -> 25.9 us
  local copies, waits for them, and re-layouts: 1.92 us -> 0.03 us
    all_to_all x1 -> x0, blocking collectives: 17.6 us -> none  [body(): stats = lax.all_to_all(stats, NEAR, 0, 0, tiled=True)]
    all_to_all x0 -> x1, starting transfers between devices: none -> 10.8 us  [body(): stats = lax.all_to_all(stats, NEAR, 0, 0, tiled=True)]
    all_to_all x0 -> x1, waiting for transfers between devices: none -> 6.11 us  [body(): stats = lax.all_to_all(stats, NEAR, 0, 0, tiled=True)]
    ppermute x1 -> x0, starting transfers between devices: 2.59 us -> none  [body(): send = lax.ppermute(send, 'co', [(0, 1), (1, 0)])]
    all_gather x0 -> x1, blocking collectives: none -> 2.59 us  [body(): both = lax.all_gather(send, 'co', axis=0, tiled=False)]
    unnamed x16 -> x14, local copies, waits for them, and re-layouts: 1.92 us -> 0.03 us
    ppermute x1 -> x0, waiting for transfers between devices: 1.23 us -> none  [body(): send = lax.ppermute(send, 'co', [(0, 1), (1, 0)])]
    pallas_call x1, Pallas kernels: 1.44 us -> 2.58 us  [body(): pl.pallas_call(start_kernel, out_shape=(shape((CELLS, C), BF16), shape((C...]
where the time goes in v4:
time: 107 us
  starting transfers between devices  45.3 us (42%)
  waiting for transfers between devices  25.9 us (24%)
  blocking collectives  23.9 us (22%)
  Pallas kernels  10.8 us (10%)
    all_to_all x1, starting transfers between devices, body(): stats = lax.all_to_all(stats, NEAR, 0, 0, tiled=True)  10.8 us
    all_to_all x2, waiting for transfers between devices, exchanged(): return lax.all_to_all(x, axes, 0, 0, tiled=True)  10.5 us
    all_to_all x2, starting transfers between devices, exchanged(): return lax.all_to_all(x, axes, 0, 0, tiled=True)  10.3 us
    all_to_all x1, blocking collectives, exchanged(): return lax.all_to_all(x, axes, 0, 0, tiled=True)  9.78 us
    all_to_all x1, starting transfers between devices, body(): stats = lax.all_to_all(stats, FAR, 0, 0, tiled=True)  9.68 us
    ppermute x1, starting transfers between devices, body(): came = lax.ppermute(edges, 'z2', [(0, 1), (1, 0)])  6.77 us
    all_gather x1, blocking collectives, body(): whole = lax.all_gather(half, 'co', axis=0, tiled=True)  6.52 us
    all_to_all x1, waiting for transfers between devices, body(): stats = lax.all_to_all(stats, NEAR, 0, 0, tiled=True)  6.11 us
  transfers between devices with their start and end apart: 8, of which 6 were waited for; matrix products, arithmetic and copies ran while one was open for 0% of the time, Pallas kernels for 3%

profile of v4, /device:TPU:1, one launch (start us, length us, event | category | flops | bytes accessed | tf_op | source)
XLA Modules:
  0.0 106.9 jit_solution(17358815666398480220)
XLA Ops:
  0.7 2.6 %shard_map.102 = (bf16[1024,128]{1,0:T(8,128)(2,1)S(1)}, bf16[1024,128]{1,0:T(8,128)(2,1)}, bf16[2,160,128]{2,1,0:T(8,128)(2,1)S(1)}, f32[32,1,128]{2,1,0:T(1,128)}) custom-call(bf16[1,128,1024]{2,1,0:T(8,128)(2,1)} %x_hbm.1, bf16[1,128,1024]{2,1,0:T(8,128)(2,1)} %cot_ref.1), custom_call_target="tpu_custom_call" | custom-call | tf_op jit(solution)/shard_map/pallas_call | solution.py:406
  3.3 6.8 %collective-permute-start = (bf16[2,160,128]{2,1,0:T(8,128)(2,1)S(1)}, bf16[2,160,128]{2,1,0:T(8,128)(2,1)S(1)}, u32[]{:S(2)}, u32[]{:S(2)}) collective-permute-start(bf16[2,160,128]{2,1,0:T(8,128)(2,1)S(1)} %get-tuple-element.25.own_ref), channel_id=1, source_target_pairs={{0,2},{2,0},{1,3},{3,1},{4,6},{6,4},{5,7},{7,5},{8,10},{10,8},{9,1... | collective-permute-start | bytes 245768 | tf_op jit(solution)/shard_map/ppermute | solution.py:421
  10.0 9.7 %all-to-all-start = ((f32[32,1,128]{2,1,0:T(1,128)}), f32[32,1,128]{2,1,0:T(1,128)S(1)}, u32[]{:S(2)}, u32[]{:S(2)}) async-start(f32[32,1,128]{2,1,0:T(1,128)} %get-tuple-element.30), calls=%async_computation | async-start | bytes 32768 | tf_op jit(solution)/shard_map/all_to_all | solution.py:422
  20.5 5.0 %all-gather = bf16[6,128,128]{2,1,0:T(8,128)(2,1)S(1)} all-gather(bf16[3,128,128]{2,1,0:T(8,128)(2,1)S(1)} %get-tuple-element.29), channel_id=2, replica_groups=mesh['y'=8,'x'=4,'zh'=2,'co'=2,'z2'=2,'z1'=2] {'z1'}, dimensions={0}, use_global_device_ids=true | all-gather | bytes 294912 | tf_op jit(solution)/shard_map/all_gather | solution.py:436
  25.5 2.7 %all-to-all-done.in_stat_ref = f32[32,1,128]{2,1,0:T(1,128)S(1)} async-done(((f32[32,1,128]{2,1,0:T(1,128)}), f32[32,1,128]{2,1,0:T(1,128)S(1)}, u32[]{:S(2)}, u32[]{:S(2)}) %all-to-all-start) | async-done | bytes 16416 | tf_op jit(solution)/shard_map/all_to_all | solution.py:422
  28.3 0.8 shard_map.104
  29.1 3.6 %collective-permute-start.1 = (bf16[128,128]{1,0:T(8,128)(2,1)S(1)}, bf16[128,128]{1,0:T(8,128)(2,1)S(1)}, u32[]{:S(2)}, u32[]{:S(2)}) collective-permute-start(bf16[128,128]{1,0:T(8,128)(2,1)S(1)} %get-tuple-element.36), channel_id=1, source_target_pairs={{0,498},{1,7},{2,16},{3,509},{4,502},{5,11},{6,20},{7,1},{8,506},{... | collective-permute-start | bytes 98312 | tf_op jit(solution)/shard_map/ppermute | solution.py:449
  32.7 10.8 %all-to-all-start.1 = ((f32[16,1,128]{2,1,0:T(1,128)}), f32[16,1,128]{2,1,0:T(1,128)S(1)}, u32[]{:S(2)}, u32[]{:S(2)}) async-start(f32[16,1,128]{2,1,0:T(1,128)} %get-tuple-element.32), calls=%async_computation.1 | async-start | bytes 16384 | tf_op jit(solution)/shard_map/all_to_all | solution.py:454
  44.3 6.1 %all-to-all-done.1.in_stat_ref = f32[16,1,128]{2,1,0:T(1,128)S(1)} async-done(((f32[16,1,128]{2,1,0:T(1,128)}), f32[16,1,128]{2,1,0:T(1,128)S(1)}, u32[]{:S(2)}, u32[]{:S(2)}) %all-to-all-start.1) | async-done | bytes 8224 | tf_op jit(solution)/shard_map/all_to_all | solution.py:454
  50.4 1.3 %shard_map.106 = (f32[640,128]{1,0:T(8,128)S(1)}, f32[640,128]{1,0:T(8,128)S(1)}, f32[1024,128]{1,0:T(8,128)S(1)}, f32[2,128]{1,0:T(2,128)S(1)}) custom-call(f32[16,128]{1,0:T(8,128)S(1)} %get-tuple-element.26.mark_ref, bf16[1024,128]{1,0:T(8,128)(2,1)S(1)} %get-tuple-element.27.xt_ref, bf16[1,128,1024]{2,1,0:T(8,128)(2,1)S(1)} %copy-done.1, ...), custom_call_target="tpu_custom_call" | custom-call | tf_op jit(solution)/shard_map/pallas_call | solution.py:465
  51.6 2.6 %all-gather.1 = f32[1280,128]{1,0:T(8,128)S(1)} all-gather(f32[640,128]{1,0:T(8,128)S(1)} %get-tuple-element.40), channel_id=3, replica_groups=mesh['y'=8,'x'=4,'zh'=2,'co'=2,'z2'=2,'z1'=2] {'co'}, dimensions={0}, use_global_device_ids=true | all-gather | bytes 983040 | tf_op jit(solution)/shard_map/all_gather | solution.py:479
  54.2 0.8 shard_map.107
  55.0 5.5 %all-to-all-start.2 = ((f32[32,5,4,128]{3,2,1,0:T(4,128)}), f32[32,5,4,128]{3,2,1,0:T(4,128)S(1)}, u32[]{:S(2)}, u32[]{:S(2)}) async-start(f32[32,5,4,128]{3,2,1,0:T(4,128)} %bitcast.9), calls=%async_computation.2 | async-start | bytes 655360 | tf_op jit(solution)/shard_map/all_to_all | solution.py:393
  60.5 2.2 %collective-permute-start.2 = (bf16[128,128]{1,0:T(8,128)(2,1)S(1)}, bf16[128,128]{1,0:T(8,128)(2,1)S(1)}, u32[]{:S(2)}, u32[]{:S(2)}) collective-permute-start(bf16[128,128]{1,0:T(8,128)(2,1)S(1)} %collective-permute-done.1.in_ref.own_ref), channel_id=1, source_target_pairs={{0,1},{1,0},{2,3},{3,2},{4,5},{5,4},{6,7},{7,6},{8,9},{9,8},{10,11... | collective-permute-start | bytes 98312 | tf_op jit(solution)/shard_map/ppermute | solution.py:478
  62.7 2.7 %collective-permute-done.2.other_ref = bf16[128,128]{1,0:T(8,128)(2,1)S(1)} collective-permute-done((bf16[128,128]{1,0:T(8,128)(2,1)S(1)}, bf16[128,128]{1,0:T(8,128)(2,1)S(1)}, u32[]{:S(2)}, u32[]{:S(2)}) %collective-permute-start.2) | collective-permute-done | bytes 32800 | tf_op jit(solution)/shard_map/ppermute | solution.py:478
  65.5 7.8 %all-to-all-done.2 = f32[32,5,4,128]{3,2,1,0:T(4,128)S(1)} async-done(((f32[32,5,4,128]{3,2,1,0:T(4,128)}), f32[32,5,4,128]{3,2,1,0:T(4,128)S(1)}, u32[]{:S(2)}, u32[]{:S(2)}) %all-to-all-start.2) | async-done | bytes 327712 | tf_op jit(solution)/shard_map/all_to_all | solution.py:393
  73.3 9.8 %all_to_all.25 = f32[8,5,4,128]{3,2,1,0:T(4,128)S(1)} all-to-all(f32[8,5,4,128]{3,2,1,0:T(4,128)S(1)} %bitcast.25), channel_id=1, replica_groups=mesh['y'=8,'x'=4,'zh'=2,'co'=2,'z2'=2,'z1'=2] {'zh','z2','z1'}, dimensions={0} | all-to-all | bytes 163840 | tf_op jit(solution)/shard_map/all_to_all | solution.py:393
  83.8 4.8 %all-to-all-start.4 = ((f32[32,5,4,128]{3,2,1,0:T(4,128)}), f32[32,5,4,128]{3,2,1,0:T(4,128)S(1)}, u32[]{:S(2)}, u32[]{:S(2)}) async-start(f32[32,5,4,128]{3,2,1,0:T(4,128)} %bitcast.13), calls=%async_computation.4 | async-start | bytes 655360 | tf_op jit(solution)/shard_map/all_to_all | solution.py:393
  88.6 2.0 %collective-permute-start.3 = (bf16[2,64,128]{2,1,0:T(8,128)(2,1)S(1)}, bf16[2,64,128]{2,1,0:T(8,128)(2,1)S(1)}, u32[]{:S(2)}, u32[]{:S(2)}) collective-permute-start(bf16[2,64,128]{2,1,0:T(8,128)(2,1)S(1)} %get-tuple-element.42.pair_ref), channel_id=1, source_target_pairs={{0,2},{2,0},{1,3},{3,1},{4,6},{6,4},{5,7},{7,5},{8,10},{10,8},{9,1... | collective-permute-start | bytes 98312 | tf_op jit(solution)/shard_map/ppermute | solution.py:494
  90.6 3.9 %collective-permute-done.3.others_ref = bf16[2,64,128]{2,1,0:T(8,128)(2,1)S(1)} collective-permute-done((bf16[2,64,128]{2,1,0:T(8,128)(2,1)S(1)}, bf16[2,64,128]{2,1,0:T(8,128)(2,1)S(1)}, u32[]{:S(2)}, u32[]{:S(2)}) %collective-permute-start.3) | collective-permute-done | bytes 32800 | tf_op jit(solution)/shard_map/ppermute | solution.py:494
  94.5 2.3 %shard_map.110 = (bf16[1,128,1024]{2,1,0:T(8,128)(2,1)}, f32[1,128]{1,0:T(1,128)}, f32[1,128]{1,0:T(1,128)}) custom-call(s32[10]{0:T(128)S(1)} %pad_add_fusion.info_ref, f32[1024,128]{1,0:T(8,128)S(1)} %get-tuple-element.37.pre_ref, bf16[1024,128]{1,0:T(8,128)(2,1)S(1)} %get-tuple-element.27.xt_ref, f32[2,128]{1,0:T(2,128)S(1)} %get-tuple-element.38.norm_ref, ...), custom_call_target="tpu_custom_call" | custom-call | tf_op jit(solution)/shard_map/pallas_call | solution.py:498
  96.8 2.7 %all-to-all-done.4 = f32[32,5,4,128]{3,2,1,0:T(4,128)S(1)} async-done(((f32[32,5,4,128]{3,2,1,0:T(4,128)}), f32[32,5,4,128]{3,2,1,0:T(4,128)S(1)}, u32[]{:S(2)}, u32[]{:S(2)}) %all-to-all-start.4) | async-done | bytes 327712 | tf_op jit(solution)/shard_map/all_to_all | solution.py:393
  99.5 6.5 %all_gather.19 = f32[64,5,4,128]{3,2,1,0:T(4,128)S(1)} all-gather(f32[32,5,4,128]{3,2,1,0:T(4,128)S(1)} %all-to-all-done.4), channel_id=1, replica_groups=mesh['y'=8,'x'=4,'zh'=2,'co'=2,'z2'=2,'z1'=2] {'co'}, dimensions={0}, use_global_device_ids=true | all-gather | bytes 983040 | tf_op jit(solution)/shard_map/all_gather | solution.py:497
  106.0 0.9 shard_map.111
  (21 shorter events, 2.3 us)
Async XLA Ops:
  0.6 19.1 %copy-start.5 = (s32[1,4]{1,0:T(1,128)S(1)}, s32[1,4]{1,0:T(1,128)}, u32[]{:S(2)}) copy-start(s32[1,4]{1,0:T(1,128)} %param.13) | copy-start | bytes 52
  0.6 19.1 %copy-start.6 = (s32[1,4]{1,0:T(1,128)S(1)}, s32[1,4]{1,0:T(1,128)}, u32[]{:S(2)}) copy-start(s32[1,4]{1,0:T(1,128)} %param.12) | copy-start | bytes 52
  0.7 19.2 %copy-start.3 = (f32[128]{0:T(128)S(1)}, f32[128]{0:T(128)}, u32[]{:S(2)}) copy-start(f32[128]{0:T(128)} %param.10) | copy-start | bytes 1540
  0.7 19.2 %copy-start.4 = (f32[128]{0:T(128)S(1)}, f32[128]{0:T(128)}, u32[]{:S(2)}) copy-start(f32[128]{0:T(128)} %param.11) | copy-start | bytes 1540
  3.3 25.0 %copy-start = (bf16[128,9,128]{2,0,1:T(8,128)(2,1)S(1)}, bf16[128,9,128]{2,0,1:T(8,128)(2,1)}, u32[]{:S(2)}) copy-start(bf16[128,9,128]{2,0,1:T(8,128)(2,1)} %param.9) | copy-start | bytes 884740
  3.3 16.6 %collective-permute-start = (bf16[2,160,128]{2,1,0:T(8,128)(2,1)S(1)}, bf16[2,160,128]{2,1,0:T(8,128)(2,1)S(1)}, u32[]{:S(2)}, u32[]{:S(2)}) collective-permute-start(bf16[2,160,128]{2,1,0:T(8,128)(2,1)S(1)} %get-tuple-element.25.own_ref), channel_id=1, source_target_pairs={{0,2},{2,0},{1,3},{3,1},{4,6},{6,4},{5,7},{7,5},{8,10},{10,8},{9,1... | collective-permute-start | bytes 245768 | tf_op jit(solution)/shard_map/ppermute | solution.py:421
  10.0 18.2 %all-to-all-start = ((f32[32,1,128]{2,1,0:T(1,128)}), f32[32,1,128]{2,1,0:T(1,128)S(1)}, u32[]{:S(2)}, u32[]{:S(2)}) async-start(f32[32,1,128]{2,1,0:T(1,128)} %get-tuple-element.30), calls=%async_computation | async-start | bytes 32768 | tf_op jit(solution)/shard_map/all_to_all | solution.py:422
  28.3 15.2 %copy-start.2 = (bf16[1024,128]{1,0:T(8,128)(2,1)S(1)}, bf16[1024,128]{1,0:T(8,128)(2,1)}, u32[]{:S(2)}) copy-start(bf16[1024,128]{1,0:T(8,128)(2,1)} %get-tuple-element.34.ct_ref) | copy-start | bytes 786436
  29.1 21.3 %collective-permute-start.1 = (bf16[128,128]{1,0:T(8,128)(2,1)S(1)}, bf16[128,128]{1,0:T(8,128)(2,1)S(1)}, u32[]{:S(2)}, u32[]{:S(2)}) collective-permute-start(bf16[128,128]{1,0:T(8,128)(2,1)S(1)} %get-tuple-element.36), channel_id=1, source_target_pairs={{0,498},{1,7},{2,16},{3,509},{4,502},{5,11},{6,20},{7,1},{8,506},{... | collective-permute-start | bytes 98312 | tf_op jit(solution)/shard_map/ppermute | solution.py:449
  32.7 17.7 %all-to-all-start.1 = ((f32[16,1,128]{2,1,0:T(1,128)}), f32[16,1,128]{2,1,0:T(1,128)S(1)}, u32[]{:S(2)}, u32[]{:S(2)}) async-start(f32[16,1,128]{2,1,0:T(1,128)} %get-tuple-element.32), calls=%async_computation.1 | async-start | bytes 16384 | tf_op jit(solution)/shard_map/all_to_all | solution.py:454
  43.5 6.9 %copy-start.1 = (bf16[1,128,1024]{2,1,0:T(8,128)(2,1)S(1)}, bf16[1,128,1024]{2,1,0:T(8,128)(2,1)}, u32[]{:S(2)}) copy-start(bf16[1,128,1024]{2,1,0:T(8,128)(2,1)} %cot_ref.1) | copy-start | bytes 786436
  55.0 18.3 %all-to-all-start.2 = ((f32[32,5,4,128]{3,2,1,0:T(4,128)}), f32[32,5,4,128]{3,2,1,0:T(4,128)S(1)}, u32[]{:S(2)}, u32[]{:S(2)}) async-start(f32[32,5,4,128]{3,2,1,0:T(4,128)} %bitcast.9), calls=%async_computation.2 | async-start | bytes 655360 | tf_op jit(solution)/shard_map/all_to_all | solution.py:393
  60.5 5.0 %collective-permute-start.2 = (bf16[128,128]{1,0:T(8,128)(2,1)S(1)}, bf16[128,128]{1,0:T(8,128)(2,1)S(1)}, u32[]{:S(2)}, u32[]{:S(2)}) collective-permute-start(bf16[128,128]{1,0:T(8,128)(2,1)S(1)} %collective-permute-done.1.in_ref.own_ref), channel_id=1, source_target_pairs={{0,1},{1,0},{2,3},{3,2},{4,5},{5,4},{6,7},{7,6},{8,9},{9,8},{10,11... | collective-permute-start | bytes 98312 | tf_op jit(solution)/shard_map/ppermute | solution.py:478
  83.8 15.6 %all-to-all-start.4 = ((f32[32,5,4,128]{3,2,1,0:T(4,128)}), f32[32,5,4,128]{3,2,1,0:T(4,128)S(1)}, u32[]{:S(2)}, u32[]{:S(2)}) async-start(f32[32,5,4,128]{3,2,1,0:T(4,128)} %bitcast.13), calls=%async_computation.4 | async-start | bytes 655360 | tf_op jit(solution)/shard_map/all_to_all | solution.py:393
  88.6 5.9 %collective-permute-start.3 = (bf16[2,64,128]{2,1,0:T(8,128)(2,1)S(1)}, bf16[2,64,128]{2,1,0:T(8,128)(2,1)S(1)}, u32[]{:S(2)}, u32[]{:S(2)}) collective-permute-start(bf16[2,64,128]{2,1,0:T(8,128)(2,1)S(1)} %get-tuple-element.42.pair_ref), channel_id=1, source_target_pairs={{0,2},{2,0},{1,3},{3,1},{4,6},{6,4},{5,7},{7,5},{8,10},{10,8},{9,1... | collective-permute-start | bytes 98312 | tf_op jit(solution)/shard_map/ppermute | solution.py:494

commit v5 on v4

--- a/solution.py
+++ b/solution.py
@@ -37,7 +37,7 @@
 BF16 = jnp.bfloat16
 VMEM = pl.BlockSpec(memory_space=pltpu.VMEM)
 SMEM = pl.BlockSpec(memory_space=pltpu.SMEM)
-START_VMEM = 56098816
+START_VMEM = 56360960
 PARAMS = pltpu.CompilerParams(vmem_limit_bytes=40 * 1024 * 1024)
 
 
@@ -72,36 +72,41 @@
     return mean, spread
 
 
-def start_kernel(
-    x_hbm, c_hbm, xt_ref, ct_ref, edge_ref, stat_ref, x_in, c_in, x_scr, c_scr, sems
-):
+def edge_picker():
+    row = lax.broadcasted_iota(jnp.int32, (EDGE, CELLS), 0)
+    cell = lax.broadcasted_iota(jnp.int32, (EDGE, CELLS), 1)
+    wanted = jnp.where(row < S, row, row + CELLS - 2 * S)
+    wanted = jnp.where(row >= 2 * S, (row - 2 * S) * S + S - 1, wanted)
+    wanted = jnp.where(row >= 2 * S + ROWS, (row - 2 * S - ROWS) * S, wanted)
+    return jnp.where(cell == wanted, 1.0, 0.0).astype(BF16)
+
+
+def start_kernel(x_hbm, c_hbm, edge_ref, stat_ref, x_in, c_in, sems):
     copies = []
     for kind, (far, near) in enumerate(((x_hbm, x_in), (c_hbm, c_in))):
         for k in range(4):
             at = pl.ds(k * 32, 32)
             copies.append(pltpu.make_async_copy(far.at[0, at], near.at[at], sems.at[kind, k]))
             copies[-1].start()
+    picker = edge_picker()
     for copy in copies[:4]:
         copy.wait()
-    x = x_in[...].astype(F32).T
-    x_scr[...] = x
-    xt_ref[...] = x.astype(BF16)
+    x = x_in[...].astype(F32)
+    blocks = [x[:, k * C : (k + 1) * C] for k in range(CELLS // C)]
+
+    def channel_sums(parts):
+        return group_sum(jnp.sum(sum(parts).T, axis=0, keepdims=True))
+
+    mean = channel_sums(blocks) * (1.0 / LOCAL)
+    column = jnp.broadcast_to(mean, (C, C)).T
+    spread = channel_sums([(v - column) * (v - column) for v in blocks])
+    stat_ref[...] = jnp.broadcast_to(packed(mean, spread)[None], (N_FAR, 1, C))
     for copy in copies[4:]:
         copy.wait()
-    c = c_in[...].astype(F32).T
-    c_scr[...] = c
-    ct_ref[...] = c.astype(BF16)
-    for kind, (scr, flat) in enumerate(((x_scr, xt_ref), (c_scr, ct_ref))):
-        edge_ref[kind, 0:S] = flat[0:S]
-        edge_ref[kind, S : 2 * S] = flat[CELLS - S : CELLS]
-        for k, column in enumerate((S - 1, 0)):
-            edge_ref[kind, 2 * S + k * ROWS : 2 * S + (k + 1) * ROWS] = scr[
-                pl.ds(column, ROWS, stride=S), :
-            ].astype(BF16)
-    mean = group_sum(jnp.sum(x, axis=0, keepdims=True)) * (1.0 / LOCAL)
-    gap = x - mean
-    spread = group_sum(jnp.sum(gap * gap, axis=0, keepdims=True))
-    stat_ref[...] = jnp.broadcast_to(packed(mean, spread)[None], (N_FAR, 1, C))
+    for kind, ref in enumerate((x_in, c_in)):
+        edge_ref[kind] = lax.dot_general(
+            picker, ref[...], (((1,), (1,)), ((), ())), preferred_element_type=F32
+        ).astype(BF16)
 
 
 def corners_of(info_ref, side):
@@ -217,10 +222,10 @@
     return before.astype(BF16), middle.astype(BF16), after.astype(BF16)
 
 
-def grad_kernel(ct_ref, rows_ref, w_ref, out_ref):
-    grads = jnp.concatenate(
-        [rows_ref[2 * S : 3 * S], ct_ref[...], rows_ref[3 * S : 4 * S]], axis=0
-    ).astype(F32)
+def grad_kernel(x_ref, c_ref, rows_ref, w_ref, out_ref, xt_ref):
+    xt_ref[...] = x_ref[0].astype(F32).T.astype(BF16)
+    above, below = rows_ref[2 * S : 3 * S].astype(F32), rows_ref[3 * S : 4 * S].astype(F32)
+    grads = jnp.concatenate([above, c_ref[0].astype(F32).T, below], axis=0)
     shifted = jnp.concatenate(beside(grads)[::-1], axis=1)
     act_grad = None
     for i in range(3):
@@ -314,16 +319,22 @@
         put(k, row, row)
 
 
+def slope_kernel(xt_ref, norm_ref, affine_ref, out_ref):
+    normed = (xt_ref[...].astype(F32) - norm_ref[0:1]) * norm_ref[1:2]
+    pre = normed * affine_ref[0:1] + affine_ref[1:2]
+    sig = 1.0 / (1.0 + jnp.exp(-pre))
+    out_ref[...] = sig * (1.0 + pre * (1.0 - sig))
+
+
 def end_kernel(
-    info_ref, pre_ref, xt_ref, norm_ref, affine_ref, total_ref, pair_ref, others_ref,
+    info_ref, pre_ref, xt_ref, norm_ref, affine_ref, total_ref, in_ref, slope_ref,
     out_ref, gain_sum_ref, shift_sum_ref, side_scr, more_scr,
 ):
     place = info_ref[0]
-    base, odd = place // 2 * 2, place % 2
-    for k in range(2):
-        at = (odd + k) % 2
-        side_scr[base + at] = pair_ref[k]
-        side_scr[(base + 2) % 4 + at] = others_ref[k]
+    odd = place % 2
+    for half in range(2):
+        for k in range(2):
+            side_scr[2 * half + (odd + k) % 2] = in_ref[half, k]
 
     def returned(e, start, size):
         at = pl.ds(pl.multiple_of(start, ROWS), size)
@@ -335,14 +346,12 @@
     for e, column in ((3, 0), (1, S - 1)):
         more_scr[pl.ds(column, ROWS, stride=S), :] += returned(e, place * ROWS, ROWS)
     mean, rstd = norm_ref[0:1], norm_ref[1:2]
-    gain, shift = affine_ref[0:1], affine_ref[1:2]
-    gain_total, shift_total = total_ref[18:19], total_ref[19:20]
+    gain = affine_ref[0:1]
+    gain_total, shift_total = total_ref[0:1], total_ref[1:2]
     first = group_sum(gain * shift_total) * (1.0 / ENTRIES)
     second = group_sum(gain * gain_total) * (1.0 / ENTRIES)
     normed = (xt_ref[...].astype(F32) - mean) * rstd
-    pre = normed * gain + shift
-    sig = 1.0 / (1.0 + jnp.exp(-pre))
-    pre_grad = pre_ref[...] + more_scr[...] * (sig * (1.0 + pre * (1.0 - sig)))
+    pre_grad = pre_ref[...] + more_scr[...] * slope_ref[...]
     out = rstd * (pre_grad * gain - first - normed * second)
     out_ref[0] = out.T.astype(BF16)
     gain_sum_ref[...] = gain_total * SCALE
@@ -366,23 +375,17 @@
         out_ref[k * rows : (k + 1) * rows] = total
 
 
+def last_sum_kernel(in_ref, out_ref, sums_ref):
+    sum_kernel(8, N_FAR, in_ref, out_ref)
+    sums_ref[...] = out_ref[18:20]
+
+
 def add_kernel(mark_ref, own_ref, both_ref, out_ref):
     second = mark_ref[CORE : CORE + 1] > 0.5
     out_ref[...] = own_ref[...] + jnp.where(second, both_ref[0], both_ref[1])
 
 
-def summed(x, parts, copies):
-    rows = x.size // C
-    return pl.pallas_call(
-        functools.partial(sum_kernel, parts, copies),
-        out_shape=shape((rows // parts * copies, C), F32),
-        in_specs=[VMEM],
-        out_specs=VMEM,
-        compiler_params=PARAMS,
-    )(x.reshape(rows, C))
-
-
-def sum_and_pair_kernel(parts, copies, in_ref, own_ref, other_ref, out_ref, pair_ref):
+def sum_and_pair_kernel(parts, copies, in_ref, own_ref, other_ref, _, out_ref, pair_ref):
     pair_ref[0] = own_ref[S : 2 * S]
     pair_ref[1] = other_ref[S : 2 * S]
     sum_kernel(parts, copies, in_ref, out_ref)
@@ -403,19 +406,12 @@
     info = jnp.concatenate([place, seam_code[0], corner_map[0], core])
     weight = conv_weight.transpose(1, 0, 2)
     gain, shift = norm_gain.reshape(1, C), norm_shift.reshape(1, C)
-    xt, ct, edges, stats = pl.pallas_call(
+    edges, stats = pl.pallas_call(
         start_kernel,
-        out_shape=(
-            shape((CELLS, C), BF16),
-            shape((CELLS, C), BF16),
-            shape((2, EDGE, C), BF16),
-            shape((N_FAR, 1, C), F32),
-        ),
+        out_shape=(shape((2, EDGE, C), BF16), shape((N_FAR, 1, C), F32)),
         in_specs=[pl.BlockSpec(memory_space=pltpu.HBM)] * 2,
-        out_specs=(VMEM,) * 4,
-        scratch_shapes=[pltpu.VMEM((C, CELLS), BF16)] * 2
-        + [pltpu.VMEM((CELLS, C), F32)] * 2
-        + [pltpu.SemaphoreType.DMA((2, 4))],
+        out_specs=(VMEM,) * 2,
+        scratch_shapes=[pltpu.VMEM((C, CELLS), BF16)] * 2 + [pltpu.SemaphoreType.DMA((2, 4))],
         compiler_params=pltpu.CompilerParams(vmem_limit_bytes=START_VMEM),
     )(features, cotangent)
     came = lax.ppermute(edges, "z2", [(0, 1), (1, 0)])
@@ -452,16 +448,16 @@
         [(4 * t + s, 4 * ((t + STEPS[s]) % 128) + (s + 2) % 4) for t in range(128) for s in range(4)],
     )
     stats = lax.all_to_all(stats, NEAR, 0, 0, tiled=True)
-    act_grad = pl.pallas_call(
+    act_grad, xt = pl.pallas_call(
         grad_kernel,
-        out_shape=shape((CELLS, C), F32),
-        in_specs=[VMEM] * 3,
-        out_specs=VMEM,
+        out_shape=(shape((CELLS, C), F32), shape((CELLS, C), BF16)),
+        in_specs=[VMEM] * 4,
+        out_specs=(VMEM,) * 2,
         compiler_params=PARAMS,
         cost_estimate=pl.CostEstimate(
             flops=18 * CELLS * C * C, bytes_accessed=10 * CELLS * C, transcendentals=0
         ),
-    )(ct, rows, weight)
+    )(features, cotangent, rows, weight)
     parts, send, pre_grad, norm = pl.pallas_call(
         main_kernel,
         out_shape=(
@@ -475,6 +471,13 @@
         scratch_shapes=[pltpu.VMEM((9, C, C), F32)],
         compiler_params=PARAMS,
     )(marks, xt, cotangent, rows, stats, affine, act_grad, strips, message)
+    slope = pl.pallas_call(
+        slope_kernel,
+        out_shape=shape((CELLS, C), F32),
+        in_specs=[VMEM] * 3,
+        out_specs=VMEM,
+        compiler_params=PARAMS,
+    )(xt, norm, affine)
     other = lax.ppermute(message, "z1", [(0, 1), (1, 0)])
     both = lax.all_gather(send, "co", axis=0, tiled=False)
     parts = pl.pallas_call(
@@ -487,12 +490,18 @@
     parts, pair = pl.pallas_call(
         functools.partial(sum_and_pair_kernel, N_FAR, 8),
         out_shape=(shape((8 * CHUNK, C), F32), shape((2, S, C), BF16)),
-        in_specs=[VMEM] * 3,
+        in_specs=[VMEM] * 4,
         out_specs=(VMEM,) * 2,
         compiler_params=PARAMS,
-    )(exchanged(parts, FAR, N_FAR).reshape(N_FAR * CHUNK, C), message, other)
-    others = lax.ppermute(pair, "z2", [(0, 1), (1, 0)])
-    parts = summed(exchanged(parts, ("zh", "z2", "z1"), 8), 8, N_FAR)
+    )(exchanged(parts, FAR, N_FAR).reshape(N_FAR * CHUNK, C), message, other, slope)
+    sides = lax.all_gather(pair, "z2", axis=0, tiled=False)
+    parts, sums = pl.pallas_call(
+        last_sum_kernel,
+        out_shape=(shape((N_FAR * CHUNK, C), F32), shape((2, C), F32)),
+        in_specs=[VMEM],
+        out_specs=(VMEM,) * 2,
+        compiler_params=PARAMS,
+    )(exchanged(parts, ("zh", "z2", "z1"), 8).reshape(8 * CHUNK, C))
     half = exchanged(parts, FAR, N_FAR)
     whole = lax.all_gather(half, "co", axis=0, tiled=True)
     grad_input, grad_gain, grad_shift = pl.pallas_call(
@@ -502,7 +511,7 @@
         out_specs=(VMEM,) * 3,
         scratch_shapes=[pltpu.VMEM((4, S, C), BF16), pltpu.VMEM((CELLS, C), F32)],
         compiler_params=PARAMS,
-    )(info, pre_grad, xt, norm, affine, parts, pair, others)
+    )(info, pre_grad, xt, norm, affine, sums, sides, slope)
     grad_weight = pl.pallas_call(
         weight_kernel,
         out_shape=shape((9, C, C), F32),

time: 107 us -> 107 us (level)
  blocking collectives: 23.9 us -> 28.6 us
  waiting for transfers between devices: 25.9 us -> 23.5 us
  starting transfers between devices: 45.3 us -> 43.3 us
    all_gather x0 -> x1, blocking collectives: none -> 4.67 us  [body(): sides = lax.all_gather(pair, 'z2', axis=0, tiled=False)]
    ppermute x1 -> x0, waiting for transfers between devices: 3.87 us -> none  [body(): others = lax.ppermute(pair, 'z2', [(0, 1), (1, 0)])]
    ppermute x1 -> x0, starting transfers between devices: 2.01 us -> none  [body(): others = lax.ppermute(pair, 'z2', [(0, 1), (1, 0)])]
    all_to_all x2, waiting for transfers between devices: 10.5 us -> 12.3 us  [exchanged(): return lax.all_to_all(x, axes, 0, 0, tiled=True)]
    pallas_call x3 -> x4, Pallas kernels: 4.1 us -> 4.25 us  [the longest x1 2.38 us: body(): pl.pallas_call(start_kernel, out_shape=(shape((2, EDGE, C), BF16), shape(...]
  transfers between devices with their start and end apart: 8 -> 7, of which waited for: 6 -> 5; matrix products, arithmetic and copies ran while one was open for 0% -> 0% of each run, Pallas kernels for 3% -> 3%
where the time goes in v5:
time: 107 us
  starting transfers between devices  43.3 us (40%)
  blocking collectives  28.6 us (27%)
  waiting for transfers between devices  23.5 us (22%)
  Pallas kernels  10.4 us (10%)
    all_to_all x2, waiting for transfers between devices, exchanged(): return lax.all_to_all(x, axes, 0, 0, tiled=True)  12.3 us
    all_to_all x1, starting transfers between devices, body(): stats = lax.all_to_all(stats, NEAR, 0, 0, tiled=True)  10.8 us
    all_to_all x2, starting transfers between devices, exchanged(): return lax.all_to_all(x, axes, 0, 0, tiled=True)  10.3 us
    all_to_all x1, blocking collectives, exchanged(): return lax.all_to_all(x, axes, 0, 0, tiled=True)  9.78 us
    all_to_all x1, starting transfers between devices, body(): stats = lax.all_to_all(stats, FAR, 0, 0, tiled=True)  9.68 us
    ppermute x1, starting transfers between devices, body(): came = lax.ppermute(edges, 'z2', [(0, 1), (1, 0)])  6.77 us
    all_gather x1, blocking collectives, body(): whole = lax.all_gather(half, 'co', axis=0, tiled=True)  6.52 us
    all_to_all x1, waiting for transfers between devices, body(): stats = lax.all_to_all(stats, NEAR, 0, 0, tiled=True)  6.03 us
  transfers between devices with their start and end apart: 7, of which 5 were waited for; matrix products, arithmetic and copies ran while one was open for 0% of the time, Pallas kernels for 3%

profile of v5, /device:TPU:1, one launch (start us, length us, event | category | flops | bytes accessed | tf_op | source)
XLA Modules:
  0.0 106.7 jit_solution(9941027686669975613)
XLA Ops:
  0.7 2.4 %shard_map.102 = (bf16[2,160,128]{2,1,0:T(8,128)(2,1)S(1)}, f32[32,1,128]{2,1,0:T(1,128)}) custom-call(bf16[1,128,1024]{2,1,0:T(8,128)(2,1)} %x_ref.1, bf16[1,128,1024]{2,1,0:T(8,128)(2,1)} %cot_ref.1), custom_call_target="tpu_custom_call" | custom-call | tf_op jit(solution)/shard_map/pallas_call | solution.py:409
  3.1 6.8 %collective-permute-start = (bf16[2,160,128]{2,1,0:T(8,128)(2,1)S(1)}, bf16[2,160,128]{2,1,0:T(8,128)(2,1)S(1)}, u32[]{:S(2)}, u32[]{:S(2)}) collective-permute-start(bf16[2,160,128]{2,1,0:T(8,128)(2,1)S(1)} %get-tuple-element.27.own_ref), channel_id=1, source_target_pairs={{0,2},{2,0},{1,3},{3,1},{4,6},{6,4},{5,7},{7,5},{8,10},{10,8},{9,1... | collective-permute-start | bytes 245768 | tf_op jit(solution)/shard_map/ppermute | solution.py:417
  9.9 9.7 %all-to-all-start = ((f32[32,1,128]{2,1,0:T(1,128)}), f32[32,1,128]{2,1,0:T(1,128)S(1)}, u32[]{:S(2)}, u32[]{:S(2)}) async-start(f32[32,1,128]{2,1,0:T(1,128)} %get-tuple-element.31), calls=%async_computation | async-start | bytes 32768 | tf_op jit(solution)/shard_map/all_to_all | solution.py:418
  20.3 5.0 %all-gather = bf16[6,128,128]{2,1,0:T(8,128)(2,1)S(1)} all-gather(bf16[3,128,128]{2,1,0:T(8,128)(2,1)S(1)} %get-tuple-element.30), channel_id=2, replica_groups=mesh['y'=8,'x'=4,'zh'=2,'co'=2,'z2'=2,'z1'=2] {'z1'}, dimensions={0}, use_global_device_ids=true | all-gather | bytes 294912 | tf_op jit(solution)/shard_map/all_gather | solution.py:432
  25.3 2.7 %all-to-all-done.in_stat_ref = f32[32,1,128]{2,1,0:T(1,128)S(1)} async-done(((f32[32,1,128]{2,1,0:T(1,128)}), f32[32,1,128]{2,1,0:T(1,128)S(1)}, u32[]{:S(2)}, u32[]{:S(2)}) %all-to-all-start) | async-done | bytes 16416 | tf_op jit(solution)/shard_map/all_to_all | solution.py:418
  28.1 0.8 shard_map.104
  28.9 3.6 %collective-permute-start.1 = (bf16[128,128]{1,0:T(8,128)(2,1)S(1)}, bf16[128,128]{1,0:T(8,128)(2,1)S(1)}, u32[]{:S(2)}, u32[]{:S(2)}) collective-permute-start(bf16[128,128]{1,0:T(8,128)(2,1)S(1)} %get-tuple-element.38), channel_id=1, source_target_pairs={{0,498},{1,7},{2,16},{3,509},{4,502},{5,11},{6,20},{7,1},{8,506},{... | collective-permute-start | bytes 98312 | tf_op jit(solution)/shard_map/ppermute | solution.py:445
  32.5 10.8 %all-to-all-start.1 = ((f32[16,1,128]{2,1,0:T(1,128)}), f32[16,1,128]{2,1,0:T(1,128)S(1)}, u32[]{:S(2)}, u32[]{:S(2)}) async-start(f32[16,1,128]{2,1,0:T(1,128)} %get-tuple-element.34), calls=%async_computation.1 | async-start | bytes 16384 | tf_op jit(solution)/shard_map/all_to_all | solution.py:450
  43.3 0.9 shard_map.105
  44.2 6.0 %all-to-all-done.1.in_stat_ref = f32[16,1,128]{2,1,0:T(1,128)S(1)} async-done(((f32[16,1,128]{2,1,0:T(1,128)}), f32[16,1,128]{2,1,0:T(1,128)S(1)}, u32[]{:S(2)}, u32[]{:S(2)}) %all-to-all-start.1) | async-done | bytes 8224 | tf_op jit(solution)/shard_map/all_to_all | solution.py:450
  50.2 1.3 %shard_map.106 = (f32[640,128]{1,0:T(8,128)S(1)}, f32[640,128]{1,0:T(8,128)S(1)}, f32[1024,128]{1,0:T(8,128)S(1)}, f32[2,128]{1,0:T(2,128)S(1)}) custom-call(f32[16,128]{1,0:T(8,128)S(1)} %get-tuple-element.28.mark_ref, bf16[1024,128]{1,0:T(8,128)(2,1)S(1)} %get-tuple-element.33.xt_ref, bf16[1,128,1024]{2,1,0:T(8,128)(2,1)S(1)} %copy-done, ...), custom_call_target="tpu_custom_call" | custom-call | tf_op jit(solution)/shard_map/pallas_call | solution.py:461
  51.5 2.6 %all-gather.1 = f32[1280,128]{1,0:T(8,128)S(1)} all-gather(f32[640,128]{1,0:T(8,128)S(1)} %get-tuple-element.42), channel_id=3, replica_groups=mesh['y'=8,'x'=4,'zh'=2,'co'=2,'z2'=2,'z1'=2] {'co'}, dimensions={0}, use_global_device_ids=true | all-gather | bytes 983040 | tf_op jit(solution)/shard_map/all_gather | solution.py:482
  54.1 0.8 shard_map.107
  54.8 5.5 %all-to-all-start.2 = ((f32[32,5,4,128]{3,2,1,0:T(4,128)}), f32[32,5,4,128]{3,2,1,0:T(4,128)S(1)}, u32[]{:S(2)}, u32[]{:S(2)}) async-start(f32[32,5,4,128]{3,2,1,0:T(4,128)} %bitcast.9), calls=%async_computation.2 | async-start | bytes 655360 | tf_op jit(solution)/shard_map/all_to_all | solution.py:396
  60.3 2.2 %collective-permute-start.2 = (bf16[128,128]{1,0:T(8,128)(2,1)S(1)}, bf16[128,128]{1,0:T(8,128)(2,1)S(1)}, u32[]{:S(2)}, u32[]{:S(2)}) collective-permute-start(bf16[128,128]{1,0:T(8,128)(2,1)S(1)} %collective-permute-done.1.in_ref.own_ref), channel_id=1, source_target_pairs={{0,1},{1,0},{2,3},{3,2},{4,5},{5,4},{6,7},{7,6},{8,9},{9,8},{10,11... | collective-permute-start | bytes 98312 | tf_op jit(solution)/shard_map/ppermute | solution.py:481
  62.8 2.5 %collective-permute-done.2.other_ref = bf16[128,128]{1,0:T(8,128)(2,1)S(1)} collective-permute-done((bf16[128,128]{1,0:T(8,128)(2,1)S(1)}, bf16[128,128]{1,0:T(8,128)(2,1)S(1)}, u32[]{:S(2)}, u32[]{:S(2)}) %collective-permute-start.2) | collective-permute-done | bytes 32800 | tf_op jit(solution)/shard_map/ppermute | solution.py:481
  65.3 7.8 %all-to-all-done.2 = f32[32,5,4,128]{3,2,1,0:T(4,128)S(1)} async-done(((f32[32,5,4,128]{3,2,1,0:T(4,128)}), f32[32,5,4,128]{3,2,1,0:T(4,128)S(1)}, u32[]{:S(2)}, u32[]{:S(2)}) %all-to-all-start.2) | async-done | bytes 327712 | tf_op jit(solution)/shard_map/all_to_all | solution.py:396
  73.1 9.8 %all_to_all.25 = f32[8,5,4,128]{3,2,1,0:T(4,128)S(1)} all-to-all(f32[8,5,4,128]{3,2,1,0:T(4,128)S(1)} %bitcast.27), channel_id=1, replica_groups=mesh['y'=8,'x'=4,'zh'=2,'co'=2,'z2'=2,'z1'=2] {'zh','z2','z1'}, dimensions={0} | all-to-all | bytes 163840 | tf_op jit(solution)/shard_map/all_to_all | solution.py:396
  83.7 4.8 %all-to-all-start.4 = ((f32[32,5,4,128]{3,2,1,0:T(4,128)}), f32[32,5,4,128]{3,2,1,0:T(4,128)S(1)}, u32[]{:S(2)}, u32[]{:S(2)}) async-start(f32[32,5,4,128]{3,2,1,0:T(4,128)} %bitcast.14), calls=%async_computation.4 | async-start | bytes 655360 | tf_op jit(solution)/shard_map/all_to_all | solution.py:396
  88.5 4.7 %all-gather.2 = bf16[4,64,128]{2,1,0:T(8,128)(2,1)S(1)} all-gather(bf16[2,64,128]{2,1,0:T(8,128)(2,1)S(1)} %get-tuple-element.45), channel_id=4, replica_groups=mesh['y'=8,'x'=4,'zh'=2,'co'=2,'z2'=2,'z1'=2] {'z2'}, dimensions={0}, use_global_device_ids=true | all-gather | bytes 98304 | tf_op jit(solution)/shard_map/all_gather | solution.py:497
  93.1 1.7 %shard_map.111 = (bf16[1,128,1024]{2,1,0:T(8,128)(2,1)}, f32[1,128]{1,0:T(1,128)}, f32[1,128]{1,0:T(1,128)}) custom-call(s32[10]{0:T(128)S(1)} %pad_add_fusion.info_ref, f32[1024,128]{1,0:T(8,128)S(1)} %get-tuple-element.39.pre_ref, bf16[1024,128]{1,0:T(8,128)(2,1)S(1)} %get-tuple-element.33.xt_ref, f32[2,128]{1,0:T(2,128)S(1)} %get-tuple-element.40.norm_ref, ...), custom_call_target="tpu_custom_call" | custom-call | tf_op jit(solution)/shard_map/pallas_call | solution.py:507
  94.8 4.5 %all-to-all-done.4 = f32[32,5,4,128]{3,2,1,0:T(4,128)S(1)} async-done(((f32[32,5,4,128]{3,2,1,0:T(4,128)}), f32[32,5,4,128]{3,2,1,0:T(4,128)S(1)}, u32[]{:S(2)}, u32[]{:S(2)}) %all-to-all-start.4) | async-done | bytes 327712 | tf_op jit(solution)/shard_map/all_to_all | solution.py:396
  99.3 6.5 %all_gather.27 = f32[64,5,4,128]{3,2,1,0:T(4,128)S(1)} all-gather(f32[32,5,4,128]{3,2,1,0:T(4,128)S(1)} %all-to-all-done.4), channel_id=1, replica_groups=mesh['y'=8,'x'=4,'zh'=2,'co'=2,'z2'=2,'z1'=2] {'co'}, dimensions={0}, use_global_device_ids=true | all-gather | bytes 983040 | tf_op jit(solution)/shard_map/all_gather | solution.py:506
  105.8 0.9 shard_map.112
  (21 shorter events, 1.8 us)
Async XLA Ops:
  0.6 18.9 %copy-start.5 = (s32[1,4]{1,0:T(1,128)S(1)}, s32[1,4]{1,0:T(1,128)}, u32[]{:S(2)}) copy-start(s32[1,4]{1,0:T(1,128)} %param.13) | copy-start | bytes 52
  0.6 18.9 %copy-start.6 = (s32[1,4]{1,0:T(1,128)S(1)}, s32[1,4]{1,0:T(1,128)}, u32[]{:S(2)}) copy-start(s32[1,4]{1,0:T(1,128)} %param.12) | copy-start | bytes 52
  0.7 19.0 %copy-start.3 = (f32[128]{0:T(128)S(1)}, f32[128]{0:T(128)}, u32[]{:S(2)}) copy-start(f32[128]{0:T(128)} %param.10) | copy-start | bytes 1540
  0.7 19.0 %copy-start.4 = (f32[128]{0:T(128)S(1)}, f32[128]{0:T(128)}, u32[]{:S(2)}) copy-start(f32[128]{0:T(128)} %param.11) | copy-start | bytes 1540
  3.1 25.0 %copy-start.1 = (bf16[128,9,128]{2,0,1:T(8,128)(2,1)S(1)}, bf16[128,9,128]{2,0,1:T(8,128)(2,1)}, u32[]{:S(2)}) copy-start(bf16[128,9,128]{2,0,1:T(8,128)(2,1)} %param.9) | copy-start | bytes 884740
  3.1 16.6 %collective-permute-start = (bf16[2,160,128]{2,1,0:T(8,128)(2,1)S(1)}, bf16[2,160,128]{2,1,0:T(8,128)(2,1)S(1)}, u32[]{:S(2)}, u32[]{:S(2)}) collective-permute-start(bf16[2,160,128]{2,1,0:T(8,128)(2,1)S(1)} %get-tuple-element.27.own_ref), channel_id=1, source_target_pairs={{0,2},{2,0},{1,3},{3,1},{4,6},{6,4},{5,7},{7,5},{8,10},{10,8},{9,1... | collective-permute-start | bytes 245768 | tf_op jit(solution)/shard_map/ppermute | solution.py:417
  9.9 18.2 %all-to-all-start = ((f32[32,1,128]{2,1,0:T(1,128)}), f32[32,1,128]{2,1,0:T(1,128)S(1)}, u32[]{:S(2)}, u32[]{:S(2)}) async-start(f32[32,1,128]{2,1,0:T(1,128)} %get-tuple-element.31), calls=%async_computation | async-start | bytes 32768 | tf_op jit(solution)/shard_map/all_to_all | solution.py:418
  28.1 15.2 %copy-start = (bf16[1,128,1024]{2,1,0:T(8,128)(2,1)S(1)}, bf16[1,128,1024]{2,1,0:T(8,128)(2,1)}, u32[]{:S(2)}) copy-start(bf16[1,128,1024]{2,1,0:T(8,128)(2,1)} %cot_ref.1) | copy-start | bytes 786436
  28.1 15.2 %copy-start.2 = (bf16[1,128,1024]{2,1,0:T(8,128)(2,1)S(1)}, bf16[1,128,1024]{2,1,0:T(8,128)(2,1)}, u32[]{:S(2)}) copy-start(bf16[1,128,1024]{2,1,0:T(8,128)(2,1)} %x_ref.1) | copy-start | bytes 786436
  28.9 21.3 %collective-permute-start.1 = (bf16[128,128]{1,0:T(8,128)(2,1)S(1)}, bf16[128,128]{1,0:T(8,128)(2,1)S(1)}, u32[]{:S(2)}, u32[]{:S(2)}) collective-permute-start(bf16[128,128]{1,0:T(8,128)(2,1)S(1)} %get-tuple-element.38), channel_id=1, source_target_pairs={{0,498},{1,7},{2,16},{3,509},{4,502},{5,11},{6,20},{7,1},{8,506},{... | collective-permute-start | bytes 98312 | tf_op jit(solution)/shard_map/ppermute | solution.py:445
  32.5 17.7 %all-to-all-start.1 = ((f32[16,1,128]{2,1,0:T(1,128)}), f32[16,1,128]{2,1,0:T(1,128)S(1)}, u32[]{:S(2)}, u32[]{:S(2)}) async-start(f32[16,1,128]{2,1,0:T(1,128)} %get-tuple-element.34), calls=%async_computation.1 | async-start | bytes 16384 | tf_op jit(solution)/shard_map/all_to_all | solution.py:450
  54.8 18.2 %all-to-all-start.2 = ((f32[32,5,4,128]{3,2,1,0:T(4,128)}), f32[32,5,4,128]{3,2,1,0:T(4,128)S(1)}, u32[]{:S(2)}, u32[]{:S(2)}) async-start(f32[32,5,4,128]{3,2,1,0:T(4,128)} %bitcast.9), calls=%async_computation.2 | async-start | bytes 655360 | tf_op jit(solution)/shard_map/all_to_all | solution.py:396
  60.3 5.0 %collective-permute-start.2 = (bf16[128,128]{1,0:T(8,128)(2,1)S(1)}, bf16[128,128]{1,0:T(8,128)(2,1)S(1)}, u32[]{:S(2)}, u32[]{:S(2)}) collective-permute-start(bf16[128,128]{1,0:T(8,128)(2,1)S(1)} %collective-permute-done.1.in_ref.own_ref), channel_id=1, source_target_pairs={{0,1},{1,0},{2,3},{3,2},{4,5},{5,4},{6,7},{7,6},{8,9},{9,8},{10,11... | collective-permute-start | bytes 98312 | tf_op jit(solution)/shard_map/ppermute | solution.py:481
  83.7 15.6 %all-to-all-start.4 = ((f32[32,5,4,128]{3,2,1,0:T(4,128)}), f32[32,5,4,128]{3,2,1,0:T(4,128)S(1)}, u32[]{:S(2)}, u32[]{:S(2)}) async-start(f32[32,5,4,128]{3,2,1,0:T(4,128)} %bitcast.14), calls=%async_computation.4 | async-start | bytes 655360 | tf_op jit(solution)/shard_map/all_to_all | solution.py:396

commit v6 on v5

--- a/solution.py
+++ b/solution.py
@@ -20,6 +20,7 @@
 LINE = 2 * S
 EDGE = 2 * S + 2 * ROWS
 CHUNK = 20
+TAPPED = 18
 
 TILE = ("y", "x", "zh", "co")
 AXES = {"y": 8, "x": 4, "zh": 2, "co": 2, "z2": 2, "z1": 2}
@@ -362,7 +363,7 @@
     for tap in range(9):
         for h in range(2):
             out_ref[tap, h * 64 : (h + 1) * 64] = (
-                whole_ref[pl.ds(h * 9 + tap, 64, stride=CHUNK), :] * SCALE
+                whole_ref[pl.ds(h * 9 + tap, 64, stride=TAPPED), :] * SCALE
             )
 
 
@@ -376,8 +377,12 @@
 
 
 def last_sum_kernel(in_ref, out_ref, sums_ref):
-    sum_kernel(8, N_FAR, in_ref, out_ref)
-    sums_ref[...] = out_ref[18:20]
+    total = in_ref[0:CHUNK]
+    for k in range(1, 8):
+        total = total + in_ref[k * CHUNK : (k + 1) * CHUNK]
+    for k in range(N_FAR):
+        out_ref[k * TAPPED : (k + 1) * TAPPED] = total[0:TAPPED]
+    sums_ref[...] = total[TAPPED:CHUNK]
 
 
 def add_kernel(mark_ref, own_ref, both_ref, out_ref):
@@ -497,12 +502,12 @@
     sides = lax.all_gather(pair, "z2", axis=0, tiled=False)
     parts, sums = pl.pallas_call(
         last_sum_kernel,
-        out_shape=(shape((N_FAR * CHUNK, C), F32), shape((2, C), F32)),
+        out_shape=(shape((N_FAR * TAPPED, C), F32), shape((2, C), F32)),
         in_specs=[VMEM],
         out_specs=(VMEM,) * 2,
         compiler_params=PARAMS,
     )(exchanged(parts, ("zh", "z2", "z1"), 8).reshape(8 * CHUNK, C))
-    half = exchanged(parts, FAR, N_FAR)
+    half = lax.all_to_all(parts.reshape(N_FAR, TAPPED // 2, 2, C), FAR, 0, 0, tiled=True)
     whole = lax.all_gather(half, "co", axis=0, tiled=True)
     grad_input, grad_gain, grad_shift = pl.pallas_call(
         end_kernel,
@@ -518,7 +523,7 @@
         in_specs=[VMEM],
         out_specs=VMEM,
         compiler_params=PARAMS,
-    )(whole.reshape(64 * CHUNK, C)).transpose(1, 0, 2)
+    )(whole.reshape(64 * TAPPED, C)).transpose(1, 0, 2)
     return grad_input, grad_weight, grad_gain.reshape(C), grad_shift.reshape(C)
 
 

time: 107 us -> 106 us (level)
    all_to_all x2 -> x1, starting transfers between devices: 10.3 us -> 5.48 us  [exchanged(): return lax.all_to_all(x, axes, 0, 0, tiled=True)]
    all_to_all x0 -> x1, starting transfers between devices: none -> 4.78 us  [body(): lax.all_to_all(parts.reshape(N_FAR, TAPPED // 2, 2, C), FAR, 0, 0, tiled=...]
    all_to_all x2 -> x1, waiting for transfers between devices: 12.3 us -> 7.8 us  [exchanged(): return lax.all_to_all(x, axes, 0, 0, tiled=True)]
    all_to_all x0 -> x1, waiting for transfers between devices: none -> 4.39 us  [body(): lax.all_to_all(parts.reshape(N_FAR, TAPPED // 2, 2, C), FAR, 0, 0, tiled=...]
where the time goes in v6:
time: 106 us
  starting transfers between devices  43.3 us (41%)
  blocking collectives  27.9 us (26%)
  waiting for transfers between devices  23.4 us (22%)
  Pallas kernels  10.3 us (10%)
    all_to_all x1, starting transfers between devices, body(): stats = lax.all_to_all(stats, NEAR, 0, 0, tiled=True)  10.8 us
    all_to_all x1, blocking collectives, exchanged(): return lax.all_to_all(x, axes, 0, 0, tiled=True)  9.78 us
    all_to_all x1, starting transfers between devices, body(): stats = lax.all_to_all(stats, FAR, 0, 0, tiled=True)  9.68 us
    all_to_all x1, waiting for transfers between devices, exchanged(): return lax.all_to_all(x, axes, 0, 0, tiled=True)  7.8 us
    ppermute x1, starting transfers between devices, body(): came = lax.ppermute(edges, 'z2', [(0, 1), (1, 0)])  6.77 us
    all_to_all x1, waiting for transfers between devices, body(): stats = lax.all_to_all(stats, NEAR, 0, 0, tiled=True)  6.03 us
    all_gather x1, blocking collectives, body(): whole = lax.all_gather(half, 'co', axis=0, tiled=True)  5.78 us
    all_to_all x1, starting transfers between devices, exchanged(): return lax.all_to_all(x, axes, 0, 0, tiled=True)  5.48 us
  transfers between devices with their start and end apart: 7, of which 5 were waited for; matrix products, arithmetic and copies ran while one was open for 0% of the time, Pallas kernels for 3%

profile of v6, /device:TPU:1, one launch (start us, length us, event | category | flops | bytes accessed | tf_op | source)
XLA Modules:
  0.0 105.8 jit_solution(13886794142463694134)
XLA Ops:
  0.7 2.4 %shard_map.102 = (bf16[2,160,128]{2,1,0:T(8,128)(2,1)S(1)}, f32[32,1,128]{2,1,0:T(1,128)}) custom-call(bf16[1,128,1024]{2,1,0:T(8,128)(2,1)} %x_ref.1, bf16[1,128,1024]{2,1,0:T(8,128)(2,1)} %cot_ref.1), custom_call_target="tpu_custom_call" | custom-call | tf_op jit(solution)/shard_map/pallas_call | solution.py:414
  3.1 6.8 %collective-permute-start = (bf16[2,160,128]{2,1,0:T(8,128)(2,1)S(1)}, bf16[2,160,128]{2,1,0:T(8,128)(2,1)S(1)}, u32[]{:S(2)}, u32[]{:S(2)}) collective-permute-start(bf16[2,160,128]{2,1,0:T(8,128)(2,1)S(1)} %get-tuple-element.27.own_ref), channel_id=1, source_target_pairs={{0,2},{2,0},{1,3},{3,1},{4,6},{6,4},{5,7},{7,5},{8,10},{10,8},{9,1... | collective-permute-start | bytes 245768 | tf_op jit(solution)/shard_map/ppermute | solution.py:422
  9.9 9.7 %all-to-all-start = ((f32[32,1,128]{2,1,0:T(1,128)}), f32[32,1,128]{2,1,0:T(1,128)S(1)}, u32[]{:S(2)}, u32[]{:S(2)}) async-start(f32[32,1,128]{2,1,0:T(1,128)} %get-tuple-element.31), calls=%async_computation | async-start | bytes 32768 | tf_op jit(solution)/shard_map/all_to_all | solution.py:423
  20.3 5.0 %all-gather = bf16[6,128,128]{2,1,0:T(8,128)(2,1)S(1)} all-gather(bf16[3,128,128]{2,1,0:T(8,128)(2,1)S(1)} %get-tuple-element.30), channel_id=2, replica_groups=mesh['y'=8,'x'=4,'zh'=2,'co'=2,'z2'=2,'z1'=2] {'z1'}, dimensions={0}, use_global_device_ids=true | all-gather | bytes 294912 | tf_op jit(solution)/shard_map/all_gather | solution.py:437
  25.3 2.7 %all-to-all-done.in_stat_ref = f32[32,1,128]{2,1,0:T(1,128)S(1)} async-done(((f32[32,1,128]{2,1,0:T(1,128)}), f32[32,1,128]{2,1,0:T(1,128)S(1)}, u32[]{:S(2)}, u32[]{:S(2)}) %all-to-all-start) | async-done | bytes 16416 | tf_op jit(solution)/shard_map/all_to_all | solution.py:423
  28.1 0.8 shard_map.104
  28.9 3.6 %collective-permute-start.1 = (bf16[128,128]{1,0:T(8,128)(2,1)S(1)}, bf16[128,128]{1,0:T(8,128)(2,1)S(1)}, u32[]{:S(2)}, u32[]{:S(2)}) collective-permute-start(bf16[128,128]{1,0:T(8,128)(2,1)S(1)} %get-tuple-element.38), channel_id=1, source_target_pairs={{0,498},{1,7},{2,16},{3,509},{4,502},{5,11},{6,20},{7,1},{8,506},{... | collective-permute-start | bytes 98312 | tf_op jit(solution)/shard_map/ppermute | solution.py:450
  32.5 10.8 %all-to-all-start.1 = ((f32[16,1,128]{2,1,0:T(1,128)}), f32[16,1,128]{2,1,0:T(1,128)S(1)}, u32[]{:S(2)}, u32[]{:S(2)}) async-start(f32[16,1,128]{2,1,0:T(1,128)} %get-tuple-element.34), calls=%async_computation.1 | async-start | bytes 16384 | tf_op jit(solution)/shard_map/all_to_all | solution.py:455
  43.3 0.9 shard_map.105
  44.2 6.0 %all-to-all-done.1.in_stat_ref = f32[16,1,128]{2,1,0:T(1,128)S(1)} async-done(((f32[16,1,128]{2,1,0:T(1,128)}), f32[16,1,128]{2,1,0:T(1,128)S(1)}, u32[]{:S(2)}, u32[]{:S(2)}) %all-to-all-start.1) | async-done | bytes 8224 | tf_op jit(solution)/shard_map/all_to_all | solution.py:455
  50.2 1.3 %shard_map.106 = (f32[640,128]{1,0:T(8,128)S(1)}, f32[640,128]{1,0:T(8,128)S(1)}, f32[1024,128]{1,0:T(8,128)S(1)}, f32[2,128]{1,0:T(2,128)S(1)}) custom-call(f32[16,128]{1,0:T(8,128)S(1)} %get-tuple-element.28.mark_ref, bf16[1024,128]{1,0:T(8,128)(2,1)S(1)} %get-tuple-element.33.xt_ref, bf16[1,128,1024]{2,1,0:T(8,128)(2,1)S(1)} %copy-done, ...), custom_call_target="tpu_custom_call" | custom-call | tf_op jit(solution)/shard_map/pallas_call | solution.py:466
  51.5 2.6 %all-gather.1 = f32[1280,128]{1,0:T(8,128)S(1)} all-gather(f32[640,128]{1,0:T(8,128)S(1)} %get-tuple-element.42), channel_id=3, replica_groups=mesh['y'=8,'x'=4,'zh'=2,'co'=2,'z2'=2,'z1'=2] {'co'}, dimensions={0}, use_global_device_ids=true | all-gather | bytes 983040 | tf_op jit(solution)/shard_map/all_gather | solution.py:487
  54.1 0.8 shard_map.107
  54.8 5.5 %all-to-all-start.2 = ((f32[32,5,4,128]{3,2,1,0:T(4,128)}), f32[32,5,4,128]{3,2,1,0:T(4,128)S(1)}, u32[]{:S(2)}, u32[]{:S(2)}) async-start(f32[32,5,4,128]{3,2,1,0:T(4,128)} %bitcast.9), calls=%async_computation.2 | async-start | bytes 655360 | tf_op jit(solution)/shard_map/all_to_all | solution.py:401
  60.3 2.2 %collective-permute-start.2 = (bf16[128,128]{1,0:T(8,128)(2,1)S(1)}, bf16[128,128]{1,0:T(8,128)(2,1)S(1)}, u32[]{:S(2)}, u32[]{:S(2)}) collective-permute-start(bf16[128,128]{1,0:T(8,128)(2,1)S(1)} %collective-permute-done.1.in_ref.own_ref), channel_id=1, source_target_pairs={{0,1},{1,0},{2,3},{3,2},{4,5},{5,4},{6,7},{7,6},{8,9},{9,8},{10,11... | collective-permute-start | bytes 98312 | tf_op jit(solution)/shard_map/ppermute | solution.py:486
  62.8 2.5 %collective-permute-done.2.other_ref = bf16[128,128]{1,0:T(8,128)(2,1)S(1)} collective-permute-done((bf16[128,128]{1,0:T(8,128)(2,1)S(1)}, bf16[128,128]{1,0:T(8,128)(2,1)S(1)}, u32[]{:S(2)}, u32[]{:S(2)}) %collective-permute-start.2) | collective-permute-done | bytes 32800 | tf_op jit(solution)/shard_map/ppermute | solution.py:486
  65.3 7.8 %all-to-all-done.2 = f32[32,5,4,128]{3,2,1,0:T(4,128)S(1)} async-done(((f32[32,5,4,128]{3,2,1,0:T(4,128)}), f32[32,5,4,128]{3,2,1,0:T(4,128)S(1)}, u32[]{:S(2)}, u32[]{:S(2)}) %all-to-all-start.2) | async-done | bytes 327712 | tf_op jit(solution)/shard_map/all_to_all | solution.py:401
  73.1 9.8 %all_to_all.25 = f32[8,5,4,128]{3,2,1,0:T(4,128)S(1)} all-to-all(f32[8,5,4,128]{3,2,1,0:T(4,128)S(1)} %bitcast.27), channel_id=1, replica_groups=mesh['y'=8,'x'=4,'zh'=2,'co'=2,'z2'=2,'z1'=2] {'zh','z2','z1'}, dimensions={0} | all-to-all | bytes 163840 | tf_op jit(solution)/shard_map/all_to_all | solution.py:401
  83.7 4.8 %all-to-all-start.4 = ((f32[32,9,2,128]{3,2,1,0:T(2,128)}), f32[32,9,2,128]{3,2,1,0:T(2,128)S(1)}, u32[]{:S(2)}, u32[]{:S(2)}) async-start(f32[32,9,2,128]{3,2,1,0:T(2,128)} %bitcast.14), calls=%async_computation.4 | async-start | bytes 589824 | tf_op jit(solution)/shard_map/all_to_all | solution.py:510
  88.5 4.7 %all-gather.2 = bf16[4,64,128]{2,1,0:T(8,128)(2,1)S(1)} all-gather(bf16[2,64,128]{2,1,0:T(8,128)(2,1)S(1)} %get-tuple-element.45), channel_id=4, replica_groups=mesh['y'=8,'x'=4,'zh'=2,'co'=2,'z2'=2,'z1'=2] {'z2'}, dimensions={0}, use_global_device_ids=true | all-gather | bytes 98304 | tf_op jit(solution)/shard_map/all_gather | solution.py:502
  93.1 1.7 %shard_map.111 = (bf16[1,128,1024]{2,1,0:T(8,128)(2,1)}, f32[1,128]{1,0:T(1,128)}, f32[1,128]{1,0:T(1,128)}) custom-call(s32[10]{0:T(128)S(1)} %pad_add_fusion.info_ref, f32[1024,128]{1,0:T(8,128)S(1)} %get-tuple-element.39.pre_ref, bf16[1024,128]{1,0:T(8,128)(2,1)S(1)} %get-tuple-element.33.xt_ref, f32[2,128]{1,0:T(2,128)S(1)} %get-tuple-element.40.norm_ref, ...), custom_call_target="tpu_custom_call" | custom-call | tf_op jit(solution)/shard_map/pallas_call | solution.py:512
  94.8 4.4 %all-to-all-done.4 = f32[32,9,2,128]{3,2,1,0:T(2,128)S(1)} async-done(((f32[32,9,2,128]{3,2,1,0:T(2,128)}), f32[32,9,2,128]{3,2,1,0:T(2,128)S(1)}, u32[]{:S(2)}, u32[]{:S(2)}) %all-to-all-start.4) | async-done | bytes 294944 | tf_op jit(solution)/shard_map/all_to_all | solution.py:510
  99.2 5.8 %all_gather.27 = f32[64,9,2,128]{3,2,1,0:T(2,128)S(1)} all-gather(f32[32,9,2,128]{3,2,1,0:T(2,128)S(1)} %all-to-all-done.4), channel_id=1, replica_groups=mesh['y'=8,'x'=4,'zh'=2,'co'=2,'z2'=2,'z1'=2] {'co'}, dimensions={0}, use_global_device_ids=true | all-gather | bytes 884736 | tf_op jit(solution)/shard_map/all_gather | solution.py:511
  105.0 0.9 shard_map.112
  (21 shorter events, 1.8 us)
Async XLA Ops:
  0.6 18.9 %copy-start.5 = (s32[1,4]{1,0:T(1,128)S(1)}, s32[1,4]{1,0:T(1,128)}, u32[]{:S(2)}) copy-start(s32[1,4]{1,0:T(1,128)} %param.13) | copy-start | bytes 52
  0.6 18.9 %copy-start.6 = (s32[1,4]{1,0:T(1,128)S(1)}, s32[1,4]{1,0:T(1,128)}, u32[]{:S(2)}) copy-start(s32[1,4]{1,0:T(1,128)} %param.12) | copy-start | bytes 52
  0.7 19.0 %copy-start.3 = (f32[128]{0:T(128)S(1)}, f32[128]{0:T(128)}, u32[]{:S(2)}) copy-start(f32[128]{0:T(128)} %param.10) | copy-start | bytes 1540
  0.7 19.0 %copy-start.4 = (f32[128]{0:T(128)S(1)}, f32[128]{0:T(128)}, u32[]{:S(2)}) copy-start(f32[128]{0:T(128)} %param.11) | copy-start | bytes 1540
  3.1 25.0 %copy-start.1 = (bf16[128,9,128]{2,0,1:T(8,128)(2,1)S(1)}, bf16[128,9,128]{2,0,1:T(8,128)(2,1)}, u32[]{:S(2)}) copy-start(bf16[128,9,128]{2,0,1:T(8,128)(2,1)} %param.9) | copy-start | bytes 884740
  3.1 16.6 %collective-permute-start = (bf16[2,160,128]{2,1,0:T(8,128)(2,1)S(1)}, bf16[2,160,128]{2,1,0:T(8,128)(2,1)S(1)}, u32[]{:S(2)}, u32[]{:S(2)}) collective-permute-start(bf16[2,160,128]{2,1,0:T(8,128)(2,1)S(1)} %get-tuple-element.27.own_ref), channel_id=1, source_target_pairs={{0,2},{2,0},{1,3},{3,1},{4,6},{6,4},{5,7},{7,5},{8,10},{10,8},{9,1... | collective-permute-start | bytes 245768 | tf_op jit(solution)/shard_map/ppermute | solution.py:422
  9.9 18.2 %all-to-all-start = ((f32[32,1,128]{2,1,0:T(1,128)}), f32[32,1,128]{2,1,0:T(1,128)S(1)}, u32[]{:S(2)}, u32[]{:S(2)}) async-start(f32[32,1,128]{2,1,0:T(1,128)} %get-tuple-element.31), calls=%async_computation | async-start | bytes 32768 | tf_op jit(solution)/shard_map/all_to_all | solution.py:423
  28.1 15.2 %copy-start = (bf16[1,128,1024]{2,1,0:T(8,128)(2,1)S(1)}, bf16[1,128,1024]{2,1,0:T(8,128)(2,1)}, u32[]{:S(2)}) copy-start(bf16[1,128,1024]{2,1,0:T(8,128)(2,1)} %cot_ref.1) | copy-start | bytes 786436
  28.1 15.2 %copy-start.2 = (bf16[1,128,1024]{2,1,0:T(8,128)(2,1)S(1)}, bf16[1,128,1024]{2,1,0:T(8,128)(2,1)}, u32[]{:S(2)}) copy-start(bf16[1,128,1024]{2,1,0:T(8,128)(2,1)} %x_ref.1) | copy-start | bytes 786436
  28.9 21.3 %collective-permute-start.1 = (bf16[128,128]{1,0:T(8,128)(2,1)S(1)}, bf16[128,128]{1,0:T(8,128)(2,1)S(1)}, u32[]{:S(2)}, u32[]{:S(2)}) collective-permute-start(bf16[128,128]{1,0:T(8,128)(2,1)S(1)} %get-tuple-element.38), channel_id=1, source_target_pairs={{0,498},{1,7},{2,16},{3,509},{4,502},{5,11},{6,20},{7,1},{8,506},{... | collective-permute-start | bytes 98312 | tf_op jit(solution)/shard_map/ppermute | solution.py:450
  32.5 17.7 %all-to-all-start.1 = ((f32[16,1,128]{2,1,0:T(1,128)}), f32[16,1,128]{2,1,0:T(1,128)S(1)}, u32[]{:S(2)}, u32[]{:S(2)}) async-start(f32[16,1,128]{2,1,0:T(1,128)} %get-tuple-element.34), calls=%async_computation.1 | async-start | bytes 16384 | tf_op jit(solution)/shard_map/all_to_all | solution.py:455
  54.8 18.2 %all-to-all-start.2 = ((f32[32,5,4,128]{3,2,1,0:T(4,128)}), f32[32,5,4,128]{3,2,1,0:T(4,128)S(1)}, u32[]{:S(2)}, u32[]{:S(2)}) async-start(f32[32,5,4,128]{3,2,1,0:T(4,128)} %bitcast.9), calls=%async_computation.2 | async-start | bytes 655360 | tf_op jit(solution)/shard_map/all_to_all | solution.py:401
  60.3 5.0 %collective-permute-start.2 = (bf16[128,128]{1,0:T(8,128)(2,1)S(1)}, bf16[128,128]{1,0:T(8,128)(2,1)S(1)}, u32[]{:S(2)}, u32[]{:S(2)}) collective-permute-start(bf16[128,128]{1,0:T(8,128)(2,1)S(1)} %collective-permute-done.1.in_ref.own_ref), channel_id=1, source_target_pairs={{0,1},{1,0},{2,3},{3,2},{4,5},{5,4},{6,7},{7,6},{8,9},{9,8},{10,11... | collective-permute-start | bytes 98312 | tf_op jit(solution)/shard_map/ppermute | solution.py:486
  83.7 15.5 %all-to-all-start.4 = ((f32[32,9,2,128]{3,2,1,0:T(2,128)}), f32[32,9,2,128]{3,2,1,0:T(2,128)S(1)}, u32[]{:S(2)}, u32[]{:S(2)}) async-start(f32[32,9,2,128]{3,2,1,0:T(2,128)} %bitcast.14), calls=%async_computation.4 | async-start | bytes 589824 | tf_op jit(solution)/shard_map/all_to_all | solution.py:510

commit v7 on v6

--- a/solution.py
+++ b/solution.py
@@ -397,7 +397,7 @@
 
 
 def exchanged(x, axes, parts):
-    x = x.reshape(parts, x.shape[0] // parts // 4, 4, C)
+    x = x.reshape(parts, x.shape[0] // parts // 2, 2, C)
     return lax.all_to_all(x, axes, 0, 0, tiled=True)
 
 

time: 106 us -> 106 us (level)
  no operation moved by 1% of the time
where the time goes in v7:
time: 106 us
  starting transfers between devices  43.3 us (41%)
  blocking collectives  27.9 us (26%)
  waiting for transfers between devices  23.4 us (22%)
  Pallas kernels  10.3 us (10%)
    all_to_all x1, starting transfers between devices, body(): stats = lax.all_to_all(stats, NEAR, 0, 0, tiled=True)  10.8 us
    all_to_all x1, blocking collectives, exchanged(): return lax.all_to_all(x, axes, 0, 0, tiled=True)  9.78 us
    all_to_all x1, starting transfers between devices, body(): stats = lax.all_to_all(stats, FAR, 0, 0, tiled=True)  9.68 us
    all_to_all x1, waiting for transfers between devices, exchanged(): return lax.all_to_all(x, axes, 0, 0, tiled=True)  7.8 us
    ppermute x1, starting transfers between devices, body(): came = lax.ppermute(edges, 'z2', [(0, 1), (1, 0)])  6.77 us
    all_to_all x1, waiting for transfers between devices, body(): stats = lax.all_to_all(stats, NEAR, 0, 0, tiled=True)  6.03 us
    all_gather x1, blocking collectives, body(): whole = lax.all_gather(half, 'co', axis=0, tiled=True)  5.78 us
    all_to_all x1, starting transfers between devices, exchanged(): return lax.all_to_all(x, axes, 0, 0, tiled=True)  5.48 us
  transfers between devices with their start and end apart: 7, of which 5 were waited for; matrix products, arithmetic and copies ran while one was open for 0% of the time, Pallas kernels for 3%

profile of v7, /device:TPU:1, one launch (start us, length us, event | category | flops | bytes accessed | tf_op | source)
XLA Modules:
  0.0 105.8 jit_solution(13886794142463694134)
XLA Ops:
  0.7 2.4 %shard_map.102 = (bf16[2,160,128]{2,1,0:T(8,128)(2,1)S(1)}, f32[32,1,128]{2,1,0:T(1,128)}) custom-call(bf16[1,128,1024]{2,1,0:T(8,128)(2,1)} %x_ref.1, bf16[1,128,1024]{2,1,0:T(8,128)(2,1)} %cot_ref.1), custom_call_target="tpu_custom_call" | custom-call | tf_op jit(solution)/shard_map/pallas_call | solution.py:414
  3.1 6.8 %collective-permute-start = (bf16[2,160,128]{2,1,0:T(8,128)(2,1)S(1)}, bf16[2,160,128]{2,1,0:T(8,128)(2,1)S(1)}, u32[]{:S(2)}, u32[]{:S(2)}) collective-permute-start(bf16[2,160,128]{2,1,0:T(8,128)(2,1)S(1)} %get-tuple-element.27.own_ref), channel_id=1, source_target_pairs={{0,2},{2,0},{1,3},{3,1},{4,6},{6,4},{5,7},{7,5},{8,10},{10,8},{9,1... | collective-permute-start | bytes 245768 | tf_op jit(solution)/shard_map/ppermute | solution.py:422
  9.9 9.7 %all-to-all-start = ((f32[32,1,128]{2,1,0:T(1,128)}), f32[32,1,128]{2,1,0:T(1,128)S(1)}, u32[]{:S(2)}, u32[]{:S(2)}) async-start(f32[32,1,128]{2,1,0:T(1,128)} %get-tuple-element.31), calls=%async_computation | async-start | bytes 32768 | tf_op jit(solution)/shard_map/all_to_all | solution.py:423
  20.3 5.0 %all-gather = bf16[6,128,128]{2,1,0:T(8,128)(2,1)S(1)} all-gather(bf16[3,128,128]{2,1,0:T(8,128)(2,1)S(1)} %get-tuple-element.30), channel_id=2, replica_groups=mesh['y'=8,'x'=4,'zh'=2,'co'=2,'z2'=2,'z1'=2] {'z1'}, dimensions={0}, use_global_device_ids=true | all-gather | bytes 294912 | tf_op jit(solution)/shard_map/all_gather | solution.py:437
  25.3 2.7 %all-to-all-done.in_stat_ref = f32[32,1,128]{2,1,0:T(1,128)S(1)} async-done(((f32[32,1,128]{2,1,0:T(1,128)}), f32[32,1,128]{2,1,0:T(1,128)S(1)}, u32[]{:S(2)}, u32[]{:S(2)}) %all-to-all-start) | async-done | bytes 16416 | tf_op jit(solution)/shard_map/all_to_all | solution.py:423
  28.1 0.8 shard_map.104
  28.9 3.6 %collective-permute-start.1 = (bf16[128,128]{1,0:T(8,128)(2,1)S(1)}, bf16[128,128]{1,0:T(8,128)(2,1)S(1)}, u32[]{:S(2)}, u32[]{:S(2)}) collective-permute-start(bf16[128,128]{1,0:T(8,128)(2,1)S(1)} %get-tuple-element.38), channel_id=1, source_target_pairs={{0,498},{1,7},{2,16},{3,509},{4,502},{5,11},{6,20},{7,1},{8,506},{... | collective-permute-start | bytes 98312 | tf_op jit(solution)/shard_map/ppermute | solution.py:450
  32.5 10.8 %all-to-all-start.1 = ((f32[16,1,128]{2,1,0:T(1,128)}), f32[16,1,128]{2,1,0:T(1,128)S(1)}, u32[]{:S(2)}, u32[]{:S(2)}) async-start(f32[16,1,128]{2,1,0:T(1,128)} %get-tuple-element.34), calls=%async_computation.1 | async-start | bytes 16384 | tf_op jit(solution)/shard_map/all_to_all | solution.py:455
  43.3 0.9 shard_map.105
  44.2 6.0 %all-to-all-done.1.in_stat_ref = f32[16,1,128]{2,1,0:T(1,128)S(1)} async-done(((f32[16,1,128]{2,1,0:T(1,128)}), f32[16,1,128]{2,1,0:T(1,128)S(1)}, u32[]{:S(2)}, u32[]{:S(2)}) %all-to-all-start.1) | async-done | bytes 8224 | tf_op jit(solution)/shard_map/all_to_all | solution.py:455
  50.2 1.3 %shard_map.106 = (f32[640,128]{1,0:T(8,128)S(1)}, f32[640,128]{1,0:T(8,128)S(1)}, f32[1024,128]{1,0:T(8,128)S(1)}, f32[2,128]{1,0:T(2,128)S(1)}) custom-call(f32[16,128]{1,0:T(8,128)S(1)} %get-tuple-element.28.mark_ref, bf16[1024,128]{1,0:T(8,128)(2,1)S(1)} %get-tuple-element.33.xt_ref, bf16[1,128,1024]{2,1,0:T(8,128)(2,1)S(1)} %copy-done, ...), custom_call_target="tpu_custom_call" | custom-call | tf_op jit(solution)/shard_map/pallas_call | solution.py:466
  51.5 2.6 %all-gather.1 = f32[1280,128]{1,0:T(8,128)S(1)} all-gather(f32[640,128]{1,0:T(8,128)S(1)} %get-tuple-element.42), channel_id=3, replica_groups=mesh['y'=8,'x'=4,'zh'=2,'co'=2,'z2'=2,'z1'=2] {'co'}, dimensions={0}, use_global_device_ids=true | all-gather | bytes 983040 | tf_op jit(solution)/shard_map/all_gather | solution.py:487
  54.1 0.8 shard_map.107
  54.8 5.5 %all-to-all-start.2 = ((f32[32,10,2,128]{3,2,1,0:T(2,128)}), f32[32,10,2,128]{3,2,1,0:T(2,128)S(1)}, u32[]{:S(2)}, u32[]{:S(2)}) async-start(f32[32,10,2,128]{3,2,1,0:T(2,128)} %bitcast.9), calls=%async_computation.2 | async-start | bytes 655360 | tf_op jit(solution)/shard_map/all_to_all | solution.py:401
  60.3 2.2 %collective-permute-start.2 = (bf16[128,128]{1,0:T(8,128)(2,1)S(1)}, bf16[128,128]{1,0:T(8,128)(2,1)S(1)}, u32[]{:S(2)}, u32[]{:S(2)}) collective-permute-start(bf16[128,128]{1,0:T(8,128)(2,1)S(1)} %collective-permute-done.1.in_ref.own_ref), channel_id=1, source_target_pairs={{0,1},{1,0},{2,3},{3,2},{4,5},{5,4},{6,7},{7,6},{8,9},{9,8},{10,11... | collective-permute-start | bytes 98312 | tf_op jit(solution)/shard_map/ppermute | solution.py:486
  62.8 2.5 %collective-permute-done.2.other_ref = bf16[128,128]{1,0:T(8,128)(2,1)S(1)} collective-permute-done((bf16[128,128]{1,0:T(8,128)(2,1)S(1)}, bf16[128,128]{1,0:T(8,128)(2,1)S(1)}, u32[]{:S(2)}, u32[]{:S(2)}) %collective-permute-start.2) | collective-permute-done | bytes 32800 | tf_op jit(solution)/shard_map/ppermute | solution.py:486
  65.3 7.8 %all-to-all-done.2 = f32[32,10,2,128]{3,2,1,0:T(2,128)S(1)} async-done(((f32[32,10,2,128]{3,2,1,0:T(2,128)}), f32[32,10,2,128]{3,2,1,0:T(2,128)S(1)}, u32[]{:S(2)}, u32[]{:S(2)}) %all-to-all-start.2) | async-done | bytes 327712 | tf_op jit(solution)/shard_map/all_to_all | solution.py:401
  73.1 9.8 %all_to_all.25 = f32[8,10,2,128]{3,2,1,0:T(2,128)S(1)} all-to-all(f32[8,10,2,128]{3,2,1,0:T(2,128)S(1)} %bitcast.27), channel_id=1, replica_groups=mesh['y'=8,'x'=4,'zh'=2,'co'=2,'z2'=2,'z1'=2] {'zh','z2','z1'}, dimensions={0} | all-to-all | bytes 163840 | tf_op jit(solution)/shard_map/all_to_all | solution.py:401
  83.7 4.8 %all-to-all-start.4 = ((f32[32,9,2,128]{3,2,1,0:T(2,128)}), f32[32,9,2,128]{3,2,1,0:T(2,128)S(1)}, u32[]{:S(2)}, u32[]{:S(2)}) async-start(f32[32,9,2,128]{3,2,1,0:T(2,128)} %bitcast.14), calls=%async_computation.4 | async-start | bytes 589824 | tf_op jit(solution)/shard_map/all_to_all | solution.py:510
  88.5 4.7 %all-gather.2 = bf16[4,64,128]{2,1,0:T(8,128)(2,1)S(1)} all-gather(bf16[2,64,128]{2,1,0:T(8,128)(2,1)S(1)} %get-tuple-element.45), channel_id=4, replica_groups=mesh['y'=8,'x'=4,'zh'=2,'co'=2,'z2'=2,'z1'=2] {'z2'}, dimensions={0}, use_global_device_ids=true | all-gather | bytes 98304 | tf_op jit(solution)/shard_map/all_gather | solution.py:502
  93.1 1.7 %shard_map.111 = (bf16[1,128,1024]{2,1,0:T(8,128)(2,1)}, f32[1,128]{1,0:T(1,128)}, f32[1,128]{1,0:T(1,128)}) custom-call(s32[10]{0:T(128)S(1)} %pad_add_fusion.info_ref, f32[1024,128]{1,0:T(8,128)S(1)} %get-tuple-element.39.pre_ref, bf16[1024,128]{1,0:T(8,128)(2,1)S(1)} %get-tuple-element.33.xt_ref, f32[2,128]{1,0:T(2,128)S(1)} %get-tuple-element.40.norm_ref, ...), custom_call_target="tpu_custom_call" | custom-call | tf_op jit(solution)/shard_map/pallas_call | solution.py:512
  94.8 4.4 %all-to-all-done.4 = f32[32,9,2,128]{3,2,1,0:T(2,128)S(1)} async-done(((f32[32,9,2,128]{3,2,1,0:T(2,128)}), f32[32,9,2,128]{3,2,1,0:T(2,128)S(1)}, u32[]{:S(2)}, u32[]{:S(2)}) %all-to-all-start.4) | async-done | bytes 294944 | tf_op jit(solution)/shard_map/all_to_all | solution.py:510
  99.2 5.8 %all_gather.27 = f32[64,9,2,128]{3,2,1,0:T(2,128)S(1)} all-gather(f32[32,9,2,128]{3,2,1,0:T(2,128)S(1)} %all-to-all-done.4), channel_id=1, replica_groups=mesh['y'=8,'x'=4,'zh'=2,'co'=2,'z2'=2,'z1'=2] {'co'}, dimensions={0}, use_global_device_ids=true | all-gather | bytes 884736 | tf_op jit(solution)/shard_map/all_gather | solution.py:511
  105.0 0.9 shard_map.112
  (21 shorter events, 1.8 us)
Async XLA Ops:
  0.6 18.9 %copy-start.5 = (s32[1,4]{1,0:T(1,128)S(1)}, s32[1,4]{1,0:T(1,128)}, u32[]{:S(2)}) copy-start(s32[1,4]{1,0:T(1,128)} %param.13) | copy-start | bytes 52
  0.6 18.9 %copy-start.6 = (s32[1,4]{1,0:T(1,128)S(1)}, s32[1,4]{1,0:T(1,128)}, u32[]{:S(2)}) copy-start(s32[1,4]{1,0:T(1,128)} %param.12) | copy-start | bytes 52
  0.7 19.0 %copy-start.3 = (f32[128]{0:T(128)S(1)}, f32[128]{0:T(128)}, u32[]{:S(2)}) copy-start(f32[128]{0:T(128)} %param.10) | copy-start | bytes 1540
  0.7 19.0 %copy-start.4 = (f32[128]{0:T(128)S(1)}, f32[128]{0:T(128)}, u32[]{:S(2)}) copy-start(f32[128]{0:T(128)} %param.11) | copy-start | bytes 1540
  3.1 25.0 %copy-start.1 = (bf16[128,9,128]{2,0,1:T(8,128)(2,1)S(1)}, bf16[128,9,128]{2,0,1:T(8,128)(2,1)}, u32[]{:S(2)}) copy-start(bf16[128,9,128]{2,0,1:T(8,128)(2,1)} %param.9) | copy-start | bytes 884740
  3.1 16.6 %collective-permute-start = (bf16[2,160,128]{2,1,0:T(8,128)(2,1)S(1)}, bf16[2,160,128]{2,1,0:T(8,128)(2,1)S(1)}, u32[]{:S(2)}, u32[]{:S(2)}) collective-permute-start(bf16[2,160,128]{2,1,0:T(8,128)(2,1)S(1)} %get-tuple-element.27.own_ref), channel_id=1, source_target_pairs={{0,2},{2,0},{1,3},{3,1},{4,6},{6,4},{5,7},{7,5},{8,10},{10,8},{9,1... | collective-permute-start | bytes 245768 | tf_op jit(solution)/shard_map/ppermute | solution.py:422
  9.9 18.2 %all-to-all-start = ((f32[32,1,128]{2,1,0:T(1,128)}), f32[32,1,128]{2,1,0:T(1,128)S(1)}, u32[]{:S(2)}, u32[]{:S(2)}) async-start(f32[32,1,128]{2,1,0:T(1,128)} %get-tuple-element.31), calls=%async_computation | async-start | bytes 32768 | tf_op jit(solution)/shard_map/all_to_all | solution.py:423
  28.1 15.2 %copy-start = (bf16[1,128,1024]{2,1,0:T(8,128)(2,1)S(1)}, bf16[1,128,1024]{2,1,0:T(8,128)(2,1)}, u32[]{:S(2)}) copy-start(bf16[1,128,1024]{2,1,0:T(8,128)(2,1)} %cot_ref.1) | copy-start | bytes 786436
  28.1 15.2 %copy-start.2 = (bf16[1,128,1024]{2,1,0:T(8,128)(2,1)S(1)}, bf16[1,128,1024]{2,1,0:T(8,128)(2,1)}, u32[]{:S(2)}) copy-start(bf16[1,128,1024]{2,1,0:T(8,128)(2,1)} %x_ref.1) | copy-start | bytes 786436
  28.9 21.3 %collective-permute-start.1 = (bf16[128,128]{1,0:T(8,128)(2,1)S(1)}, bf16[128,128]{1,0:T(8,128)(2,1)S(1)}, u32[]{:S(2)}, u32[]{:S(2)}) collective-permute-start(bf16[128,128]{1,0:T(8,128)(2,1)S(1)} %get-tuple-element.38), channel_id=1, source_target_pairs={{0,498},{1,7},{2,16},{3,509},{4,502},{5,11},{6,20},{7,1},{8,506},{... | collective-permute-start | bytes 98312 | tf_op jit(solution)/shard_map/ppermute | solution.py:450
  32.5 17.7 %all-to-all-start.1 = ((f32[16,1,128]{2,1,0:T(1,128)}), f32[16,1,128]{2,1,0:T(1,128)S(1)}, u32[]{:S(2)}, u32[]{:S(2)}) async-start(f32[16,1,128]{2,1,0:T(1,128)} %get-tuple-element.34), calls=%async_computation.1 | async-start | bytes 16384 | tf_op jit(solution)/shard_map/all_to_all | solution.py:455
  54.8 18.2 %all-to-all-start.2 = ((f32[32,10,2,128]{3,2,1,0:T(2,128)}), f32[32,10,2,128]{3,2,1,0:T(2,128)S(1)}, u32[]{:S(2)}, u32[]{:S(2)}) async-start(f32[32,10,2,128]{3,2,1,0:T(2,128)} %bitcast.9), calls=%async_computation.2 | async-start | bytes 655360 | tf_op jit(solution)/shard_map/all_to_all | solution.py:401
  60.3 5.0 %collective-permute-start.2 = (bf16[128,128]{1,0:T(8,128)(2,1)S(1)}, bf16[128,128]{1,0:T(8,128)(2,1)S(1)}, u32[]{:S(2)}, u32[]{:S(2)}) collective-permute-start(bf16[128,128]{1,0:T(8,128)(2,1)S(1)} %collective-permute-done.1.in_ref.own_ref), channel_id=1, source_target_pairs={{0,1},{1,0},{2,3},{3,2},{4,5},{5,4},{6,7},{7,6},{8,9},{9,8},{10,11... | collective-permute-start | bytes 98312 | tf_op jit(solution)/shard_map/ppermute | solution.py:486
  83.7 15.5 %all-to-all-start.4 = ((f32[32,9,2,128]{3,2,1,0:T(2,128)}), f32[32,9,2,128]{3,2,1,0:T(2,128)S(1)}, u32[]{:S(2)}, u32[]{:S(2)}) async-start(f32[32,9,2,128]{3,2,1,0:T(2,128)} %bitcast.14), calls=%async_computation.4 | async-start | bytes 589824 | tf_op jit(solution)/shard_map/all_to_all | solution.py:510
